TPU v7x, 32 devices: a whole 2x2x4 slice. The times are simulated.
32 devices in a mesh: clip: 2 (over x), tm: 4 (over z), tensor: 4 (over y, core).
Axes of the slice: x: 2, y: 2, z: 4, core: 2. Of those that a mesh axis runs over, the one named last changes fastest.
Arguments:
- resid: bfloat16 [16, 4, 256, 6144], P('tm', 'clip', 'tensor'), parts along dimension 1, may hold values from -16 to 16
- spatial_q: bfloat16 [16, 4, 256, 3072], P('tm', 'clip', None, 'tensor'), parts along dimension 1, may hold values from -100 to 100
- spatial_k: bfloat16 [16, 4, 256, 3072], P('tm', 'clip', None, 'tensor'), parts along dimension 1, may hold values from -5 to 5
- spatial_v: bfloat16 [16, 4, 256, 3072], P('tm', 'clip', None, 'tensor'), parts along dimension 1, may hold values from -6 to 6
- out_weight: bfloat16 [3072, 6144], P('tensor'), may hold values from -0.109375 to 0.109375
- norm_gain: float32 [6144], replicated, may hold values from 0.1 to 1.9
- qkv_weight: bfloat16 [6144, 3, 3072], P('tm', None, 'tensor'), may hold values from -4 to 4
Outputs:
- resid_out: bfloat16 [16, 4, 256, 6144], P('tm', 'clip', 'tensor'), parts along dimension 1
- temporal_ctx: bfloat16 [16, 4, 256, 3072], P('tm', 'clip', None, 'tensor'), parts along dimension 1
There are 2 independent parts, one for each index of `clip`. A program takes and returns all parts, laid end to end along the dimension named above; an argument that names none is the same for every part. Nothing has to cross between parts.
All inputs are finite; a program needn't handle non-finite values.
Results may differ from a plain program's by a relative error of at most 0.017.
Values may be sent and summed in bfloat16 or wider, within the bound.
No kernel may reach another device: no remote copies, remote signals or barrier semaphores. Data moves between devices by JAX's collectives and lax.ppermute only.
A program may use at most 320 MiB of HBM per device.

v0:
```python
import math

import jax
import jax.numpy as jnp
from jax import lax
from jax.sharding import PartitionSpec as P

HD = 128


def layer_norm(stream_in, norm_gain):
    average = jnp.mean(stream_in, axis=-1, keepdims=True)
    centred = stream_in - average
    variance = jnp.mean(centred * centred, axis=-1, keepdims=True)
    return (centred * lax.rsqrt(variance + 1e-06) * norm_gain).astype(jnp.bfloat16)


def spatial_attend(queries, keys_in, values):
    dims_in = queries.shape
    head_shape = dims_in[:3] + (dims_in[3] // HD, HD)
    query_heads = queries.reshape(head_shape)
    key_heads = keys_in.reshape(head_shape)
    value_heads = values.reshape(head_shape)
    scores = jnp.einsum(
        "fcphd,fcqhd->fchpq", query_heads, key_heads, preferred_element_type=jnp.float32
    ) / math.sqrt(HD)
    weights = jax.nn.softmax(scores, axis=-1).astype(jnp.bfloat16)
    context = jnp.einsum(
        "fchpq,fcqhd->fcphd", weights, value_heads, preferred_element_type=jnp.float32
    )
    return context.astype(jnp.bfloat16).reshape(dims_in)


def temporal_attend(queries, keys_in, values):
    query_dims = queries.shape
    heads_here = query_dims[3] // HD
    query_heads = queries.reshape(query_dims[:3] + (heads_here, HD))
    key_heads = keys_in.reshape(keys_in.shape[:3] + (heads_here, HD))
    value_heads = values.reshape(values.shape[:3] + (heads_here, HD))
    scores = jnp.einsum(
        "fcphd,gcphd->cphfg", query_heads, key_heads, preferred_element_type=jnp.float32
    ) / math.sqrt(HD)
    weights = jax.nn.softmax(scores, axis=-1).astype(jnp.bfloat16)
    context = jnp.einsum(
        "cphfg,gcphd->fcphd", weights, value_heads, preferred_element_type=jnp.float32
    )
    return context.astype(jnp.bfloat16).reshape(query_dims)


def local_temporal(exchanged):
    return temporal_attend(exchanged[:, :, :, 0], exchanged[:, :, :, 1], exchanged[:, :, :, 2])


def per_device(resid, spatial_q, spatial_k, spatial_v, out_weight, norm_gain, qkv_weight):
    context = spatial_attend(spatial_q, spatial_k, spatial_v)
    frames_here, clips_here, patches_all, heads_width = context.shape
    model_width = out_weight.shape[1]
    patch_major = context.transpose(2, 0, 1, 3)
    own_share = lax.psum_scatter(
        jnp.einsum(
            "pfcj,jd->pfcd", patch_major, out_weight, preferred_element_type=jnp.float32
        ).astype(jnp.bfloat16),
        "tensor",
        scatter_dimension=0,
        tiled=True,
    ).astype(jnp.float32)
    stream = resid.astype(jnp.float32) + own_share.transpose(1, 2, 0, 3)
    resid_out = stream.astype(jnp.bfloat16)
    normed = lax.all_gather(layer_norm(stream, norm_gain), "tensor", axis=2, tiled=True)
    flat_rows = normed.reshape(-1, model_width)
    qkv_width = 3 * qkv_weight.shape[2]
    block_rows = lax.all_gather(qkv_weight, "tm", axis=0, tiled=True)
    accumulated = jnp.dot(
        flat_rows,
        block_rows.reshape(block_rows.shape[0], qkv_width),
        preferred_element_type=jnp.float32,
    )
    projected = accumulated.astype(jnp.bfloat16).reshape(
        frames_here, clips_here, patches_all, 3, qkv_weight.shape[2]
    )
    patch_context = local_temporal(
        lax.all_to_all(projected, "tm", split_axis=2, concat_axis=0, tiled=True)
    )
    temporal_ctx = lax.all_to_all(patch_context, "tm", split_axis=0, concat_axis=2, tiled=True)
    return (resid_out, temporal_ctx)


def solution(mesh):
    placed = (
        P("tm", "clip", "tensor", None),
        P("tm", "clip", None, "tensor"),
        P("tm", "clip", None, "tensor"),
        P("tm", "clip", None, "tensor"),
        P("tensor", None),
        P(),
        P("tm", None, "tensor"),
    )
    return jax.shard_map(
        per_device,
        mesh=mesh,
        in_specs=placed,
        out_specs=(P("tm", "clip", "tensor", None), P("tm", "clip", None, "tensor")),
        check_vma=False,
    )
```

profile of v0, /device:TPU:0, one launch (start us, length us, event | category | flops | bytes accessed | tf_op | source)
XLA Modules:
  0.0 1213.5 jit_solution(17183162838132810751)
XLA Ops:
  8.0 0.0 copy-start.2
  8.0 0.0 reduce-scatter.2.cloned.1.call-start
  8.1 4.8 copy.65
  12.8 0.0 copy-done.2
  12.8 2.8 copy.66
  15.6 3.2 copy.69
  18.8 11.7 fusion.29
  30.5 7.4 fusion.23
  37.8 3.2 copy.71
  41.0 26.7 %convolution_convert_fusion = bf16[256,4,2,6144]{3,0,2,1:T(8,128)(2,1)} fusion(bf16[768,6144]{1,0:T(8,128)(2,1)} %param.11, bf16[4,2,256,768]{3,2,1,0:T(8,128)(2,1)S(1)} %copy.71), kind=kOutput, calls=%fused_computation.2 | convolution fusion | flops 19339935744 | bytes 37748736 | tf_op jit(solution)/shard_map/pfcj,jd->pfcd/dot_general | solution.py:60
  67.7 0.0 reduce-scatter.2.cloned.1.call-update
  67.7 0.0 all-gather.5.cloned.1.call-start
  67.8 10.4 copy.72
  78.2 0.0 all-gather.5.cloned.1.call-update
  78.3 0.3 all-gather.3.cloned.1.call-start
  78.6 172.5 %reduce-scatter.2.cloned.1.call-done = bf16[64,4,2,6144]{3,0,2,1:T(8,128)(2,1)} async-done(((bf16[256,4,2,6144]{3,0,2,1:T(8,128)(2,1)}), bf16[64,4,2,6144]{3,0,2,1:T(8,128)(2,1)}) %reduce-scatter.2.cloned.1.call-update) | async-done | bytes 6291472 | tf_op jit(solution)/shard_map/reduce_scatter | solution.py:59
  251.1 0.0 copy-start
  251.1 0.0 slice-start
  251.1 6.5 fusion.3
  257.6 0.0 copy-done
  257.6 0.0 slice-start.1
  257.6 0.0 copy-start.3
  257.6 5.7 multiply_reduce_fusion
  263.3 0.0 slice-done
  263.3 0.0 slice-done.1
  263.3 0.0 copy-done.3
  263.3 6.1 multiply_convert_fusion
  269.4 0.0 all-gather.3.cloned.1.call-update
  269.5 287.3 %all-gather.5.cloned.1.call-done = bf16[6144,3,768]{0,2,1:T(8,128)(2,1)} async-done(((bf16[1536,3,768]{0,2,1:T(8,128)(2,1)}), bf16[6144,3,768]{0,2,1:T(8,128)(2,1)}) %all-gather.5.cloned.1.call-update) | async-done | bytes 28311568 | tf_op jit(solution)/shard_map/all_gather | solution.py:72
  556.8 154.1 %all-gather.3.cloned.1.call-done = bf16[4,2,256,6144]{3,2,1,0:T(8,128)(2,1)} async-done(((bf16[4,2,64,6144]{3,2,1,0:T(8,128)(2,1)}), bf16[4,2,256,6144]{3,2,1,0:T(8,128)(2,1)}) %all-gather.3.cloned.1.call-update) | async-done | bytes 25165840 | tf_op jit(solution)/shard_map/all_gather | solution.py:69
  710.8 74.8 %convolution_convert_fusion.1 = bf16[2048,2304]{1,0:T(8,128)(2,1)} fusion(bf16[2048,6144]{1,0:T(8,128)(2,1)} %bitcast.66, bf16[6144,2304]{0,1:T(8,128)(2,1)} %bitcast.65), kind=kOutput, calls=%fused_computation.8 | convolution fusion | flops 57986777088 | bytes 62914560 | tf_op jit(solution)/shard_map/dot_general | solution.py:73
  785.6 21.3 %reshape.54 = bf16[4,2,256,3,768]{4,3,2,1,0:T(4,128)(2,1)} reshape(bf16[2048,2304]{1,0:T(8,128)(2,1)} %convolution_convert_fusion.1) | data formatting | bytes 18874368 | tf_op jit(solution)/shard_map/reshape | solution.py:78
  806.9 15.8 %copy.74 = bf16[4,2,256,3,768]{4,0,3,1,2:T(4,128)(2,1)S(1)} copy(bf16[4,2,256,3,768]{4,3,2,1,0:T(4,128)(2,1)} %reshape.54) | data formatting | bytes 18874368 | tf_op jit(solution)/shard_map/reshape | solution.py:78
  822.7 218.5 %all_to_all.36 = bf16[4,2,256,3,768]{4,0,3,1,2:T(4,128)(2,1)} all-to-all(bf16[4,2,256,3,768]{4,0,3,1,2:T(4,128)(2,1)S(1)} %copy.74), channel_id=1, replica_groups=mesh['clip'=2,'tm'=4,'tensor'=4] {'tm'}, dimensions={2} | all-to-all | bytes 18874368 | tf_op jit(solution)/shard_map/all_to_all | solution.py:82
  1041.3 9.4 copy.75
  1050.7 8.6 copy.76
  1059.2 5.9 fusion.28
  1065.1 7.7 reshape_squeeze.9
  1072.8 7.7 reshape_squeeze.11
  1080.5 4.7 reshape_squeeze.10
  1085.2 7.2 fusion.16
  1092.4 0.0 copy-start.1
  1092.4 26.5 %fusion.30 = (f32[2,64,6,16]{3,2,1,0:T(8,128)S(1)}, f32[2,64,6,16,16]{3,4,2,1,0:T(8,128)S(1)}) fusion(f32[2,64,6,16,16]{3,4,2,1,0:T(8,128)S(1)} %fusion.16), kind=kOutput, calls=%fused_computation.37 | output fusion | flops 786447 | bytes 1622016 | tf_op jit(solution)/shard_map/sub | solution.py:43
  1118.9 0.0 copy-done.1
  1118.9 2.6 convert_bitcast_fusion
  1121.6 3.0 copy.81
  1124.6 6.4 reshape.52
  1131.0 72.8 %all_to_all.37 = bf16[16,2,64,768]{3,2,1,0:T(8,128)(2,1)S(1)} all-to-all(bf16[16,2,64,768]{3,2,1,0:T(8,128)(2,1)S(1)} %reshape.52), channel_id=1, replica_groups=mesh['clip'=2,'tm'=4,'tensor'=4] {'tm'}, dimensions={0} | all-to-all | bytes 6291456 | tf_op jit(solution)/shard_map/all_to_all | solution.py:84
  1203.8 2.0 copy.82
  (3 shorter events, 0.0 us)
Async XLA Ops:
  8.0 4.8 copy-start.2
  8.0 243.0 %reduce-scatter.2.cloned.1.call-start = ((), (), s32[]{:S(2)}) async-start(), calls=%async_computation.3 | async-start | bytes 31457280 | tf_op jit(solution)/shard_map/reduce_scatter | solution.py:59
  67.7 489.0 %all-gather.5.cloned.1.call-start = ((), (), s32[]{:S(2)}) async-start(), calls=%async_computation.5 | async-start | bytes 35389440 | tf_op jit(solution)/shard_map/all_gather | solution.py:72
  78.3 632.6 %all-gather.3.cloned.1.call-start = ((), (), s32[]{:S(2)}) async-start(), calls=%async_computation.4 | async-start | bytes 31457280 | tf_op jit(solution)/shard_map/all_gather | solution.py:69
  251.1 6.5 copy-start
  251.1 12.2 %slice-start = ((s8[6291456]{0:T(1024)(128)(4,1)}), s8[4194304]{0:T(1024)(128)(4,1)S(1)}, s32[]{:S(2)}) async-start(s8[6291456]{0:T(1024)(128)(4,1)} %bitcast.55), calls=%async_computation.6 | async-start | bytes 8388608
  257.6 5.7 slice-start.1
  257.6 5.7 copy-start.3
  1092.4 26.5 %copy-start.1 = (bf16[16,2,64,6,128]{4,3,2,1,0:T(8,128)(2,1)S(1)}, bf16[16,2,64,6,128]{4,3,2,1,0:T(8,128)(2,1)}, u32[]{:S(2)}) copy-start(bf16[16,2,64,6,128]{4,3,2,1,0:T(8,128)(2,1)} %reshape_squeeze.9) | copy-start | bytes 9437188
Sparse Core Ops, SparseCore 0:
  67.9 183.1 reduce-scatter.1
Sparse Core Ops, SparseCore 1:
  78.3 478.4 all-gather.4
  558.3 152.5 all-gather.2
where the time goes:
time: 1220 us; the launch traced here: 1210 us
  waiting for transfers between devices  614 us (50%)
  blocking collectives  291 us (24%)
  matrix products  130 us (11%)
  local copies, waits for them, and re-layouts  117 us (10%)
  other arithmetic  44.8 us (4%)
  between operations  15.8 us (1%)
    all_gather x1, waiting for transfers between devices, per_device(): block_rows = lax.all_gather(qkv_weight, 'tm', axis=0, tiled=True)  287 us
    all_to_all x1, blocking collectives, per_device(): lax.all_to_all(projected, 'tm', split_axis=2, concat_axis=0, tiled=True)  219 us
    reduce_scatter x1, waiting for transfers between devices, per_device(): lax.psum_scatter(jnp.einsum('pfcj,jd->pfcd', patch_major, out_weight, pre...  172 us
    all_gather x1, waiting for transfers between devices, per_device(): lax.all_gather(layer_norm(stream, norm_gain), 'tensor', axis=2, tiled=True)  154 us
    dot_general x1, matrix products, per_device(): jnp.dot(flat_rows, block_rows.reshape(block_rows.shape[0], qkv_width), pr...  74.8 us
    all_to_all x1, blocking collectives, per_device(): lax.all_to_all(patch_context, 'tm', split_axis=0, concat_axis=2, tiled=True)  72.8 us
    reshape x2, local copies, waits for them, and re-layouts, per_device(): accumulated.astype(jnp.bfloat16)  37.1 us
    dot_general x1, matrix products, per_device(): jnp.einsum('pfcj,jd->pfcd', patch_major, out_weight, preferred_element_ty...  26.7 us
  transfers between devices with their start and end apart: 3, of which 3 were waited for; matrix products, arithmetic and copies ran while one was open for 2% of the time, Pallas kernels for 0%

commit v1 on v0

--- a/solution.py
+++ b/solution.py
@@ -1,11 +1,15 @@
+import functools
 import math
 
 import jax
 import jax.numpy as jnp
 from jax import lax
+from jax.experimental import pallas as pl
+from jax.experimental.pallas import tpu as pltpu
 from jax.sharding import PartitionSpec as P
 
 HD = 128
+MIB = 1 << 20
 
 
 def layer_norm(stream_in, norm_gain):
@@ -47,11 +51,7 @@
     return context.astype(jnp.bfloat16).reshape(query_dims)
 
 
-def local_temporal(exchanged):
-    return temporal_attend(exchanged[:, :, :, 0], exchanged[:, :, :, 1], exchanged[:, :, :, 2])
-
-
-def per_device(resid, spatial_q, spatial_k, spatial_v, out_weight, norm_gain, qkv_weight):
+def per_device_plain(resid, spatial_q, spatial_k, spatial_v, out_weight, norm_gain, qkv_weight):
     context = spatial_attend(spatial_q, spatial_k, spatial_v)
     frames_here, clips_here, patches_all, heads_width = context.shape
     model_width = out_weight.shape[1]
@@ -78,10 +78,403 @@
     projected = accumulated.astype(jnp.bfloat16).reshape(
         frames_here, clips_here, patches_all, 3, qkv_weight.shape[2]
     )
-    patch_context = local_temporal(
-        lax.all_to_all(projected, "tm", split_axis=2, concat_axis=0, tiled=True)
+    exchanged = lax.all_to_all(projected, "tm", split_axis=2, concat_axis=0, tiled=True)
+    patch_context = temporal_attend(
+        exchanged[:, :, :, 0], exchanged[:, :, :, 1], exchanged[:, :, :, 2]
     )
     temporal_ctx = lax.all_to_all(patch_context, "tm", split_axis=0, concat_axis=2, tiled=True)
+    return (resid_out, temporal_ctx)
+
+
+def attend(queries, keys_in, values, same=None):
+    scores = lax.dot_general(
+        queries, keys_in, (((1,), (1,)), ((), ())), preferred_element_type=jnp.float32
+    ) * (1.0 / math.sqrt(HD))
+    if same is not None:
+        scores = jnp.where(same, scores, -jnp.inf)
+    top = jnp.max(scores, axis=1, keepdims=True)
+    raised = jnp.exp(scores - top)
+    total = jnp.sum(raised, axis=1, keepdims=True)
+    probs = (raised * (1.0 / total)).astype(jnp.bfloat16)
+    context = jnp.dot(probs, values, preferred_element_type=jnp.float32)
+    return context.astype(jnp.bfloat16)
+
+
+def spatial_kernel(heads, sides, rows, where, q_ref, k_ref, v_ref, keep_ref, send_ref, held):
+    core = where[1]
+    for head in range(heads):
+        lanes = slice(head * HD, (head + 1) * HD)
+        held[:, lanes] = attend(q_ref[0, 0, :, lanes], k_ref[0, 0, :, lanes], v_ref[0, 0, :, lanes])
+    for side in range(sides):
+        own = pl.multiple_of((side * 2 + core) * rows, rows)
+        other = pl.multiple_of((side * 2 + 1 - core) * rows, rows)
+        keep_ref[0, side] = held[pl.ds(own, rows), :]
+        send_ref[0, side] = held[pl.ds(other, rows), :]
+
+
+def spatial(where, spatial_q, spatial_k, spatial_v, clip_at, rows):
+    frames, _, patches, width = spatial_q.shape
+    sides = patches // (2 * rows)
+    block = pl.BlockSpec((1, 1, patches, width), lambda f, w: (f, clip_at, 0, 0))
+    half = pl.BlockSpec((1, sides, rows, width), lambda f, w: (f, 0, 0, 0))
+    shape = jax.ShapeDtypeStruct((frames, sides, rows, width), jnp.bfloat16)
+    heads = width // HD
+    return pl.pallas_call(
+        functools.partial(spatial_kernel, heads, sides, rows),
+        grid_spec=pltpu.PrefetchScalarGridSpec(
+            num_scalar_prefetch=1,
+            grid=(frames,),
+            in_specs=[block] * 3,
+            out_specs=[half] * 2,
+            scratch_shapes=[pltpu.VMEM((patches, width), jnp.bfloat16)],
+        ),
+        out_shape=[shape, shape],
+        compiler_params=pltpu.CompilerParams(vmem_limit_bytes=32 * MIB),
+        cost_estimate=pl.CostEstimate(
+            flops=4 * frames * heads * patches * patches * HD,
+            bytes_accessed=8 * frames * patches * width,
+            transcendentals=frames * heads * patches * patches,
+        ),
+    )(where, spatial_q, spatial_k, spatial_v)
+
+
+def branch_tile(keep_ref, came_ref, own_ref, other_ref):
+    frames, _, rows, width = keep_ref.shape
+    partial = jnp.dot(
+        keep_ref[:, 0].reshape(frames * rows, width), own_ref[...],
+        preferred_element_type=jnp.float32,
+    )
+    return partial + jnp.dot(
+        came_ref[:, 0].reshape(frames * rows, width), other_ref[...],
+        preferred_element_type=jnp.float32,
+    )
+
+
+def send_kernel(where, keep_ref, came_ref, own_ref, other_ref, out_ref):
+    out_ref[...] = branch_tile(keep_ref, came_ref, own_ref, other_ref).astype(jnp.bfloat16)
+
+
+def branch_cost(frames, rows, width, model):
+    return pl.CostEstimate(
+        flops=4 * frames * rows * width * model,
+        bytes_accessed=4 * width * model + 8 * frames * rows * model,
+        transcendentals=0,
+    )
+
+
+def branch_for_other(where, keep, came, own_weight, other_weight, tile):
+    frames, _, rows, width = keep.shape
+    model = own_weight.shape[1]
+    context = pl.BlockSpec((frames, 1, rows, width), lambda n, w: (0, 1 - w[0], 0, 0))
+    weight = pl.BlockSpec((width, tile), lambda n, w: (0, n))
+    return pl.pallas_call(
+        send_kernel,
+        grid_spec=pltpu.PrefetchScalarGridSpec(
+            num_scalar_prefetch=1,
+            grid=(model // tile,),
+            in_specs=[context, context, weight, weight],
+            out_specs=pl.BlockSpec((frames * rows, tile), lambda n, w: (0, n)),
+        ),
+        out_shape=jax.ShapeDtypeStruct((frames * rows, model), jnp.bfloat16),
+        compiler_params=pltpu.CompilerParams(vmem_limit_bytes=32 * MIB),
+        cost_estimate=branch_cost(frames, rows, width, model),
+    )(where, keep, came, own_weight, other_weight)
+
+
+def norm_kernel(
+    tiles, tile, ways, where, keep_ref, came_ref, own_ref, other_ref, branch_ref, resid_ref,
+    gain_ref, *rest
+):
+    resid_out_ref, normed_refs, stream = rest[-ways - 2], rest[-ways - 1:-1], rest[-1]
+    step = pl.program_id(0)
+    frames, _, rows, _ = keep_ref.shape
+    model = tiles * tile
+    total = branch_tile(keep_ref, came_ref, own_ref, other_ref).astype(jnp.bfloat16)
+    total = total.astype(jnp.float32) + branch_ref[...].astype(jnp.float32)
+    total = total + resid_ref[:, 0].reshape(frames * rows, tile).astype(jnp.float32)
+    resid_out_ref[:, 0] = total.astype(jnp.bfloat16).reshape(frames, rows, tile)
+    stream[step] = total
+
+    @pl.when(step == tiles - 1)
+    def _():
+        share = rows // ways
+        for way in range(ways):
+            goal = lax.rem(where[2] + way, ways)
+            for frame in range(frames):
+                at = pl.multiple_of(frame * rows + goal * share, share)
+                picked = stream[:, pl.ds(at, share), :]
+                average = jnp.sum(
+                    jnp.sum(picked, axis=0), axis=-1, keepdims=True
+                ) * (1.0 / model)
+                centred = picked - average
+                variance = jnp.sum(
+                    jnp.sum(centred * centred, axis=0), axis=-1, keepdims=True
+                ) * (1.0 / model)
+                scale = lax.rsqrt(variance + 1e-06)
+                for n in range(tiles):
+                    lanes = slice(n * tile, (n + 1) * tile)
+                    normed_refs[way][frame * share:(frame + 1) * share, lanes] = (
+                        centred[n] * scale * gain_ref[:, lanes]
+                    ).astype(jnp.bfloat16)
+
+
+def norm(where, keep, came, own_weight, other_weight, branch, resid, gain, earlier, clip_at, tile, ways):
+    frames, _, rows, width = keep.shape
+    model = own_weight.shape[1]
+    tiles = model // tile
+    context = pl.BlockSpec((frames, 1, rows, width), lambda n, w: (0, w[0], 0, 0))
+    weight = pl.BlockSpec((width, tile), lambda n, w: (0, n))
+    residual = pl.BlockSpec((frames, 1, rows, tile), lambda n, w: (0, clip_at, 0, n))
+    piece = (frames * rows // ways, model)
+    return pl.pallas_call(
+        functools.partial(norm_kernel, tiles, tile, ways),
+        grid_spec=pltpu.PrefetchScalarGridSpec(
+            num_scalar_prefetch=1,
+            grid=(tiles,),
+            in_specs=[
+                context, context, weight, weight,
+                pl.BlockSpec((frames * rows, tile), lambda n, w: (0, n)),
+                residual,
+                pl.BlockSpec((1, model), lambda n, w: (0, 0)),
+            ] + [pl.BlockSpec(memory_space=pl.ANY)] * len(earlier),
+            out_specs=[residual] + [pl.BlockSpec(piece, lambda n, w: (0, 0))] * ways,
+            scratch_shapes=[pltpu.VMEM((tiles, frames * rows, tile), jnp.float32)],
+        ),
+        out_shape=[jax.ShapeDtypeStruct(resid.shape, jnp.bfloat16)]
+        + [jax.ShapeDtypeStruct(piece, jnp.bfloat16)] * ways,
+        input_output_aliases={8: 0} if earlier else {},
+        compiler_params=pltpu.CompilerParams(vmem_limit_bytes=40 * MIB),
+        cost_estimate=branch_cost(frames, rows, width, model),
+    )(where, keep, came, own_weight, other_weight, branch, resid, gain, *earlier)
+
+
+def project_kernel(steps, ways, share, piece_rows, where, *refs):
+    pieces = refs[:steps * 2 * ways]
+    at = steps * 2 * ways
+    own_ref, near, far = refs[at], refs[at + 1:at + ways], refs[at + ways:at + 2 * ways - 1]
+    outs = refs[at + 2 * ways - 1:at + 3 * ways - 1]
+    rows_buf, weight_buf, qkv_buf, rows_sem, weight_sem = refs[at + 3 * ways - 1:]
+    plane, home = where[3], where[2]
+    half = near[0].shape[0]
+    group = ways * piece_rows
+    heads = qkv_buf.shape[2] // HD
+
+    copies = [pltpu.make_async_copy(
+        own_ref, weight_buf.at[pl.ds(pl.multiple_of(home * 2 * half, half), 2 * half)],
+        weight_sem.at[0])]
+    for way in range(1, ways):
+        base = lax.rem(home + ways - way, ways) * 2 * half
+        copies.append(pltpu.make_async_copy(
+            near[way - 1],
+            weight_buf.at[pl.ds(pl.multiple_of(base + plane * half, half), half)],
+            weight_sem.at[2 * way - 1]))
+        copies.append(pltpu.make_async_copy(
+            far[way - 1],
+            weight_buf.at[pl.ds(pl.multiple_of(base + (1 - plane) * half, half), half)],
+            weight_sem.at[2 * way]))
+
+    def row_copies(step):
+        slot = step % 2
+        return [pltpu.make_async_copy(
+            pieces[step * 2 * ways + n],
+            rows_buf.at[slot, pl.ds(n * piece_rows, piece_rows)],
+            rows_sem.at[slot, n]) for n in range(2 * ways)]
+
+    for copy in row_copies(0):
+        copy.start()
+    for copy in copies:
+        copy.start()
+    position_q = lax.broadcasted_iota(jnp.int32, (group, group), 0)
+    position_k = lax.broadcasted_iota(jnp.int32, (group, group), 1)
+    same = lax.rem(position_q, share) == lax.rem(position_k, share)
+
+    def body(step, carry):
+        slot = lax.rem(step, 2)
+        for n in range(steps):
+            @pl.when(step == n)
+            def _():
+                if n + 1 < steps:
+                    for copy in row_copies(n + 1):
+                        copy.start()
+                for copy in row_copies(n):
+                    copy.wait()
+                if n == 0:
+                    for copy in copies:
+                        copy.wait()
+
+        def column(part, carry):
+            lanes = pl.ds(pl.multiple_of(part * heads * HD, heads * HD), heads * HD)
+            qkv_buf[part] = jnp.dot(
+                rows_buf[slot], weight_buf[:, lanes], preferred_element_type=jnp.float32
+            ).astype(jnp.bfloat16)
+            return carry
+
+        lax.fori_loop(0, 3, column, 0)
+        for which in range(2):
+            rows = slice(which * group, (which + 1) * group)
+            for head in range(heads):
+                lanes = slice(head * HD, (head + 1) * HD)
+                context = attend(
+                    qkv_buf[0, rows, lanes], qkv_buf[1, rows, lanes], qkv_buf[2, rows, lanes], same
+                )
+                for way in range(ways):
+                    outs[way][step * 2 + which, :, lanes] = context[
+                        way * piece_rows:(way + 1) * piece_rows
+                    ]
+        return carry
+
+    lax.fori_loop(0, steps, body, 0)
+
+
+def project(where, pieces, own, near, far, ways, share):
+    groups = len(pieces)
+    steps = groups // 2
+    piece_rows, model = pieces[0][0].shape
+    width = own.shape[1] // 3
+    flat = [piece for group in pieces for piece in group]
+    rows = piece_rows * ways * groups
+    out = (groups, piece_rows, width)
+    return pl.pallas_call(
+        functools.partial(project_kernel, steps, ways, share, piece_rows),
+        grid_spec=pltpu.PrefetchScalarGridSpec(
+            num_scalar_prefetch=1,
+            grid=(1,),
+            in_specs=[pl.BlockSpec(memory_space=pl.ANY)] * (len(flat) + 2 * ways - 1),
+            out_specs=[pl.BlockSpec(out, lambda n, w: (0, 0, 0))] * ways,
+            scratch_shapes=[
+                pltpu.VMEM((2, 2 * ways * piece_rows, model), jnp.bfloat16),
+                pltpu.VMEM((model, 3 * width), jnp.bfloat16),
+                pltpu.VMEM((3, 2 * ways * piece_rows, width), jnp.bfloat16),
+                pltpu.SemaphoreType.DMA((2, 2 * ways)),
+                pltpu.SemaphoreType.DMA((2 * ways - 1,)),
+            ],
+        ),
+        out_shape=[jax.ShapeDtypeStruct(out, jnp.bfloat16)] * ways,
+        compiler_params=pltpu.CompilerParams(vmem_limit_bytes=48 * MIB),
+        cost_estimate=pl.CostEstimate(
+            flops=6 * rows * model * width,
+            bytes_accessed=2 * rows * model + 6 * model * width,
+            transcendentals=rows * ways * piece_rows,
+        ),
+    )(where, *flat, own, *near, *far)
+
+
+def assemble_kernel(clips, sources, ways, groups, share, where, *refs):
+    out_ref = refs[-1]
+    width = refs[0].shape[-1]
+    for clip in range(clips):
+        for source in range(sources):
+            side = where[0] if source % 2 == 0 else 1 - where[0]
+            core = where[1] if source < 2 else 1 - where[1]
+            for way in range(ways):
+                origin = lax.rem(where[2] + ways - way, ways)
+                row = pl.multiple_of(
+                    ((side * 2 + core) * ways + origin) * share, share
+                )
+                for group in range(groups):
+                    out_ref[0, clip, pl.ds(row, share), group * width:(group + 1) * width] = refs[
+                        (clip * groups + group) * ways + way
+                    ][source]
+
+
+def assemble(where, arrived, frames, patches, share):
+    clips, groups, ways = len(arrived), len(arrived[0]), len(arrived[0][0])
+    flat = [array for clip in arrived for group in clip for array in group]
+    sources, _, width = flat[0].shape
+    return pl.pallas_call(
+        functools.partial(assemble_kernel, clips, sources, ways, groups, share),
+        grid_spec=pltpu.PrefetchScalarGridSpec(
+            num_scalar_prefetch=1,
+            grid=(frames,),
+            in_specs=[pl.BlockSpec((sources, share, width), lambda f, w: (0, f, 0))] * len(flat),
+            out_specs=pl.BlockSpec(
+                (1, clips, patches, groups * width), lambda f, w: (f, 0, 0, 0)
+            ),
+        ),
+        out_shape=jax.ShapeDtypeStruct((frames, clips, patches, groups * width), jnp.bfloat16),
+        compiler_params=pltpu.CompilerParams(vmem_limit_bytes=32 * MIB),
+    )(where, *flat)
+
+
+def per_device(ways, resid, spatial_q, spatial_k, spatial_v, out_weight, norm_gain, qkv_weight):
+    frames, clips, rows, model = resid.shape
+    patches, width = spatial_q.shape[2:]
+    share = rows // ways
+    block = qkv_weight.shape[0]
+    groups = 3
+    tile = 1024
+
+    plane, home, place = lax.axis_index("clip"), lax.axis_index("tm"), lax.axis_index("tensor")
+    where = jnp.stack([place // 2, place % 2, home, plane]).astype(jnp.int32)
+
+    def other_core(array):
+        return lax.ppermute(array, "tensor", [(0, 1), (1, 0), (2, 3), (3, 2)])
+
+    def other_side(array):
+        return lax.ppermute(array, "tensor", [(0, 2), (2, 0), (1, 3), (3, 1)])
+
+    def other_plane(array):
+        return lax.ppermute(array, "clip", [(0, 1), (1, 0)])
+
+    def along(array, way):
+        return lax.ppermute(array, "tm", [(n, (n + way) % ways) for n in range(ways)])
+
+    per_group = width // groups
+    own, near, far = [], [], []
+    for group in range(groups):
+        columns = qkv_weight[:, :, group * per_group:(group + 1) * per_group].reshape(
+            block, 3 * per_group
+        )
+        own.append(columns)
+        travelling = lax.dynamic_slice_in_dim(columns, plane * (block // 2), block // 2, 0)
+        near.append([])
+        far.append([])
+        for _ in range(1, ways):
+            travelling = along(travelling, 1)
+            near[-1].append(travelling)
+            far[-1].append(other_plane(travelling))
+
+    other_weight = other_core(out_weight)
+    gain = norm_gain.reshape(1, model)
+
+    written = []
+    attended = []
+    for clip in range(clips):
+        keep, send = spatial(where, spatial_q, spatial_k, spatial_v, clip, rows)
+        attended.append((keep, other_core(send)))
+    branches = []
+    for clip in range(clips):
+        branches.append(other_side(
+            branch_for_other(where, *attended[clip], out_weight, other_weight, tile)
+        ))
+    gathered = []
+    for clip in range(clips):
+        resid_out, *normed = norm(
+            where, *attended[clip], out_weight, other_weight, branches[clip], resid, gain,
+            written, clip, tile, ways,
+        )
+        written = [resid_out]
+        mine = [normed[0]] + [along(normed[way], way) for way in range(1, ways)]
+        beside = [other_side(piece) for piece in mine]
+        gathered.append([
+            mine, beside, [other_core(piece) for piece in mine],
+            [other_core(piece) for piece in beside],
+        ])
+
+    arrived = [[None] * groups for _ in range(clips)]
+    for group in range(groups):
+        for clip in range(clips):
+            contexts = project(
+                where, gathered[clip], own[group], near[group], far[group], ways, share
+            )
+            arrived[clip][group] = [contexts[0]] + [
+                along(contexts[way], ways - way) for way in range(1, ways)
+            ]
+    ordered = [
+        [[got[0]] + [got[ways - way] for way in range(1, ways)] for got in by_group]
+        for by_group in arrived
+    ]
+    temporal_ctx = assemble(where, ordered, frames, patches, share)
     return (resid_out, temporal_ctx)
 
 
@@ -95,8 +488,9 @@
         P(),
         P("tm", None, "tensor"),
     )
+    small = mesh.shape["clip"] == 2 and mesh.shape["tm"] == 4 and mesh.shape["tensor"] == 4
     return jax.shard_map(
-        per_device,
+        functools.partial(per_device, mesh.shape["tm"]) if small else per_device_plain,
         mesh=mesh,
         in_specs=placed,
         out_specs=(P("tm", "clip", "tensor", None), P("tm", "clip", None, "tensor")),

time: 1220 us -> 639 us (0.52)
  waiting for transfers between devices: 614 us -> 317 us
  blocking collectives: 291 us -> 0 us
  Pallas kernels: 0 us -> 175 us
  matrix products: 130 us -> 0 us
  starting transfers between devices: 0.38 us -> 81.8 us
  local copies, waits for them, and re-layouts: 117 us -> 63.2 us
  other arithmetic: 44.8 us -> 0.08 us
  between operations: 15.8 us -> 1.09 us
    all_gather x2 -> x0, waiting for transfers between devices: 441 us -> none  [the longest x1 287 us: per_device(): block_rows = lax.all_gather(qkv_weight, 'tm', axis=0, tiled=True)]
    ppermute x0 -> x71, waiting for transfers between devices: none -> 317 us  [the longest x33 191 us: along(): lax.ppermute(array, 'tm', [(n, (n + way) % ways) for n in range(ways)])]
    all_to_all x2 -> x0, blocking collectives: 291 us -> none  [the longest x1 219 us: per_device(): lax.all_to_all(projected, 'tm', split_axis=2, concat_axis=0, tiled=True)]
    pallas_call x0 -> x13, Pallas kernels: none -> 175 us  [the longest x6 109 us: project(): pl.pallas_call(functools.partial(project_kernel, steps, ways, share, piec...]
    reduce_scatter x1 -> x0, waiting for transfers between devices: 172 us -> none  [per_device(): lax.psum_scatter(jnp.einsum('pfcj,jd->pfcd', patch_major, out_weight, pre...]
    dot_general x5 -> x0, matrix products: 119 us -> none  [the longest x1 74.8 us: per_device(): jnp.dot(flat_rows, block_rows.reshape(block_rows.shape[0], qkv_width), pr...]
    ppermute x0 -> x71, starting transfers between devices: none -> 81.8 us  [the longest x33 53.5 us: along(): lax.ppermute(array, 'tm', [(n, (n + way) % ways) for n in range(ways)])]
    reshape x4 -> x3, local copies, waits for them, and re-layouts: 46.7 us -> 13.2 us  [per_device(): qkv_weight[:, :, group * per_group:(group + 1) * per_group]]
  transfers between devices with their start and end apart: 3 -> 71, of which waited for: 3 -> 23; matrix products, arithmetic and copies ran while one was open for 2% -> 6% of each run, Pallas kernels for 0% -> 27%
where the time goes in v1:
time: 639 us; the launch traced here: 638 us
  waiting for transfers between devices  317 us (50%)
  Pallas kernels  175 us (27%)
  starting transfers between devices  81.8 us (13%)
  local copies, waits for them, and re-layouts  63.2 us (10%)
    ppermute x33, waiting for transfers between devices, along(): lax.ppermute(array, 'tm', [(n, (n + way) % ways) for n in range(ways)])  191 us
    pallas_call x6, Pallas kernels, project(): pl.pallas_call(functools.partial(project_kernel, steps, ways, share, piec...  109 us
    ppermute x10, waiting for transfers between devices, other_side(): return lax.ppermute(array, 'tensor', [(0, 2), (2, 0), (1, 3), (3, 1)])  72.1 us
    ppermute x9, waiting for transfers between devices, other_plane(): return lax.ppermute(array, 'clip', [(0, 1), (1, 0)])  54.1 us
    ppermute x33, starting transfers between devices, along(): lax.ppermute(array, 'tm', [(n, (n + way) % ways) for n in range(ways)])  53.5 us
    unnamed x89, local copies, waits for them, and re-layouts  38.1 us
    pallas_call x2, Pallas kernels, norm(): pl.pallas_call(functools.partial(norm_kernel, tiles, tile, ways), grid_sp...  28.2 us
    pallas_call x2, Pallas kernels, branch_for_other(): pl.pallas_call(send_kernel, grid_spec=pltpu.PrefetchScalarGridSpec(num_sc...  20.3 us
  transfers between devices with their start and end apart: 71, of which 23 were waited for; matrix products, arithmetic and copies ran while one was open for 6% of the time, Pallas kernels for 27%

profile of v1, /device:TPU:0, one launch (start us, length us, event | category | flops | bytes accessed | tf_op | source)
XLA Modules:
  0.0 638.1 jit_solution(14366725110536065693)
XLA Ops:
  1.1 5.8 fusion
  6.9 2.4 copy.25
  9.4 4.5 copy.15.refs_16_
  13.8 2.4 constant_dynamic-slice_fusion.2
  16.2 2.6 collective-permute-start.20
  18.9 1.9 copy-done.4
  20.8 1.9 copy-done.6
  22.6 6.8 %shard_map.86 = (bf16[4,2,64,768]{3,2,1,0:T(8,128)(2,1)S(1)}, bf16[4,2,64,768]{3,2,1,0:T(8,128)(2,1)}) custom-call(s32[4]{0:T(128)S(1)} %pad_add_fusion.where, bf16[4,2,256,768]{3,2,1,0:T(8,128)(2,1)S(1)} %copy-done.3, bf16[4,2,256,768]{3,2,1,0:T(8,128)(2,1)S(1)} %copy-done.4, bf16[4,2,256,768]{3,2,1,0:T(8,128)(2,1)S(1)} %copy-done.6), custom_call_target="tpu_custom_call" | custom-call | flops 805306368 | bytes 6291456 | tf_op jit(solution)/shard_map/pallas_call | solution.py:122
  30.5 4.3 copy.26
  34.8 4.3 copy.18.refs_16_
  39.1 2.4 constant_dynamic-slice_fusion.1
  43.1 1.9 copy-done.5
  45.0 1.9 copy-done.7
  46.9 6.8 %shard_map.88 = (bf16[4,2,64,768]{3,2,1,0:T(8,128)(2,1)S(1)}, bf16[4,2,64,768]{3,2,1,0:T(8,128)(2,1)}) custom-call(s32[4]{0:T(128)S(1)} %pad_add_fusion.where, bf16[4,2,256,768]{3,2,1,0:T(8,128)(2,1)S(1)} %copy-done.3, bf16[4,2,256,768]{3,2,1,0:T(8,128)(2,1)S(1)} %copy-done.5, bf16[4,2,256,768]{3,2,1,0:T(8,128)(2,1)S(1)} %copy-done.7), custom_call_target="tpu_custom_call" | custom-call | flops 805306368 | bytes 6291456 | tf_op jit(solution)/shard_map/pallas_call | solution.py:122
  54.5 4.3 copy.27
  58.8 4.4 copy.21.refs_16_
  68.9 4.3 collective-permute-done.29.refs_17_
  74.9 3.7 copy-done
  79.7 9.8 %shard_map.89 = bf16[256,6144]{1,0:T(8,128)(2,1)S(1)} custom-call(s32[4]{0:T(128)S(1)} %pad_add_fusion.where, bf16[4,2,64,768]{3,2,1,0:T(8,128)(2,1)S(1)} %copy-done.11, bf16[4,2,64,768]{3,2,1,0:T(8,128)(2,1)S(1)} %copy-done.14, bf16[768,6144]{1,0:T(8,128)(2,1)S(1)} %copy-done, bf16[768,6144]{1,0:T(8,128)(2,1)} %collective-permute-done.1.other_ref), custom_call_target="tpu_custom_call" | custom-call | flops 4831838208 | bytes 31457280 | tf_op jit(solution)/shard_map/pallas_call | solution.py:170
  89.5 8.9 %collective-permute-done.38.refs_17_ = bf16[768,768]{1,0:T(8,128)(2,1)S(1)} collective-permute-done((bf16[768,768]{1,0:T(8,128)(2,1)S(1)}, bf16[768,768]{1,0:T(8,128)(2,1)S(1)}, u32[]{:S(2)}, u32[]{:S(2)}) %collective-permute-start.38) | collective-permute-done | bytes 1179680 | tf_op jit(solution)/shard_map/ppermute | solution.py:420
  98.4 1.7 collective-permute-start.4
  100.1 23.7 %collective-permute-done.21.refs_18_ = bf16[768,768]{1,0:T(8,128)(2,1)} collective-permute-done((bf16[768,768]{1,0:T(8,128)(2,1)}, bf16[768,768]{1,0:T(8,128)(2,1)}, u32[]{:S(2)}, u32[]{:S(2)}) %collective-permute-start.21) | collective-permute-done | bytes 1179680 | tf_op jit(solution)/shard_map/ppermute | solution.py:420
  125.4 23.5 %collective-permute-done.30.refs_18_ = bf16[768,768]{1,0:T(8,128)(2,1)S(1)} collective-permute-done((bf16[768,768]{1,0:T(8,128)(2,1)}, bf16[768,768]{1,0:T(8,128)(2,1)S(1)}, u32[]{:S(2)}, u32[]{:S(2)}) %collective-permute-start.30) | collective-permute-done | bytes 1179680 | tf_op jit(solution)/shard_map/ppermute | solution.py:420
  149.0 1.7 collective-permute-start.24
  150.7 10.5 %shard_map.87 = bf16[256,6144]{1,0:T(8,128)(2,1)} custom-call(s32[4]{0:T(128)S(1)} %pad_add_fusion.where, bf16[4,2,64,768]{3,2,1,0:T(8,128)(2,1)S(1)} %copy-done.9, bf16[4,2,64,768]{3,2,1,0:T(8,128)(2,1)} %collective-permute-done.came_ref, bf16[768,6144]{1,0:T(8,128)(2,1)S(1)} %bitcast.9, bf16[768,6144]{1,0:T(8,128)(2,1)} %collective-permute-done.1.other_ref), custom_call_target="tpu_custom_call" | custom-call | flops 4831838208 | bytes 31457280 | tf_op jit(solution)/shard_map/pallas_call | solution.py:170
  161.2 13.1 %collective-permute-done.39.refs_18_ = bf16[768,768]{1,0:T(8,128)(2,1)} collective-permute-done((bf16[768,768]{1,0:T(8,128)(2,1)S(1)}, bf16[768,768]{1,0:T(8,128)(2,1)}, u32[]{:S(2)}, u32[]{:S(2)}) %collective-permute-start.39) | collective-permute-done | bytes 1179680 | tf_op jit(solution)/shard_map/ppermute | solution.py:420
  174.3 1.7 collective-permute-start.2
  176.1 23.6 %collective-permute-done.22.refs_19_ = bf16[768,768]{1,0:T(8,128)(2,1)} collective-permute-done((bf16[768,768]{1,0:T(8,128)(2,1)}, bf16[768,768]{1,0:T(8,128)(2,1)}, u32[]{:S(2)}, u32[]{:S(2)}) %collective-permute-start.22) | collective-permute-done | bytes 1179680 | tf_op jit(solution)/shard_map/ppermute | solution.py:420
  201.3 23.5 %collective-permute-done.31.refs_19_ = bf16[768,768]{1,0:T(8,128)(2,1)S(1)} collective-permute-done((bf16[768,768]{1,0:T(8,128)(2,1)S(1)}, bf16[768,768]{1,0:T(8,128)(2,1)S(1)}, u32[]{:S(2)}, u32[]{:S(2)}) %collective-permute-start.31) | collective-permute-done | bytes 1179680 | tf_op jit(solution)/shard_map/ppermute | solution.py:420
  228.6 21.3 %collective-permute-done.40.refs_19_ = bf16[768,768]{1,0:T(8,128)(2,1)S(1)} collective-permute-done((bf16[768,768]{1,0:T(8,128)(2,1)}, bf16[768,768]{1,0:T(8,128)(2,1)S(1)}, u32[]{:S(2)}, u32[]{:S(2)}) %collective-permute-start.40) | collective-permute-done | bytes 1179680 | tf_op jit(solution)/shard_map/ppermute | solution.py:420
  251.4 1.7 copy-done.16
  253.6 2.8 copy-done.1
  256.4 1.9 copy-done.17
  258.3 13.9 %shard_map.90 = (bf16[4,2,64,6144]{3,2,1,0:T(8,128)(2,1)}, bf16[64,6144]{1,0:T(8,128)(2,1)S(1)}, bf16[64,6144]{1,0:T(8,128)(2,1)S(1)}, bf16[64,6144]{1,0:T(8,128)(2,1)S(1)}, bf16[64,6144]{1,0:T(8,128)(2,1)S(1)}) custom-call(s32[4]{0:T(128)S(1)} %pad_add_fusion.where, bf16[4,2,64,768]{3,2,1,0:T(8,128)(2,1)S(1)} %copy-done.12, ...), custom_call_target="tpu_custom_call" | custom-call | flops 4831838208 | bytes 31457280 | tf_op jit(solution)/shard_map/pallas_call | solution.py:229
  272.3 7.0 %collective-permute-done.25.refs_22_ = bf16[768,768]{1,0:T(8,128)(2,1)} collective-permute-done((bf16[768,768]{1,0:T(8,128)(2,1)}, bf16[768,768]{1,0:T(8,128)(2,1)}, u32[]{:S(2)}, u32[]{:S(2)}) %collective-permute-start.25) | collective-permute-done | bytes 1179680 | tf_op jit(solution)/shard_map/ppermute | solution.py:417
  280.2 24.3 %collective-permute-done.34.refs_22_ = bf16[768,768]{1,0:T(8,128)(2,1)} collective-permute-done((bf16[768,768]{1,0:T(8,128)(2,1)S(1)}, bf16[768,768]{1,0:T(8,128)(2,1)}, u32[]{:S(2)}, u32[]{:S(2)}) %collective-permute-start.34) | collective-permute-done | bytes 1179680 | tf_op jit(solution)/shard_map/ppermute | solution.py:417
  304.5 2.0 collective-permute-start.7
  306.5 22.0 %collective-permute-done.43.refs_22_ = bf16[768,768]{1,0:T(8,128)(2,1)} collective-permute-done((bf16[768,768]{1,0:T(8,128)(2,1)S(1)}, bf16[768,768]{1,0:T(8,128)(2,1)}, u32[]{:S(2)}, u32[]{:S(2)}) %collective-permute-start.43) | collective-permute-done | bytes 1179680 | tf_op jit(solution)/shard_map/ppermute | solution.py:417
  332.0 6.2 collective-permute-done.7.refs_3_
  339.3 9.7 %collective-permute-done.8.refs_4_ = bf16[64,6144]{1,0:T(8,128)(2,1)S(1)} collective-permute-done((bf16[64,6144]{1,0:T(8,128)(2,1)S(1)}, bf16[64,6144]{1,0:T(8,128)(2,1)S(1)}, u32[]{:S(2)}, u32[]{:S(2)}) %collective-permute-start.8) | collective-permute-done | bytes 786464 | tf_op jit(solution)/shard_map/ppermute | solution.py:414
  349.5 16.3 %collective-permute-done.9.refs_5_ = bf16[64,6144]{1,0:T(8,128)(2,1)S(1)} collective-permute-done((bf16[64,6144]{1,0:T(8,128)(2,1)S(1)}, bf16[64,6144]{1,0:T(8,128)(2,1)S(1)}, u32[]{:S(2)}, u32[]{:S(2)}) %collective-permute-start.9) | collective-permute-done | bytes 786464 | tf_op jit(solution)/shard_map/ppermute | solution.py:414
  365.9 16.8 %collective-permute-done.10.refs_6_ = bf16[64,6144]{1,0:T(8,128)(2,1)S(1)} collective-permute-done((bf16[64,6144]{1,0:T(8,128)(2,1)S(1)}, bf16[64,6144]{1,0:T(8,128)(2,1)S(1)}, u32[]{:S(2)}, u32[]{:S(2)}) %collective-permute-start.10) | collective-permute-done | bytes 786464 | tf_op jit(solution)/shard_map/ppermute | solution.py:414
  382.7 14.6 %collective-permute-done.11.refs_7_ = bf16[64,6144]{1,0:T(8,128)(2,1)S(1)} collective-permute-done((bf16[64,6144]{1,0:T(8,128)(2,1)S(1)}, bf16[64,6144]{1,0:T(8,128)(2,1)S(1)}, u32[]{:S(2)}, u32[]{:S(2)}) %collective-permute-start.11) | collective-permute-done | bytes 786464 | tf_op jit(solution)/shard_map/ppermute | solution.py:414
  398.8 2.8 copy-done.2
  401.6 14.3 %shard_map.91 = (bf16[4,2,64,6144]{3,2,1,0:T(8,128)(2,1)}, bf16[64,6144]{1,0:T(8,128)(2,1)S(1)}, bf16[64,6144]{1,0:T(8,128)(2,1)S(1)}, bf16[64,6144]{1,0:T(8,128)(2,1)S(1)}, bf16[64,6144]{1,0:T(8,128)(2,1)}) custom-call(s32[4]{0:T(128)S(1)} %pad_add_fusion.where, bf16[4,2,64,768]{3,2,1,0:T(8,128)(2,1)S(1)} %copy-done.9, ...), custom_call_target="tpu_custom_call", output_to_operand_aliasing={{0}: (8, {})} | custom-call | flops 4831838208 | bytes 31457280 | tf_op jit(solution)/shard_map/pallas_call | solution.py:229
  417.1 2.1 collective-permute-start.48
  419.2 1.8 collective-permute-start.49
  421.0 18.2 %shard_map.92 = (bf16[4,64,256]{2,1,0:T(8,128)(2,1)S(1)}, bf16[4,64,256]{2,1,0:T(8,128)(2,1)S(1)}, bf16[4,64,256]{2,1,0:T(8,128)(2,1)S(1)}, bf16[4,64,256]{2,1,0:T(8,128)(2,1)S(1)}) custom-call(s32[4]{0:T(128)S(1)} %pad_add_fusion.where, bf16[64,6144]{1,0:T(8,128)(2,1)S(1)} %get-tuple-element.46.refs_0_, ...), custom_call_target="tpu_custom_call" | custom-call | flops 9663676416 | bytes 22020096 | tf_op jit(solution)/shard_map/pallas_call | solution.py:337
  440.3 31.8 %collective-permute-done.48.refs_2_ = bf16[64,6144]{1,0:T(8,128)(2,1)S(1)} collective-permute-done((bf16[64,6144]{1,0:T(8,128)(2,1)S(1)}, bf16[64,6144]{1,0:T(8,128)(2,1)S(1)}, u32[]{:S(2)}, u32[]{:S(2)}) %collective-permute-start.48) | collective-permute-done | bytes 786464 | tf_op jit(solution)/shard_map/ppermute | solution.py:420
  475.6 18.2 %shard_map.93 = (bf16[4,64,256]{2,1,0:T(8,128)(2,1)S(1)}, bf16[4,64,256]{2,1,0:T(8,128)(2,1)S(1)}, bf16[4,64,256]{2,1,0:T(8,128)(2,1)S(1)}, bf16[4,64,256]{2,1,0:T(8,128)(2,1)S(1)}) custom-call(s32[4]{0:T(128)S(1)} %pad_add_fusion.where, bf16[64,6144]{1,0:T(8,128)(2,1)S(1)} %get-tuple-element.46.refs_0_, ...), custom_call_target="tpu_custom_call" | custom-call | flops 9663676416 | bytes 22020096 | tf_op jit(solution)/shard_map/pallas_call | solution.py:337
  494.4 14.6 %collective-permute-done.53.refs_7_ = bf16[64,6144]{1,0:T(8,128)(2,1)S(1)} collective-permute-done((bf16[64,6144]{1,0:T(8,128)(2,1)S(1)}, bf16[64,6144]{1,0:T(8,128)(2,1)S(1)}, u32[]{:S(2)}, u32[]{:S(2)}) %collective-permute-start.53) | collective-permute-done | bytes 786464 | tf_op jit(solution)/shard_map/ppermute | solution.py:414
  510.6 18.2 %shard_map.94 = (bf16[4,64,256]{2,1,0:T(8,128)(2,1)S(1)}, bf16[4,64,256]{2,1,0:T(8,128)(2,1)S(1)}, bf16[4,64,256]{2,1,0:T(8,128)(2,1)S(1)}, bf16[4,64,256]{2,1,0:T(8,128)(2,1)S(1)}) custom-call(s32[4]{0:T(128)S(1)} %pad_add_fusion.where, bf16[64,6144]{1,0:T(8,128)(2,1)S(1)} %get-tuple-element.46.refs_0_, ...), custom_call_target="tpu_custom_call" | custom-call | flops 9663676416 | bytes 22020096 | tf_op jit(solution)/shard_map/pallas_call | solution.py:337
  528.9 16.3 %collective-permute-start.26 = (bf16[4,64,256]{2,1,0:T(8,128)(2,1)S(1)}, bf16[4,64,256]{2,1,0:T(8,128)(2,1)S(1)}, u32[]{:S(2)}, u32[]{:S(2)}) collective-permute-start(bf16[4,64,256]{2,1,0:T(8,128)(2,1)S(1)} %get-tuple-element.51), channel_id=1, source_target_pairs={{0,4},{4,8},{8,12},{12,0},{1,5},{5,9},{9,13},{13,1},{2,6},{6,10},{... | collective-permute-start | bytes 393224 | tf_op jit(solution)/shard_map/ppermute | solution.py:420
  550.2 18.2 %shard_map.95 = (bf16[4,64,256]{2,1,0:T(8,128)(2,1)S(1)}, bf16[4,64,256]{2,1,0:T(8,128)(2,1)S(1)}, bf16[4,64,256]{2,1,0:T(8,128)(2,1)S(1)}, bf16[4,64,256]{2,1,0:T(8,128)(2,1)S(1)}) custom-call(s32[4]{0:T(128)S(1)} %pad_add_fusion.where, bf16[64,6144]{1,0:T(8,128)(2,1)S(1)} %get-tuple-element.62.refs_0_, ...), custom_call_target="tpu_custom_call" | custom-call | flops 9663676416 | bytes 22020096 | tf_op jit(solution)/shard_map/pallas_call | solution.py:337
  571.9 18.2 %shard_map.96 = (bf16[4,64,256]{2,1,0:T(8,128)(2,1)S(1)}, bf16[4,64,256]{2,1,0:T(8,128)(2,1)S(1)}, bf16[4,64,256]{2,1,0:T(8,128)(2,1)S(1)}, bf16[4,64,256]{2,1,0:T(8,128)(2,1)S(1)}) custom-call(s32[4]{0:T(128)S(1)} %pad_add_fusion.where, bf16[64,6144]{1,0:T(8,128)(2,1)S(1)} %get-tuple-element.62.refs_0_, ...), custom_call_target="tpu_custom_call" | custom-call | flops 9663676416 | bytes 22020096 | tf_op jit(solution)/shard_map/pallas_call | solution.py:337
  590.2 2.9 collective-permute-start.46
  594.1 2.9 collective-permute-start.64
  597.5 18.2 %shard_map.97 = (bf16[4,64,256]{2,1,0:T(8,128)(2,1)S(1)}, bf16[4,64,256]{2,1,0:T(8,128)(2,1)S(1)}, bf16[4,64,256]{2,1,0:T(8,128)(2,1)S(1)}, bf16[4,64,256]{2,1,0:T(8,128)(2,1)S(1)}) custom-call(s32[4]{0:T(128)S(1)} %pad_add_fusion.where, bf16[64,6144]{1,0:T(8,128)(2,1)S(1)} %get-tuple-element.62.refs_0_, ...), custom_call_target="tpu_custom_call" | custom-call | flops 9663676416 | bytes 22020096 | tf_op jit(solution)/shard_map/pallas_call | solution.py:337
  617.2 2.9 collective-permute-start.67
  621.2 2.9 collective-permute-start.70
  624.1 3.5 collective-permute-done.66.refs_18_
  627.5 2.1 collective-permute-done.68.refs_21_
  629.6 5.2 collective-permute-done.69.refs_22_
  634.9 3.3 shard_map.98
  (189 shorter events, 49.8 us)
Async XLA Ops:
  0.6 72.6 %collective-permute-start.1 = (bf16[768,6144]{1,0:T(8,128)(2,1)}, bf16[768,6144]{1,0:T(8,128)(2,1)}, u32[]{:S(2)}, u32[]{:S(2)}) collective-permute-start(bf16[768,6144]{1,0:T(8,128)(2,1)} %own_ref.7), channel_id=1, source_target_pairs={{0,1},{1,0},{2,3},{3,2},{4,5},{5,4},{6,7},{7,6},{8,9},{9,8},{10,11... | collective-permute-start | bytes 28311560 | tf_op jit(solution)/shard_map/ppermute | solution.py:411
  16.2 50.1 %collective-permute-start.20 = (bf16[768,768]{1,0:T(8,128)(2,1)}, bf16[768,768]{1,0:T(8,128)(2,1)}, u32[]{:S(2)}, u32[]{:S(2)}) collective-permute-start(bf16[768,768]{1,0:T(8,128)(2,1)} %constant_dynamic-slice_fusion.2), channel_id=1, source_target_pairs={{0,4},{4,8},{8,12},{12,0},{1,5},{5,9},{9,13},{13,1},{2,6},{6,10},{... | collective-permute-start | bytes 3538952 | tf_op jit(solution)/shard_map/ppermute | solution.py:420
  30.3 34.3 %collective-permute-start = (bf16[4,2,64,768]{3,2,1,0:T(8,128)(2,1)}, bf16[4,2,64,768]{3,2,1,0:T(8,128)(2,1)}, u32[]{:S(2)}, u32[]{:S(2)}) collective-permute-start(bf16[4,2,64,768]{3,2,1,0:T(8,128)(2,1)} %get-tuple-element.41), channel_id=1, source_target_pairs={{0,1},{1,0},{2,3},{3,2},{4,5},{5,4},{6,7},{7,6},{8,9},{9,8},{10,11... | collective-permute-start | bytes 2359304 | tf_op jit(solution)/shard_map/ppermute | solution.py:411
  41.5 31.7 %collective-permute-start.29 = (bf16[768,768]{1,0:T(8,128)(2,1)}, bf16[768,768]{1,0:T(8,128)(2,1)}, u32[]{:S(2)}, u32[]{:S(2)}) collective-permute-start(bf16[768,768]{1,0:T(8,128)(2,1)} %constant_dynamic-slice_fusion.1), channel_id=1, source_target_pairs={{0,4},{4,8},{8,12},{12,0},{1,5},{5,9},{9,13},{13,1},{2,6},{6,10},{... | collective-permute-start | bytes 3538952 | tf_op jit(solution)/shard_map/ppermute | solution.py:420
  64.6 33.8 %collective-permute-start.38 = (bf16[768,768]{1,0:T(8,128)(2,1)S(1)}, bf16[768,768]{1,0:T(8,128)(2,1)S(1)}, u32[]{:S(2)}, u32[]{:S(2)}) collective-permute-start(bf16[768,768]{1,0:T(8,128)(2,1)S(1)} %constant_dynamic-slice_fusion), channel_id=1, source_target_pairs={{0,4},{4,8},{8,12},{12,0},{1,5},{5,9},{9,13},{13,1},{2,6},{6,10},{... | collective-permute-start | bytes 3538952 | tf_op jit(solution)/shard_map/ppermute | solution.py:420
  66.3 57.5 %collective-permute-start.21 = (bf16[768,768]{1,0:T(8,128)(2,1)}, bf16[768,768]{1,0:T(8,128)(2,1)}, u32[]{:S(2)}, u32[]{:S(2)}) collective-permute-start(bf16[768,768]{1,0:T(8,128)(2,1)} %collective-permute-done.20.refs_17_), channel_id=1, source_target_pairs={{0,4},{4,8},{8,12},{12,0},{1,5},{5,9},{9,13},{13,1},{2,6},{6,10},{... | collective-permute-start | bytes 3538952 | tf_op jit(solution)/shard_map/ppermute | solution.py:420
  67.4 56.4 %collective-permute-start.23 = (bf16[768,768]{1,0:T(8,128)(2,1)}, bf16[768,768]{1,0:T(8,128)(2,1)}, u32[]{:S(2)}, u32[]{:S(2)}) collective-permute-start(bf16[768,768]{1,0:T(8,128)(2,1)} %collective-permute-done.20.refs_17_), channel_id=1, source_target_pairs={{0,16},{16,0},{1,17},{17,1},{2,18},{18,2},{3,19},{19,3},{4,20},{20... | collective-permute-start | bytes 3538952 | tf_op jit(solution)/shard_map/ppermute | solution.py:417
  73.2 75.7 %collective-permute-start.30 = (bf16[768,768]{1,0:T(8,128)(2,1)}, bf16[768,768]{1,0:T(8,128)(2,1)S(1)}, u32[]{:S(2)}, u32[]{:S(2)}) collective-permute-start(bf16[768,768]{1,0:T(8,128)(2,1)} %collective-permute-done.29.refs_17_), channel_id=1, source_target_pairs={{0,4},{4,8},{8,12},{12,0},{1,5},{5,9},{9,13},{13,1},{2,6},{6,10},{... | collective-permute-start | bytes 3538952 | tf_op jit(solution)/shard_map/ppermute | solution.py:420
  73.2 75.7 %collective-permute-start.32 = (bf16[768,768]{1,0:T(8,128)(2,1)}, bf16[768,768]{1,0:T(8,128)(2,1)}, u32[]{:S(2)}, u32[]{:S(2)}) collective-permute-start(bf16[768,768]{1,0:T(8,128)(2,1)} %collective-permute-done.29.refs_17_), channel_id=1, source_target_pairs={{0,16},{16,0},{1,17},{17,1},{2,18},{18,2},{3,19},{19,3},{4,20},{20... | collective-permute-start | bytes 3538952 | tf_op jit(solution)/shard_map/ppermute | solution.py:417
  98.4 153.0 %collective-permute-start.4 = (bf16[256,6144]{1,0:T(8,128)(2,1)S(1)}, bf16[256,6144]{1,0:T(8,128)(2,1)S(1)}, u32[]{:S(2)}, u32[]{:S(2)}) collective-permute-start(bf16[256,6144]{1,0:T(8,128)(2,1)S(1)} %shard_map.89), channel_id=1, source_target_pairs={{0,2},{2,0},{1,3},{3,1},{4,6},{6,4},{5,7},{7,5},{8,10},{10,8},{9,1... | collective-permute-start | bytes 9437192 | tf_op jit(solution)/shard_map/ppermute | solution.py:414
  123.8 50.6 %collective-permute-start.39 = (bf16[768,768]{1,0:T(8,128)(2,1)S(1)}, bf16[768,768]{1,0:T(8,128)(2,1)}, u32[]{:S(2)}, u32[]{:S(2)}) collective-permute-start(bf16[768,768]{1,0:T(8,128)(2,1)S(1)} %collective-permute-done.38.refs_17_), channel_id=1, source_target_pairs={{0,4},{4,8},{8,12},{12,0},{1,5},{5,9},{9,13},{13,1},{2,6},{6,10},{... | collective-permute-start | bytes 3538952 | tf_op jit(solution)/shard_map/ppermute | solution.py:420
  123.8 52.2 %collective-permute-start.41 = (bf16[768,768]{1,0:T(8,128)(2,1)S(1)}, bf16[768,768]{1,0:T(8,128)(2,1)S(1)}, u32[]{:S(2)}, u32[]{:S(2)}) collective-permute-start(bf16[768,768]{1,0:T(8,128)(2,1)S(1)} %collective-permute-done.38.refs_17_), channel_id=1, source_target_pairs={{0,16},{16,0},{1,17},{17,1},{2,18},{18,2},{3,19},{19,3},{4,20},{20... | collective-permute-start | bytes 3538952 | tf_op jit(solution)/shard_map/ppermute | solution.py:417
  149.0 50.7 %collective-permute-start.22 = (bf16[768,768]{1,0:T(8,128)(2,1)}, bf16[768,768]{1,0:T(8,128)(2,1)}, u32[]{:S(2)}, u32[]{:S(2)}) collective-permute-start(bf16[768,768]{1,0:T(8,128)(2,1)} %collective-permute-done.21.refs_18_), channel_id=1, source_target_pairs={{0,4},{4,8},{8,12},{12,0},{1,5},{5,9},{9,13},{13,1},{2,6},{6,10},{... | collective-permute-start | bytes 3538952 | tf_op jit(solution)/shard_map/ppermute | solution.py:420
  149.0 52.3 %collective-permute-start.24 = (bf16[768,768]{1,0:T(8,128)(2,1)}, bf16[768,768]{1,0:T(8,128)(2,1)S(1)}, u32[]{:S(2)}, u32[]{:S(2)}) collective-permute-start(bf16[768,768]{1,0:T(8,128)(2,1)} %collective-permute-done.21.refs_18_), channel_id=1, source_target_pairs={{0,16},{16,0},{1,17},{17,1},{2,18},{18,2},{3,19},{19,3},{4,20},{20... | collective-permute-start | bytes 3538952 | tf_op jit(solution)/shard_map/ppermute | solution.py:417
  174.3 155.6 %collective-permute-start.2 = (bf16[256,6144]{1,0:T(8,128)(2,1)}, bf16[256,6144]{1,0:T(8,128)(2,1)S(1)}, u32[]{:S(2)}, u32[]{:S(2)}) collective-permute-start(bf16[256,6144]{1,0:T(8,128)(2,1)} %shard_map.87), channel_id=1, source_target_pairs={{0,2},{2,0},{1,3},{3,1},{4,6},{6,4},{5,7},{7,5},{8,10},{10,8},{9,1... | collective-permute-start | bytes 9437192 | tf_op jit(solution)/shard_map/ppermute | solution.py:414
  176.0 48.8 %collective-permute-start.31 = (bf16[768,768]{1,0:T(8,128)(2,1)S(1)}, bf16[768,768]{1,0:T(8,128)(2,1)S(1)}, u32[]{:S(2)}, u32[]{:S(2)}) collective-permute-start(bf16[768,768]{1,0:T(8,128)(2,1)S(1)} %copy-done.24), channel_id=1, source_target_pairs={{0,4},{4,8},{8,12},{12,0},{1,5},{5,9},{9,13},{13,1},{2,6},{6,10},{... | collective-permute-start | bytes 3538952 | tf_op jit(solution)/shard_map/ppermute | solution.py:420
  199.6 27.6 %collective-permute-start.33 = (bf16[768,768]{1,0:T(8,128)(2,1)S(1)}, bf16[768,768]{1,0:T(8,128)(2,1)S(1)}, u32[]{:S(2)}, u32[]{:S(2)}) collective-permute-start(bf16[768,768]{1,0:T(8,128)(2,1)S(1)} %copy-done.24), channel_id=1, source_target_pairs={{0,16},{16,0},{1,17},{17,1},{2,18},{18,2},{3,19},{19,3},{4,20},{20... | collective-permute-start | bytes 3538952 | tf_op jit(solution)/shard_map/ppermute | solution.py:417
  201.3 48.6 %collective-permute-start.40 = (bf16[768,768]{1,0:T(8,128)(2,1)}, bf16[768,768]{1,0:T(8,128)(2,1)S(1)}, u32[]{:S(2)}, u32[]{:S(2)}) collective-permute-start(bf16[768,768]{1,0:T(8,128)(2,1)} %collective-permute-done.39.refs_18_), channel_id=1, source_target_pairs={{0,4},{4,8},{8,12},{12,0},{1,5},{5,9},{9,13},{13,1},{2,6},{6,10},{... | collective-permute-start | bytes 3538952 | tf_op jit(solution)/shard_map/ppermute | solution.py:420
  224.8 47.4 %collective-permute-start.42 = (bf16[768,768]{1,0:T(8,128)(2,1)}, bf16[768,768]{1,0:T(8,128)(2,1)S(1)}, u32[]{:S(2)}, u32[]{:S(2)}) collective-permute-start(bf16[768,768]{1,0:T(8,128)(2,1)} %collective-permute-done.39.refs_18_), channel_id=1, source_target_pairs={{0,16},{16,0},{1,17},{17,1},{2,18},{18,2},{3,19},{19,3},{4,20},{20... | collective-permute-start | bytes 3538952 | tf_op jit(solution)/shard_map/ppermute | solution.py:417
  227.2 52.1 %collective-permute-start.25 = (bf16[768,768]{1,0:T(8,128)(2,1)}, bf16[768,768]{1,0:T(8,128)(2,1)}, u32[]{:S(2)}, u32[]{:S(2)}) collective-permute-start(bf16[768,768]{1,0:T(8,128)(2,1)} %collective-permute-done.22.refs_19_), channel_id=1, source_target_pairs={{0,16},{16,0},{1,17},{17,1},{2,18},{18,2},{3,19},{19,3},{4,20},{20... | collective-permute-start | bytes 3538952 | tf_op jit(solution)/shard_map/ppermute | solution.py:417
  249.9 54.7 %collective-permute-start.34 = (bf16[768,768]{1,0:T(8,128)(2,1)S(1)}, bf16[768,768]{1,0:T(8,128)(2,1)}, u32[]{:S(2)}, u32[]{:S(2)}) collective-permute-start(bf16[768,768]{1,0:T(8,128)(2,1)S(1)} %collective-permute-done.31.refs_19_), channel_id=1, source_target_pairs={{0,16},{16,0},{1,17},{17,1},{2,18},{18,2},{3,19},{19,3},{4,20},{20... | collective-permute-start | bytes 3538952 | tf_op jit(solution)/shard_map/ppermute | solution.py:417
  253.0 75.5 %collective-permute-start.43 = (bf16[768,768]{1,0:T(8,128)(2,1)S(1)}, bf16[768,768]{1,0:T(8,128)(2,1)}, u32[]{:S(2)}, u32[]{:S(2)}) collective-permute-start(bf16[768,768]{1,0:T(8,128)(2,1)S(1)} %collective-permute-done.40.refs_19_), channel_id=1, source_target_pairs={{0,16},{16,0},{1,17},{17,1},{2,18},{18,2},{3,19},{19,3},{4,20},{20... | collective-permute-start | bytes 3538952 | tf_op jit(solution)/shard_map/ppermute | solution.py:417
  272.2 57.7 %collective-permute-start.5 = (bf16[64,6144]{1,0:T(8,128)(2,1)S(1)}, bf16[64,6144]{1,0:T(8,128)(2,1)S(1)}, u32[]{:S(2)}, u32[]{:S(2)}) collective-permute-start(bf16[64,6144]{1,0:T(8,128)(2,1)S(1)} %get-tuple-element.47), channel_id=1, source_target_pairs={{0,4},{4,8},{8,12},{12,0},{1,5},{5,9},{9,13},{13,1},{2,6},{6,10},{... | collective-permute-start | bytes 2359304 | tf_op jit(solution)/shard_map/ppermute | solution.py:420
  279.3 51.4 %collective-permute-start.6 = (bf16[64,6144]{1,0:T(8,128)(2,1)S(1)}, bf16[64,6144]{1,0:T(8,128)(2,1)S(1)}, u32[]{:S(2)}, u32[]{:S(2)}) collective-permute-start(bf16[64,6144]{1,0:T(8,128)(2,1)S(1)} %get-tuple-element.48), channel_id=1, source_target_pairs={{0,8},{4,12},{8,0},{12,4},{1,9},{5,13},{9,1},{13,5},{2,10},{6,14},... | collective-permute-start | bytes 2359304 | tf_op jit(solution)/shard_map/ppermute | solution.py:420
  304.5 33.7 %collective-permute-start.7 = (bf16[64,6144]{1,0:T(8,128)(2,1)S(1)}, bf16[64,6144]{1,0:T(8,128)(2,1)S(1)}, u32[]{:S(2)}, u32[]{:S(2)}) collective-permute-start(bf16[64,6144]{1,0:T(8,128)(2,1)S(1)} %get-tuple-element.49), channel_id=1, source_target_pairs={{0,12},{4,0},{8,4},{12,8},{1,13},{5,1},{9,5},{13,9},{2,14},{6,2},{... | collective-permute-start | bytes 2359304 | tf_op jit(solution)/shard_map/ppermute | solution.py:420
  328.5 20.5 %collective-permute-start.8 = (bf16[64,6144]{1,0:T(8,128)(2,1)S(1)}, bf16[64,6144]{1,0:T(8,128)(2,1)S(1)}, u32[]{:S(2)}, u32[]{:S(2)}) collective-permute-start(bf16[64,6144]{1,0:T(8,128)(2,1)S(1)} %get-tuple-element.46.refs_0_), channel_id=1, source_target_pairs={{0,2},{2,0},{1,3},{3,1},{4,6},{6,4},{5,7},{7,5},{8,10},{10,8},{9,1... | collective-permute-start | bytes 2359304 | tf_op jit(solution)/shard_map/ppermute | solution.py:414
  329.9 35.9 %collective-permute-start.9 = (bf16[64,6144]{1,0:T(8,128)(2,1)S(1)}, bf16[64,6144]{1,0:T(8,128)(2,1)S(1)}, u32[]{:S(2)}, u32[]{:S(2)}) collective-permute-start(bf16[64,6144]{1,0:T(8,128)(2,1)S(1)} %collective-permute-done.5.refs_1_), channel_id=1, source_target_pairs={{0,2},{2,0},{1,3},{3,1},{4,6},{6,4},{5,7},{7,5},{8,10},{10,8},{9,1... | collective-permute-start | bytes 2359304 | tf_op jit(solution)/shard_map/ppermute | solution.py:414
  330.6 52.1 %collective-permute-start.10 = (bf16[64,6144]{1,0:T(8,128)(2,1)S(1)}, bf16[64,6144]{1,0:T(8,128)(2,1)S(1)}, u32[]{:S(2)}, u32[]{:S(2)}) collective-permute-start(bf16[64,6144]{1,0:T(8,128)(2,1)S(1)} %collective-permute-done.6.refs_2_), channel_id=1, source_target_pairs={{0,2},{2,0},{1,3},{3,1},{4,6},{6,4},{5,7},{7,5},{8,10},{10,8},{9,1... | collective-permute-start | bytes 2359304 | tf_op jit(solution)/shard_map/ppermute | solution.py:414
  338.3 59.1 %collective-permute-start.11 = (bf16[64,6144]{1,0:T(8,128)(2,1)S(1)}, bf16[64,6144]{1,0:T(8,128)(2,1)S(1)}, u32[]{:S(2)}, u32[]{:S(2)}) collective-permute-start(bf16[64,6144]{1,0:T(8,128)(2,1)S(1)} %collective-permute-done.7.refs_3_), channel_id=1, source_target_pairs={{0,2},{2,0},{1,3},{3,1},{4,6},{6,4},{5,7},{7,5},{8,10},{10,8},{9,1... | collective-permute-start | bytes 2359304 | tf_op jit(solution)/shard_map/ppermute | solution.py:414
  349.0 48.4 %collective-permute-start.13 = (bf16[64,6144]{1,0:T(8,128)(2,1)S(1)}, bf16[64,6144]{1,0:T(8,128)(2,1)S(1)}, u32[]{:S(2)}, u32[]{:S(2)}) collective-permute-start(bf16[64,6144]{1,0:T(8,128)(2,1)S(1)} %collective-permute-done.5.refs_1_), channel_id=1, source_target_pairs={{0,1},{1,0},{2,3},{3,2},{4,5},{5,4},{6,7},{7,6},{8,9},{9,8},{10,11... | collective-permute-start | bytes 2359304 | tf_op jit(solution)/shard_map/ppermute | solution.py:411
  349.0 48.9 %collective-permute-start.14 = (bf16[64,6144]{1,0:T(8,128)(2,1)S(1)}, bf16[64,6144]{1,0:T(8,128)(2,1)S(1)}, u32[]{:S(2)}, u32[]{:S(2)}) collective-permute-start(bf16[64,6144]{1,0:T(8,128)(2,1)S(1)} %collective-permute-done.6.refs_2_), channel_id=1, source_target_pairs={{0,1},{1,0},{2,3},{3,2},{4,5},{5,4},{6,7},{7,6},{8,9},{9,8},{10,11... | collective-permute-start | bytes 2359304 | tf_op jit(solution)/shard_map/ppermute | solution.py:411
  365.9 50.0 %collective-permute-start.15 = (bf16[64,6144]{1,0:T(8,128)(2,1)S(1)}, bf16[64,6144]{1,0:T(8,128)(2,1)S(1)}, u32[]{:S(2)}, u32[]{:S(2)}) collective-permute-start(bf16[64,6144]{1,0:T(8,128)(2,1)S(1)} %collective-permute-done.7.refs_3_), channel_id=1, source_target_pairs={{0,1},{1,0},{2,3},{3,2},{4,5},{5,4},{6,7},{7,6},{8,9},{9,8},{10,11... | collective-permute-start | bytes 2359304 | tf_op jit(solution)/shard_map/ppermute | solution.py:411
  382.7 34.3 %collective-permute-start.16 = (bf16[64,6144]{1,0:T(8,128)(2,1)S(1)}, bf16[64,6144]{1,0:T(8,128)(2,1)}, u32[]{:S(2)}, u32[]{:S(2)}) collective-permute-start(bf16[64,6144]{1,0:T(8,128)(2,1)S(1)} %collective-permute-done.8.refs_4_), channel_id=1, source_target_pairs={{0,1},{1,0},{2,3},{3,2},{4,5},{5,4},{6,7},{7,6},{8,9},{9,8},{10,11... | collective-permute-start | bytes 2359304 | tf_op jit(solution)/shard_map/ppermute | solution.py:411
  397.4 19.7 %collective-permute-start.17 = (bf16[64,6144]{1,0:T(8,128)(2,1)S(1)}, bf16[64,6144]{1,0:T(8,128)(2,1)}, u32[]{:S(2)}, u32[]{:S(2)}) collective-permute-start(bf16[64,6144]{1,0:T(8,128)(2,1)S(1)} %collective-permute-done.9.refs_5_), channel_id=1, source_target_pairs={{0,1},{1,0},{2,3},{3,2},{4,5},{5,4},{6,7},{7,6},{8,9},{9,8},{10,11... | collective-permute-start | bytes 2359304 | tf_op jit(solution)/shard_map/ppermute | solution.py:411
  397.4 19.7 %collective-permute-start.18 = (bf16[64,6144]{1,0:T(8,128)(2,1)S(1)}, bf16[64,6144]{1,0:T(8,128)(2,1)}, u32[]{:S(2)}, u32[]{:S(2)}) collective-permute-start(bf16[64,6144]{1,0:T(8,128)(2,1)S(1)} %collective-permute-done.10.refs_6_), channel_id=1, source_target_pairs={{0,1},{1,0},{2,3},{3,2},{4,5},{5,4},{6,7},{7,6},{8,9},{9,8},{10,11... | collective-permute-start | bytes 2359304 | tf_op jit(solution)/shard_map/ppermute | solution.py:411
  397.9 21.3 %collective-permute-start.19 = (bf16[64,6144]{1,0:T(8,128)(2,1)S(1)}, bf16[64,6144]{1,0:T(8,128)(2,1)}, u32[]{:S(2)}, u32[]{:S(2)}) collective-permute-start(bf16[64,6144]{1,0:T(8,128)(2,1)S(1)} %collective-permute-done.11.refs_7_), channel_id=1, source_target_pairs={{0,1},{1,0},{2,3},{3,2},{4,5},{5,4},{6,7},{7,6},{8,9},{9,8},{10,11... | collective-permute-start | bytes 2359304 | tf_op jit(solution)/shard_map/ppermute | solution.py:411
  415.9 57.3 %collective-permute-start.50 = (bf16[64,6144]{1,0:T(8,128)(2,1)S(1)}, bf16[64,6144]{1,0:T(8,128)(2,1)S(1)}, u32[]{:S(2)}, u32[]{:S(2)}) collective-permute-start(bf16[64,6144]{1,0:T(8,128)(2,1)S(1)} %get-tuple-element.62.refs_0_), channel_id=1, source_target_pairs={{0,2},{2,0},{1,3},{3,1},{4,6},{6,4},{5,7},{7,5},{8,10},{10,8},{9,1... | collective-permute-start | bytes 2359304 | tf_op jit(solution)/shard_map/ppermute | solution.py:414
  417.0 56.3 %collective-permute-start.54 = (bf16[64,6144]{1,0:T(8,128)(2,1)S(1)}, bf16[64,6144]{1,0:T(8,128)(2,1)S(1)}, u32[]{:S(2)}, u32[]{:S(2)}) collective-permute-start(bf16[64,6144]{1,0:T(8,128)(2,1)S(1)} %get-tuple-element.62.refs_0_), channel_id=1, source_target_pairs={{0,1},{1,0},{2,3},{3,2},{4,5},{5,4},{6,7},{7,6},{8,9},{9,8},{10,11... | collective-permute-start | bytes 2359304 | tf_op jit(solution)/shard_map/ppermute | solution.py:411
  417.0 22.3 %collective-permute-start.47 = (bf16[64,6144]{1,0:T(8,128)(2,1)S(1)}, bf16[64,6144]{1,0:T(8,128)(2,1)S(1)}, u32[]{:S(2)}, u32[]{:S(2)}) collective-permute-start(bf16[64,6144]{1,0:T(8,128)(2,1)S(1)} %get-tuple-element.63), channel_id=1, source_target_pairs={{0,4},{4,8},{8,12},{12,0},{1,5},{5,9},{9,13},{13,1},{2,6},{6,10},{... | collective-permute-start | bytes 2359304 | tf_op jit(solution)/shard_map/ppermute | solution.py:420
  417.1 55.1 %collective-permute-start.48 = (bf16[64,6144]{1,0:T(8,128)(2,1)S(1)}, bf16[64,6144]{1,0:T(8,128)(2,1)S(1)}, u32[]{:S(2)}, u32[]{:S(2)}) collective-permute-start(bf16[64,6144]{1,0:T(8,128)(2,1)S(1)} %get-tuple-element.64), channel_id=1, source_target_pairs={{0,8},{4,12},{8,0},{12,4},{1,9},{5,13},{9,1},{13,5},{2,10},{6,14},... | collective-permute-start | bytes 2359304 | tf_op jit(solution)/shard_map/ppermute | solution.py:420
  419.2 53.0 %collective-permute-start.49 = (bf16[64,6144]{1,0:T(8,128)(2,1)}, bf16[64,6144]{1,0:T(8,128)(2,1)S(1)}, u32[]{:S(2)}, u32[]{:S(2)}) collective-permute-start(bf16[64,6144]{1,0:T(8,128)(2,1)} %get-tuple-element.65), channel_id=1, source_target_pairs={{0,12},{4,0},{8,4},{12,8},{1,13},{5,1},{9,5},{13,9},{2,14},{6,2},{... | collective-permute-start | bytes 2359304 | tf_op jit(solution)/shard_map/ppermute | solution.py:420
  439.4 54.5 %collective-permute-start.51 = (bf16[64,6144]{1,0:T(8,128)(2,1)S(1)}, bf16[64,6144]{1,0:T(8,128)(2,1)S(1)}, u32[]{:S(2)}, u32[]{:S(2)}) collective-permute-start(bf16[64,6144]{1,0:T(8,128)(2,1)S(1)} %collective-permute-done.47.refs_1_), channel_id=1, source_target_pairs={{0,2},{2,0},{1,3},{3,1},{4,6},{6,4},{5,7},{7,5},{8,10},{10,8},{9,1... | collective-permute-start | bytes 2359304 | tf_op jit(solution)/shard_map/ppermute | solution.py:414
  472.2 36.8 %collective-permute-start.55 = (bf16[64,6144]{1,0:T(8,128)(2,1)S(1)}, bf16[64,6144]{1,0:T(8,128)(2,1)S(1)}, u32[]{:S(2)}, u32[]{:S(2)}) collective-permute-start(bf16[64,6144]{1,0:T(8,128)(2,1)S(1)} %collective-permute-done.47.refs_1_), channel_id=1, source_target_pairs={{0,1},{1,0},{2,3},{3,2},{4,5},{5,4},{6,7},{7,6},{8,9},{9,8},{10,11... | collective-permute-start | bytes 2359304 | tf_op jit(solution)/shard_map/ppermute | solution.py:411
  472.2 21.7 %collective-permute-start.52 = (bf16[64,6144]{1,0:T(8,128)(2,1)S(1)}, bf16[64,6144]{1,0:T(8,128)(2,1)S(1)}, u32[]{:S(2)}, u32[]{:S(2)}) collective-permute-start(bf16[64,6144]{1,0:T(8,128)(2,1)S(1)} %collective-permute-done.48.refs_2_), channel_id=1, source_target_pairs={{0,2},{2,0},{1,3},{3,1},{4,6},{6,4},{5,7},{7,5},{8,10},{10,8},{9,1... | collective-permute-start | bytes 2359304 | tf_op jit(solution)/shard_map/ppermute | solution.py:414
  473.1 36.4 %collective-permute-start.56 = (bf16[64,6144]{1,0:T(8,128)(2,1)S(1)}, bf16[64,6144]{1,0:T(8,128)(2,1)S(1)}, u32[]{:S(2)}, u32[]{:S(2)}) collective-permute-start(bf16[64,6144]{1,0:T(8,128)(2,1)S(1)} %collective-permute-done.48.refs_2_), channel_id=1, source_target_pairs={{0,1},{1,0},{2,3},{3,2},{4,5},{5,4},{6,7},{7,6},{8,9},{9,8},{10,11... | collective-permute-start | bytes 2359304 | tf_op jit(solution)/shard_map/ppermute | solution.py:411
  473.4 35.6 %collective-permute-start.53 = (bf16[64,6144]{1,0:T(8,128)(2,1)S(1)}, bf16[64,6144]{1,0:T(8,128)(2,1)S(1)}, u32[]{:S(2)}, u32[]{:S(2)}) collective-permute-start(bf16[64,6144]{1,0:T(8,128)(2,1)S(1)} %collective-permute-done.49.refs_3_), channel_id=1, source_target_pairs={{0,2},{2,0},{1,3},{3,1},{4,6},{6,4},{5,7},{7,5},{8,10},{10,8},{9,1... | collective-permute-start | bytes 2359304 | tf_op jit(solution)/shard_map/ppermute | solution.py:414
  493.8 35.0 %collective-permute-start.57 = (bf16[64,6144]{1,0:T(8,128)(2,1)S(1)}, bf16[64,6144]{1,0:T(8,128)(2,1)S(1)}, u32[]{:S(2)}, u32[]{:S(2)}) collective-permute-start(bf16[64,6144]{1,0:T(8,128)(2,1)S(1)} %collective-permute-done.49.refs_3_), channel_id=1, source_target_pairs={{0,1},{1,0},{2,3},{3,2},{4,5},{5,4},{6,7},{7,6},{8,9},{9,8},{10,11... | collective-permute-start | bytes 2359304 | tf_op jit(solution)/shard_map/ppermute | solution.py:411
  493.9 51.3 %collective-permute-start.58 = (bf16[64,6144]{1,0:T(8,128)(2,1)S(1)}, bf16[64,6144]{1,0:T(8,128)(2,1)}, u32[]{:S(2)}, u32[]{:S(2)}) collective-permute-start(bf16[64,6144]{1,0:T(8,128)(2,1)S(1)} %collective-permute-done.50.refs_4_), channel_id=1, source_target_pairs={{0,1},{1,0},{2,3},{3,2},{4,5},{5,4},{6,7},{7,6},{8,9},{9,8},{10,11... | collective-permute-start | bytes 2359304 | tf_op jit(solution)/shard_map/ppermute | solution.py:411
  509.0 37.5 %collective-permute-start.59 = (bf16[64,6144]{1,0:T(8,128)(2,1)S(1)}, bf16[64,6144]{1,0:T(8,128)(2,1)}, u32[]{:S(2)}, u32[]{:S(2)}) collective-permute-start(bf16[64,6144]{1,0:T(8,128)(2,1)S(1)} %collective-permute-done.51.refs_5_), channel_id=1, source_target_pairs={{0,1},{1,0},{2,3},{3,2},{4,5},{5,4},{6,7},{7,6},{8,9},{9,8},{10,11... | collective-permute-start | bytes 2359304 | tf_op jit(solution)/shard_map/ppermute | solution.py:411
  509.0 38.7 %collective-permute-start.60 = (bf16[64,6144]{1,0:T(8,128)(2,1)S(1)}, bf16[64,6144]{1,0:T(8,128)(2,1)}, u32[]{:S(2)}, u32[]{:S(2)}) collective-permute-start(bf16[64,6144]{1,0:T(8,128)(2,1)S(1)} %collective-permute-done.52.refs_6_), channel_id=1, source_target_pairs={{0,1},{1,0},{2,3},{3,2},{4,5},{5,4},{6,7},{7,6},{8,9},{9,8},{10,11... | collective-permute-start | bytes 2359304 | tf_op jit(solution)/shard_map/ppermute | solution.py:411
  510.4 38.1 %collective-permute-start.61 = (bf16[64,6144]{1,0:T(8,128)(2,1)S(1)}, bf16[64,6144]{1,0:T(8,128)(2,1)}, u32[]{:S(2)}, u32[]{:S(2)}) collective-permute-start(bf16[64,6144]{1,0:T(8,128)(2,1)S(1)} %collective-permute-done.53.refs_7_), channel_id=1, source_target_pairs={{0,1},{1,0},{2,3},{3,2},{4,5},{5,4},{6,7},{7,6},{8,9},{9,8},{10,11... | collective-permute-start | bytes 2359304 | tf_op jit(solution)/shard_map/ppermute | solution.py:411
  528.9 39.6 %collective-permute-start.26 = (bf16[4,64,256]{2,1,0:T(8,128)(2,1)S(1)}, bf16[4,64,256]{2,1,0:T(8,128)(2,1)S(1)}, u32[]{:S(2)}, u32[]{:S(2)}) collective-permute-start(bf16[4,64,256]{2,1,0:T(8,128)(2,1)S(1)} %get-tuple-element.51), channel_id=1, source_target_pairs={{0,4},{4,8},{8,12},{12,0},{1,5},{5,9},{9,13},{13,1},{2,6},{6,10},{... | collective-permute-start | bytes 393224 | tf_op jit(solution)/shard_map/ppermute | solution.py:420
  545.2 24.6 %collective-permute-start.27 = (bf16[4,64,256]{2,1,0:T(8,128)(2,1)S(1)}, bf16[4,64,256]{2,1,0:T(8,128)(2,1)S(1)}, u32[]{:S(2)}, u32[]{:S(2)}) collective-permute-start(bf16[4,64,256]{2,1,0:T(8,128)(2,1)S(1)} %get-tuple-element.52), channel_id=1, source_target_pairs={{0,8},{4,12},{8,0},{12,4},{1,9},{5,13},{9,1},{13,5},{2,10},{6,14},... | collective-permute-start | bytes 393224 | tf_op jit(solution)/shard_map/ppermute | solution.py:420
  546.5 24.0 %collective-permute-start.28 = (bf16[4,64,256]{2,1,0:T(8,128)(2,1)S(1)}, bf16[4,64,256]{2,1,0:T(8,128)(2,1)S(1)}, u32[]{:S(2)}, u32[]{:S(2)}) collective-permute-start(bf16[4,64,256]{2,1,0:T(8,128)(2,1)S(1)} %get-tuple-element.53), channel_id=1, source_target_pairs={{0,12},{4,0},{8,4},{12,8},{1,13},{5,1},{9,5},{13,9},{2,14},{6,2},{... | collective-permute-start | bytes 393224 | tf_op jit(solution)/shard_map/ppermute | solution.py:420
  547.7 42.5 %collective-permute-start.35 = (bf16[4,64,256]{2,1,0:T(8,128)(2,1)S(1)}, bf16[4,64,256]{2,1,0:T(8,128)(2,1)S(1)}, u32[]{:S(2)}, u32[]{:S(2)}) collective-permute-start(bf16[4,64,256]{2,1,0:T(8,128)(2,1)S(1)} %get-tuple-element.55), channel_id=1, source_target_pairs={{0,4},{4,8},{8,12},{12,0},{1,5},{5,9},{9,13},{13,1},{2,6},{6,10},{... | collective-permute-start | bytes 393224 | tf_op jit(solution)/shard_map/ppermute | solution.py:420
  548.5 44.5 %collective-permute-start.36 = (bf16[4,64,256]{2,1,0:T(8,128)(2,1)S(1)}, bf16[4,64,256]{2,1,0:T(8,128)(2,1)S(1)}, u32[]{:S(2)}, u32[]{:S(2)}) collective-permute-start(bf16[4,64,256]{2,1,0:T(8,128)(2,1)S(1)} %get-tuple-element.56), channel_id=1, source_target_pairs={{0,8},{4,12},{8,0},{12,4},{1,9},{5,13},{9,1},{13,5},{2,10},{6,14},... | collective-permute-start | bytes 393224 | tf_op jit(solution)/shard_map/ppermute | solution.py:420
  568.4 24.6 %collective-permute-start.37 = (bf16[4,64,256]{2,1,0:T(8,128)(2,1)S(1)}, bf16[4,64,256]{2,1,0:T(8,128)(2,1)S(1)}, u32[]{:S(2)}, u32[]{:S(2)}) collective-permute-start(bf16[4,64,256]{2,1,0:T(8,128)(2,1)S(1)} %get-tuple-element.57), channel_id=1, source_target_pairs={{0,12},{4,0},{8,4},{12,8},{1,13},{5,1},{9,5},{13,9},{2,14},{6,2},{... | collective-permute-start | bytes 393224 | tf_op jit(solution)/shard_map/ppermute | solution.py:420
  569.8 24.2 %collective-permute-start.44 = (bf16[4,64,256]{2,1,0:T(8,128)(2,1)S(1)}, bf16[4,64,256]{2,1,0:T(8,128)(2,1)S(1)}, u32[]{:S(2)}, u32[]{:S(2)}) collective-permute-start(bf16[4,64,256]{2,1,0:T(8,128)(2,1)S(1)} %get-tuple-element.59), channel_id=1, source_target_pairs={{0,4},{4,8},{8,12},{12,0},{1,5},{5,9},{9,13},{13,1},{2,6},{6,10},{... | collective-permute-start | bytes 393224 | tf_op jit(solution)/shard_map/ppermute | solution.py:420
  570.5 26.4 %collective-permute-start.45 = (bf16[4,64,256]{2,1,0:T(8,128)(2,1)S(1)}, bf16[4,64,256]{2,1,0:T(8,128)(2,1)S(1)}, u32[]{:S(2)}, u32[]{:S(2)}) collective-permute-start(bf16[4,64,256]{2,1,0:T(8,128)(2,1)S(1)} %get-tuple-element.60), channel_id=1, source_target_pairs={{0,8},{4,12},{8,0},{12,4},{1,9},{5,13},{9,1},{13,5},{2,10},{6,14},... | collective-permute-start | bytes 393224 | tf_op jit(solution)/shard_map/ppermute | solution.py:420
  590.2 25.6 %collective-permute-start.46 = (bf16[4,64,256]{2,1,0:T(8,128)(2,1)S(1)}, bf16[4,64,256]{2,1,0:T(8,128)(2,1)S(1)}, u32[]{:S(2)}, u32[]{:S(2)}) collective-permute-start(bf16[4,64,256]{2,1,0:T(8,128)(2,1)S(1)} %get-tuple-element.61), channel_id=1, source_target_pairs={{0,12},{4,0},{8,4},{12,8},{1,13},{5,1},{9,5},{13,9},{2,14},{6,2},{... | collective-permute-start | bytes 393224 | tf_op jit(solution)/shard_map/ppermute | solution.py:420
  593.1 24.2 %collective-permute-start.62 = (bf16[4,64,256]{2,1,0:T(8,128)(2,1)S(1)}, bf16[4,64,256]{2,1,0:T(8,128)(2,1)S(1)}, u32[]{:S(2)}, u32[]{:S(2)}) collective-permute-start(bf16[4,64,256]{2,1,0:T(8,128)(2,1)S(1)} %get-tuple-element.67), channel_id=1, source_target_pairs={{0,4},{4,8},{8,12},{12,0},{1,5},{5,9},{9,13},{13,1},{2,6},{6,10},{... | collective-permute-start | bytes 393224 | tf_op jit(solution)/shard_map/ppermute | solution.py:420
  593.1 27.1 %collective-permute-start.63 = (bf16[4,64,256]{2,1,0:T(8,128)(2,1)S(1)}, bf16[4,64,256]{2,1,0:T(8,128)(2,1)S(1)}, u32[]{:S(2)}, u32[]{:S(2)}) collective-permute-start(bf16[4,64,256]{2,1,0:T(8,128)(2,1)S(1)} %get-tuple-element.68), channel_id=1, source_target_pairs={{0,8},{4,12},{8,0},{12,4},{1,9},{5,13},{9,1},{13,5},{2,10},{6,14},... | collective-permute-start | bytes 393224 | tf_op jit(solution)/shard_map/ppermute | solution.py:420
  594.1 26.1 %collective-permute-start.64 = (bf16[4,64,256]{2,1,0:T(8,128)(2,1)S(1)}, bf16[4,64,256]{2,1,0:T(8,128)(2,1)S(1)}, u32[]{:S(2)}, u32[]{:S(2)}) collective-permute-start(bf16[4,64,256]{2,1,0:T(8,128)(2,1)S(1)} %get-tuple-element.69), channel_id=1, source_target_pairs={{0,12},{4,0},{8,4},{12,8},{1,13},{5,1},{9,5},{13,9},{2,14},{6,2},{... | collective-permute-start | bytes 393224 | tf_op jit(solution)/shard_map/ppermute | solution.py:420
  597.0 24.3 %collective-permute-start.65 = (bf16[4,64,256]{2,1,0:T(8,128)(2,1)S(1)}, bf16[4,64,256]{2,1,0:T(8,128)(2,1)S(1)}, u32[]{:S(2)}, u32[]{:S(2)}) collective-permute-start(bf16[4,64,256]{2,1,0:T(8,128)(2,1)S(1)} %get-tuple-element.71), channel_id=1, source_target_pairs={{0,4},{4,8},{8,12},{12,0},{1,5},{5,9},{9,13},{13,1},{2,6},{6,10},{... | collective-permute-start | bytes 393224 | tf_op jit(solution)/shard_map/ppermute | solution.py:420
  (50 other events, 1421.4 us)

commit v2 on v1

--- a/solution.py
+++ b/solution.py
@@ -100,7 +100,8 @@
     return context.astype(jnp.bfloat16)
 
 
-def spatial_kernel(heads, sides, rows, where, q_ref, k_ref, v_ref, keep_ref, send_ref, held):
+def spatial_kernel(heads, sides, rows, where, q_ref, k_ref, v_ref, *refs):
+    keep_ref, send_ref, held = refs[-3:]
     core = where[1]
     for head in range(heads):
         lanes = slice(head * HD, (head + 1) * HD)
@@ -112,7 +113,7 @@
         send_ref[0, side] = held[pl.ds(other, rows), :]
 
 
-def spatial(where, spatial_q, spatial_k, spatial_v, clip_at, rows):
+def spatial(where, spatial_q, spatial_k, spatial_v, clip_at, rows, earlier):
     frames, _, patches, width = spatial_q.shape
     sides = patches // (2 * rows)
     block = pl.BlockSpec((1, 1, patches, width), lambda f, w: (f, clip_at, 0, 0))
@@ -124,18 +125,14 @@
         grid_spec=pltpu.PrefetchScalarGridSpec(
             num_scalar_prefetch=1,
             grid=(frames,),
-            in_specs=[block] * 3,
+            in_specs=[block] * 3 + [pl.BlockSpec(memory_space=pl.ANY)] * len(earlier),
             out_specs=[half] * 2,
             scratch_shapes=[pltpu.VMEM((patches, width), jnp.bfloat16)],
         ),
         out_shape=[shape, shape],
         compiler_params=pltpu.CompilerParams(vmem_limit_bytes=32 * MIB),
-        cost_estimate=pl.CostEstimate(
-            flops=4 * frames * heads * patches * patches * HD,
-            bytes_accessed=8 * frames * patches * width,
-            transcendentals=frames * heads * patches * patches,
-        ),
-    )(where, spatial_q, spatial_k, spatial_v)
+        cost_estimate=pl.CostEstimate(flops=0, bytes_accessed=0, transcendentals=0),
+    )(where, spatial_q, spatial_k, spatial_v, *earlier)
 
 
 def branch_tile(keep_ref, came_ref, own_ref, other_ref):
@@ -150,8 +147,8 @@
     )
 
 
-def send_kernel(where, keep_ref, came_ref, own_ref, other_ref, out_ref):
-    out_ref[...] = branch_tile(keep_ref, came_ref, own_ref, other_ref).astype(jnp.bfloat16)
+def send_kernel(where, keep_ref, came_ref, own_ref, other_ref, *refs):
+    refs[-1][...] = branch_tile(keep_ref, came_ref, own_ref, other_ref).astype(jnp.bfloat16)
 
 
 def branch_cost(frames, rows, width, model):
@@ -162,7 +159,7 @@
     )
 
 
-def branch_for_other(where, keep, came, own_weight, other_weight, tile):
+def branch_for_other(where, keep, came, own_weight, other_weight, tile, earlier):
     frames, _, rows, width = keep.shape
     model = own_weight.shape[1]
     context = pl.BlockSpec((frames, 1, rows, width), lambda n, w: (0, 1 - w[0], 0, 0))
@@ -172,13 +169,14 @@
         grid_spec=pltpu.PrefetchScalarGridSpec(
             num_scalar_prefetch=1,
             grid=(model // tile,),
-            in_specs=[context, context, weight, weight],
+            in_specs=[context, context, weight, weight]
+            + [pl.BlockSpec(memory_space=pl.ANY)] * len(earlier),
             out_specs=pl.BlockSpec((frames * rows, tile), lambda n, w: (0, n)),
         ),
         out_shape=jax.ShapeDtypeStruct((frames * rows, model), jnp.bfloat16),
         compiler_params=pltpu.CompilerParams(vmem_limit_bytes=32 * MIB),
-        cost_estimate=branch_cost(frames, rows, width, model),
-    )(where, keep, came, own_weight, other_weight)
+        cost_estimate=pl.CostEstimate(flops=0, bytes_accessed=0, transcendentals=0),
+    )(where, keep, came, own_weight, other_weight, *earlier)
 
 
 def norm_kernel(
@@ -218,7 +216,7 @@
                     ).astype(jnp.bfloat16)
 
 
-def norm(where, keep, came, own_weight, other_weight, branch, resid, gain, earlier, clip_at, tile, ways):
+def norm(where, keep, came, own_weight, other_weight, branch, resid, gain, written, clip_at, tile, ways, earlier):
     frames, _, rows, width = keep.shape
     model = own_weight.shape[1]
     tiles = model // tile
@@ -236,42 +234,47 @@
                 pl.BlockSpec((frames * rows, tile), lambda n, w: (0, n)),
                 residual,
                 pl.BlockSpec((1, model), lambda n, w: (0, 0)),
-            ] + [pl.BlockSpec(memory_space=pl.ANY)] * len(earlier),
+            ] + [pl.BlockSpec(memory_space=pl.ANY)] * (len(written) + len(earlier)),
             out_specs=[residual] + [pl.BlockSpec(piece, lambda n, w: (0, 0))] * ways,
             scratch_shapes=[pltpu.VMEM((tiles, frames * rows, tile), jnp.float32)],
         ),
         out_shape=[jax.ShapeDtypeStruct(resid.shape, jnp.bfloat16)]
         + [jax.ShapeDtypeStruct(piece, jnp.bfloat16)] * ways,
-        input_output_aliases={8: 0} if earlier else {},
+        input_output_aliases={8: 0} if written else {},
         compiler_params=pltpu.CompilerParams(vmem_limit_bytes=40 * MIB),
-        cost_estimate=branch_cost(frames, rows, width, model),
-    )(where, keep, came, own_weight, other_weight, branch, resid, gain, *earlier)
-
-
-def project_kernel(steps, ways, share, piece_rows, where, *refs):
+        cost_estimate=pl.CostEstimate(flops=0, bytes_accessed=0, transcendentals=0),
+    )(where, keep, came, own_weight, other_weight, branch, resid, gain, *written, *earlier)
+
+
+def project_kernel(steps, ways, share, piece_rows, part_at, where, *refs):
     pieces = refs[:steps * 2 * ways]
     at = steps * 2 * ways
     own_ref, near, far = refs[at], refs[at + 1:at + ways], refs[at + ways:at + 2 * ways - 1]
-    outs = refs[at + 2 * ways - 1:at + 3 * ways - 1]
-    rows_buf, weight_buf, qkv_buf, rows_sem, weight_sem = refs[at + 3 * ways - 1:]
+    outs = refs[-5 - ways:-5]
+    rows_buf, weight_buf, qkv_buf, rows_sem, weight_sem = refs[-5:]
     plane, home = where[3], where[2]
     half = near[0].shape[0]
     group = ways * piece_rows
     heads = qkv_buf.shape[2] // HD
 
+    width = heads * HD
     copies = [pltpu.make_async_copy(
-        own_ref, weight_buf.at[pl.ds(pl.multiple_of(home * 2 * half, half), 2 * half)],
-        weight_sem.at[0])]
+        own_ref.at[part, :, part_at * width:(part_at + 1) * width],
+        weight_buf.at[
+            pl.ds(pl.multiple_of(home * 2 * half, half), 2 * half),
+            part * width:(part + 1) * width,
+        ],
+        weight_sem.at[2 * ways - 2 + part]) for part in range(3)]
     for way in range(1, ways):
         base = lax.rem(home + ways - way, ways) * 2 * half
         copies.append(pltpu.make_async_copy(
             near[way - 1],
             weight_buf.at[pl.ds(pl.multiple_of(base + plane * half, half), half)],
-            weight_sem.at[2 * way - 1]))
+            weight_sem.at[2 * way - 2]))
         copies.append(pltpu.make_async_copy(
             far[way - 1],
             weight_buf.at[pl.ds(pl.multiple_of(base + (1 - plane) * half, half), half)],
-            weight_sem.at[2 * way]))
+            weight_sem.at[2 * way - 1]))
 
     def row_copies(step):
         slot = step % 2
@@ -326,27 +329,27 @@
     lax.fori_loop(0, steps, body, 0)
 
 
-def project(where, pieces, own, near, far, ways, share):
+def project(where, pieces, weight, near, far, group, ways, share, earlier):
     groups = len(pieces)
     steps = groups // 2
     piece_rows, model = pieces[0][0].shape
-    width = own.shape[1] // 3
+    width = near[0].shape[1] // 3
     flat = [piece for group in pieces for piece in group]
     rows = piece_rows * ways * groups
     out = (groups, piece_rows, width)
     return pl.pallas_call(
-        functools.partial(project_kernel, steps, ways, share, piece_rows),
+        functools.partial(project_kernel, steps, ways, share, piece_rows, group),
         grid_spec=pltpu.PrefetchScalarGridSpec(
             num_scalar_prefetch=1,
             grid=(1,),
-            in_specs=[pl.BlockSpec(memory_space=pl.ANY)] * (len(flat) + 2 * ways - 1),
+            in_specs=[pl.BlockSpec(memory_space=pl.ANY)] * (len(flat) + 2 * ways - 1 + len(earlier)),
             out_specs=[pl.BlockSpec(out, lambda n, w: (0, 0, 0))] * ways,
             scratch_shapes=[
                 pltpu.VMEM((2, 2 * ways * piece_rows, model), jnp.bfloat16),
                 pltpu.VMEM((model, 3 * width), jnp.bfloat16),
                 pltpu.VMEM((3, 2 * ways * piece_rows, width), jnp.bfloat16),
                 pltpu.SemaphoreType.DMA((2, 2 * ways)),
-                pltpu.SemaphoreType.DMA((2 * ways - 1,)),
+                pltpu.SemaphoreType.DMA((2 * ways + 1,)),
             ],
         ),
         out_shape=[jax.ShapeDtypeStruct(out, jnp.bfloat16)] * ways,
@@ -356,7 +359,7 @@
             bytes_accessed=2 * rows * model + 6 * model * width,
             transcendentals=rows * ways * piece_rows,
         ),
-    )(where, *flat, own, *near, *far)
+    )(where, *flat, weight, *near, *far, *earlier)
 
 
 def assemble_kernel(clips, sources, ways, groups, share, where, *refs):
@@ -396,11 +399,53 @@
     )(where, *flat)
 
 
+def passing_kernel(*refs):
+    del refs
+
+
+def after(arrays, *earlier):
+    count = len(arrays)
+    return list(pl.pallas_call(
+        passing_kernel,
+        in_specs=[pl.BlockSpec(memory_space=pl.ANY)] * (count + len(earlier)),
+        out_specs=[pl.BlockSpec(memory_space=pl.ANY)] * count,
+        out_shape=[jax.ShapeDtypeStruct(array.shape, array.dtype) for array in arrays],
+        input_output_aliases={n: n for n in range(count)},
+        cost_estimate=pl.CostEstimate(flops=0, bytes_accessed=0, transcendentals=0),
+    )(*arrays, *earlier))
+
+
+def columns_kernel(where, weight_ref, *refs):
+    half_ref = refs[-1]
+    width = weight_ref.shape[2]
+    for part in range(3):
+        half_ref[:, part * width:(part + 1) * width] = weight_ref[part]
+
+
+def columns_of(where, weight, group, groups, earlier):
+    _, block, width = weight.shape
+    width = width // groups
+    steps = 2
+    rows = block // (2 * steps)
+    return pl.pallas_call(
+        columns_kernel,
+        grid_spec=pltpu.PrefetchScalarGridSpec(
+            num_scalar_prefetch=1,
+            grid=(steps,),
+            in_specs=[pl.BlockSpec((3, rows, width), lambda n, w: (0, n + steps * w[3], group))]
+            + [pl.BlockSpec(memory_space=pl.ANY)] * len(earlier),
+            out_specs=pl.BlockSpec((rows, 3 * width), lambda n, w: (n, 0)),
+        ),
+        out_shape=jax.ShapeDtypeStruct((block // 2, 3 * width), jnp.bfloat16),
+        compiler_params=pltpu.CompilerParams(vmem_limit_bytes=32 * MIB),
+        cost_estimate=pl.CostEstimate(flops=0, bytes_accessed=0, transcendentals=0),
+    )(where, weight, *earlier)
+
+
 def per_device(ways, resid, spatial_q, spatial_k, spatial_v, out_weight, norm_gain, qkv_weight):
     frames, clips, rows, model = resid.shape
     patches, width = spatial_q.shape[2:]
     share = rows // ways
-    block = qkv_weight.shape[0]
     groups = 3
     tile = 1024
 
@@ -419,57 +464,83 @@
     def along(array, way):
         return lax.ppermute(array, "tm", [(n, (n + way) % ways) for n in range(ways)])
 
-    per_group = width // groups
-    own, near, far = [], [], []
-    for group in range(groups):
-        columns = qkv_weight[:, :, group * per_group:(group + 1) * per_group].reshape(
-            block, 3 * per_group
+    def norm_of(clip, written, *earlier):
+        return norm(
+            where, *attended[clip], out_weight, other_weight, branches[clip], resid, gain,
+            written, clip, tile, ways, earlier,
         )
-        own.append(columns)
-        travelling = lax.dynamic_slice_in_dim(columns, plane * (block // 2), block // 2, 0)
-        near.append([])
-        far.append([])
-        for _ in range(1, ways):
-            travelling = along(travelling, 1)
-            near[-1].append(travelling)
-            far[-1].append(other_plane(travelling))
+
+    weight = qkv_weight.transpose(1, 0, 2)
+    gain = norm_gain.reshape(1, model)
+    near = [[] for _ in range(groups)]
+    far = [[] for _ in range(groups)]
+
+    def pass_on(group, *earlier):
+        (came,) = after([near[group][-1]], *earlier)
+        near[group][-1] = came
+        far[group].append(other_plane(came))
+        if len(near[group]) < ways - 1:
+            near[group].append(along(came, 1))
+        return came
 
     other_weight = other_core(out_weight)
-    gain = norm_gain.reshape(1, model)
-
-    written = []
-    attended = []
-    for clip in range(clips):
-        keep, send = spatial(where, spatial_q, spatial_k, spatial_v, clip, rows)
-        attended.append((keep, other_core(send)))
-    branches = []
-    for clip in range(clips):
-        branches.append(other_side(
-            branch_for_other(where, *attended[clip], out_weight, other_weight, tile)
-        ))
-    gathered = []
-    for clip in range(clips):
-        resid_out, *normed = norm(
-            where, *attended[clip], out_weight, other_weight, branches[clip], resid, gain,
-            written, clip, tile, ways,
+    start = [columns_of(where, weight, 0, groups, [])]
+    near[0].append(along(start[0], 1))
+    keep, send = spatial(where, spatial_q, spatial_k, spatial_v, 0, rows, [start[0]])
+    attended = [(keep, other_core(send))]
+    start.append(columns_of(where, weight, 1, groups, [send]))
+    near[1].append(along(start[1], 1))
+    first = branch_for_other(where, *attended[0], out_weight, other_weight, tile, [start[1]])
+    branches = [other_side(first)]
+    latest = pass_on(0, first)
+    keep, send = spatial(where, spatial_q, spatial_k, spatial_v, 1, rows, [latest])
+    attended.append((keep, other_core(send)))
+    start.append(columns_of(where, weight, 2, groups, [send]))
+    latest = pass_on(1, start[2])
+    second = branch_for_other(where, *attended[1], out_weight, other_weight, tile, [latest])
+    latest = pass_on(0, second)
+    latest = pass_on(1, latest, far[0][0])
+    (second,) = after([second], branches[0], latest)
+    branches.append(other_side(second))
+    resid_out, *normed = norm_of(0, [], second)
+    mine = [[normed[0]] + [along(normed[way], way) for way in range(1, ways)]]
+    latest = pass_on(0, normed[0], far[1][0])
+    latest = pass_on(1, latest, far[0][1])
+    resid_out, *normed = norm_of(1, [resid_out], latest)
+    mine.append([normed[0]] + [along(normed[way], way) for way in range(1, ways)])
+    mine[0][1:] = after(mine[0][1:], normed[0], far[1][1])
+    beside = [[other_side(piece) for piece in mine[0]]]
+    beside[0] = after(beside[0], mine[0][1], far[0][2])
+    across = [[other_core(piece) for piece in mine[0] + beside[0]]]
+
+    def project_of(clip, group, *earlier):
+        pieces = [mine[clip], beside[clip], across[clip][:ways], across[clip][ways:]]
+        return project(
+            where, pieces, weight, near[group], far[group], group, ways, share, earlier
         )
-        written = [resid_out]
-        mine = [normed[0]] + [along(normed[way], way) for way in range(1, ways)]
-        beside = [other_side(piece) for piece in mine]
-        gathered.append([
-            mine, beside, [other_core(piece) for piece in mine],
-            [other_core(piece) for piece in beside],
-        ])
 
     arrived = [[None] * groups for _ in range(clips)]
-    for group in range(groups):
-        for clip in range(clips):
-            contexts = project(
-                where, gathered[clip], own[group], near[group], far[group], ways, share
-            )
-            arrived[clip][group] = [contexts[0]] + [
-                along(contexts[way], ways - way) for way in range(1, ways)
-            ]
+
+    def give_back(clip, group, contexts):
+        arrived[clip][group] = [contexts[0]] + [
+            along(contexts[way], ways - way) for way in range(1, ways)
+        ]
+        return contexts[0]
+
+    *mine[1][1:], travelling = after(mine[1][1:] + [start[2]], beside[0][0], far[1][2])
+    beside.append([other_side(piece) for piece in mine[1]])
+    near[2].append(along(travelling, 1))
+    latest = give_back(0, 0, project_of(0, 0, travelling))
+    latest = pass_on(2, latest)
+    latest = give_back(0, 1, project_of(0, 1, latest))
+    latest = pass_on(2, latest)
+    beside[1] = after(beside[1], latest)
+    across.append([other_core(piece) for piece in mine[1] + beside[1]])
+    latest = pass_on(2, beside[1][0], far[2][0])
+    latest = give_back(1, 0, project_of(1, 0, latest))
+    latest = give_back(1, 1, project_of(1, 1, latest))
+    latest = give_back(0, 2, project_of(0, 2, latest))
+    latest = give_back(1, 2, project_of(1, 2, latest))
     ordered = [
         [[got[0]] + [got[ways - way] for way in range(1, ways)] for got in by_group]
         for by_group in arrived

time: 639 us -> 601 us (0.941)
  waiting for transfers between devices: 317 us -> 272 us
  local copies, waits for them, and re-layouts: 63.2 us -> 39.9 us
  starting transfers between devices: 81.8 us -> 104 us
  Pallas kernels: 175 us -> 183 us
    ppermute x33, waiting for transfers between devices: 191 us -> 149 us  [along(): lax.ppermute(array, 'tm', [(n, (n + way) % ways) for n in range(ways)])]
    ppermute x33, starting transfers between devices: 53.5 us -> 79.3 us  [along(): lax.ppermute(array, 'tm', [(n, (n + way) % ways) for n in range(ways)])]
    ppermute x10, waiting for transfers between devices: 72.1 us -> 46.7 us  [other_side(): return lax.ppermute(array, 'tensor', [(0, 2), (2, 0), (1, 3), (3, 1)])]
    ppermute x9, waiting for transfers between devices: 54.1 us -> 70 us  [other_plane(): return lax.ppermute(array, 'clip', [(0, 1), (1, 0)])]
    reshape x3 -> x0, local copies, waits for them, and re-layouts: 13.2 us -> none  [per_device(): qkv_weight[:, :, group * per_group:(group + 1) * per_group]]
    unnamed x89 -> x122, local copies, waits for them, and re-layouts: 38.1 us -> 39.9 us
  transfers between devices with their start and end apart: 71 -> 71, of which waited for: 23 -> 27; matrix products, arithmetic and copies ran while one was open for 6% -> 0% of each run, Pallas kernels for 27% -> 28%
where the time goes in v2:
time: 601 us; the launch traced here: 600 us
  waiting for transfers between devices  272 us (45%)
  Pallas kernels  183 us (30%)
  starting transfers between devices  104 us (17%)
  local copies, waits for them, and re-layouts  39.9 us (7%)
    ppermute x33, waiting for transfers between devices, along(): lax.ppermute(array, 'tm', [(n, (n + way) % ways) for n in range(ways)])  149 us
    pallas_call x6, Pallas kernels, project(): pl.pallas_call(functools.partial(project_kernel, steps, ways, share, piec...  114 us
    ppermute x33, starting transfers between devices, along(): lax.ppermute(array, 'tm', [(n, (n + way) % ways) for n in range(ways)])  79.3 us
    ppermute x9, waiting for transfers between devices, other_plane(): return lax.ppermute(array, 'clip', [(0, 1), (1, 0)])  70 us
    ppermute x10, waiting for transfers between devices, other_side(): return lax.ppermute(array, 'tensor', [(0, 2), (2, 0), (1, 3), (3, 1)])  46.7 us
    unnamed x122, local copies, waits for them, and re-layouts  39.9 us
    pallas_call x2, Pallas kernels, norm(): pl.pallas_call(functools.partial(norm_kernel, tiles, tile, ways), grid_sp...  30.8 us
    pallas_call x2, Pallas kernels, branch_for_other(): pl.pallas_call(send_kernel, grid_spec=pltpu.PrefetchScalarGridSpec(num_sc...  19.7 us
  transfers between devices with their start and end apart: 71, of which 27 were waited for; matrix products, arithmetic and copies ran while one was open for 0% of the time, Pallas kernels for 28%

profile of v2, /device:TPU:0, one launch (start us, length us, event | category | flops | bytes accessed | tf_op | source)
XLA Modules:
  0.0 600.3 jit_solution(16486130274673666192)
XLA Ops:
  1.2 3.0 copy-done.1
  5.0 2.2 copy-done.5
  7.2 1.9 copy-done.7
  9.1 1.9 copy-done.9
  11.0 6.1 %shard_map.87 = (bf16[4,2,64,768]{3,2,1,0:T(8,128)(2,1)S(1)}, bf16[4,2,64,768]{3,2,1,0:T(8,128)(2,1)S(1)}) custom-call(s32[4]{0:T(128)S(1)} %pad_add_fusion.where, bf16[4,2,256,768]{3,2,1,0:T(8,128)(2,1)S(1)} %copy-done.5, bf16[4,2,256,768]{3,2,1,0:T(8,128)(2,1)S(1)} %copy-done.7, bf16[4,2,256,768]{3,2,1,0:T(8,128)(2,1)S(1)} %copy-done.9, ...), custom_call_target="tpu_custom_call" | custom-call | tf_op jit(solution)/shard_map/pallas_call | solution.py:123
  17.3 1.7 shard_map.88.refs_0_
  19.6 10.3 %shard_map.89.refs_1_ = bf16[256,6144]{1,0:T(8,128)(2,1)} custom-call(s32[4]{0:T(128)S(1)} %pad_add_fusion.where, bf16[4,2,64,768]{3,2,1,0:T(8,128)(2,1)S(1)} %get-tuple-element.55.keep_ref, bf16[4,2,64,768]{3,2,1,0:T(8,128)(2,1)S(1)} %collective-permute-done.1.came_ref, bf16[768,6144]{1,0:T(8,128)(2,1)S(1)} %bitcast.7, ...), custom_call_target="tpu_custom_call" | custom-call | tf_op jit(solution)/shard_map/pallas_call | solution.py:167
  29.9 2.7 collective-permute-start.5
  32.5 1.6 collective-permute-start
  34.1 1.6 collective-permute-start.4
  35.7 27.6 %collective-permute-done.refs_0_ = bf16[768,768]{1,0:T(8,128)(2,1)} collective-permute-done((bf16[768,768]{1,0:T(8,128)(2,1)S(1)}, bf16[768,768]{1,0:T(8,128)(2,1)}, u32[]{:S(2)}, u32[]{:S(2)}) %collective-permute-start) | collective-permute-done | bytes 1179680 | tf_op jit(solution)/shard_map/ppermute | solution.py:465
  63.2 2.0 copy-done.6
  65.3 1.9 copy-done.8
  67.2 1.9 copy-done.10
  69.1 6.1 %shard_map.91 = (bf16[4,2,64,768]{3,2,1,0:T(8,128)(2,1)S(1)}, bf16[4,2,64,768]{3,2,1,0:T(8,128)(2,1)S(1)}) custom-call(s32[4]{0:T(128)S(1)} %pad_add_fusion.where, bf16[4,2,256,768]{3,2,1,0:T(8,128)(2,1)S(1)} %copy-done.6, bf16[4,2,256,768]{3,2,1,0:T(8,128)(2,1)S(1)} %copy-done.8, bf16[4,2,256,768]{3,2,1,0:T(8,128)(2,1)S(1)} %copy-done.10, ...), custom_call_target="tpu_custom_call" | custom-call | tf_op jit(solution)/shard_map/pallas_call | solution.py:123
  77.4 11.1 %collective-permute-done.4.refs_0_ = bf16[768,768]{1,0:T(8,128)(2,1)} collective-permute-done((bf16[768,768]{1,0:T(8,128)(2,1)}, bf16[768,768]{1,0:T(8,128)(2,1)}, u32[]{:S(2)}, u32[]{:S(2)}) %collective-permute-start.4) | collective-permute-done | bytes 1179680 | tf_op jit(solution)/shard_map/ppermute | solution.py:465
  88.5 1.6 collective-permute-start.8
  90.1 2.3 collective-permute-done.3.came_ref
  92.4 3.7 copy-done
  96.1 9.4 %shard_map.94.refs_1_.refs_0_ = bf16[256,6144]{1,0:T(8,128)(2,1)S(1)} custom-call(s32[4]{0:T(128)S(1)} %pad_add_fusion.where, bf16[4,2,64,768]{3,2,1,0:T(8,128)(2,1)S(1)} %copy-done.15, bf16[4,2,64,768]{3,2,1,0:T(8,128)(2,1)S(1)} %collective-permute-done.3.came_ref, bf16[768,6144]{1,0:T(8,128)(2,1)S(1)} %copy-done, ...), custom_call_target="tpu_custom_call" | custom-call | tf_op jit(solution)/shard_map/pallas_call | solution.py:167
  105.5 1.6 copy-done.3
  107.1 6.7 %collective-permute-done.7.refs_0_ = bf16[768,768]{1,0:T(8,128)(2,1)} collective-permute-done((bf16[768,768]{1,0:T(8,128)(2,1)}, bf16[768,768]{1,0:T(8,128)(2,1)}, u32[]{:S(2)}, u32[]{:S(2)}) %collective-permute-start.7) | collective-permute-done | bytes 1179680 | tf_op jit(solution)/shard_map/ppermute | solution.py:465
  113.8 24.4 %collective-permute-done.6.refs_0_ = bf16[768,768]{1,0:T(8,128)(2,1)S(1)} collective-permute-done((bf16[768,768]{1,0:T(8,128)(2,1)}, bf16[768,768]{1,0:T(8,128)(2,1)S(1)}, u32[]{:S(2)}, u32[]{:S(2)}) %collective-permute-start.6) | collective-permute-done | bytes 1179680 | tf_op jit(solution)/shard_map/ppermute | solution.py:465
  143.1 25.8 %collective-permute-done.12.refs_2_.refs_20_ = bf16[768,768]{1,0:T(8,128)(2,1)S(1)} collective-permute-done((bf16[768,768]{1,0:T(8,128)(2,1)}, bf16[768,768]{1,0:T(8,128)(2,1)S(1)}, u32[]{:S(2)}, u32[]{:S(2)}) %collective-permute-start.12) | collective-permute-done | bytes 1179680 | tf_op jit(solution)/shard_map/ppermute | solution.py:462
  170.4 1.9 copy-done.4
  174.1 15.8 %shard_map.98 = (bf16[4,2,64,6144]{3,2,1,0:T(8,128)(2,1)}, bf16[64,6144]{1,0:T(8,128)(2,1)}, bf16[64,6144]{1,0:T(8,128)(2,1)S(1)}, bf16[64,6144]{1,0:T(8,128)(2,1)}, bf16[64,6144]{1,0:T(8,128)(2,1)}) custom-call(s32[4]{0:T(128)S(1)} %pad_add_fusion.where, bf16[4,2,64,768]{3,2,1,0:T(8,128)(2,1)S(1)} %copy-done.17, bf16[4,2,64,768]{3,2,1,0:T(8,128)(2,1)S(1)} %copy-done.19, ...), custom_call_target="tpu_custom_call" | custom-call | tf_op jit(solution)/shard_map/pallas_call | solution.py:227
  190.0 7.6 %collective-permute-done.10.refs_0_ = bf16[768,768]{1,0:T(8,128)(2,1)S(1)} collective-permute-done((bf16[768,768]{1,0:T(8,128)(2,1)}, bf16[768,768]{1,0:T(8,128)(2,1)S(1)}, u32[]{:S(2)}, u32[]{:S(2)}) %collective-permute-start.10) | collective-permute-done | bytes 1179680 | tf_op jit(solution)/shard_map/ppermute | solution.py:465
  198.0 19.7 %collective-permute-done.17.refs_4_.refs_21_ = bf16[768,768]{1,0:T(8,128)(2,1)S(1)} collective-permute-done((bf16[768,768]{1,0:T(8,128)(2,1)}, bf16[768,768]{1,0:T(8,128)(2,1)S(1)}, u32[]{:S(2)}, u32[]{:S(2)}) %collective-permute-start.17) | collective-permute-done | bytes 1179680 | tf_op jit(solution)/shard_map/ppermute | solution.py:462
  219.0 26.9 %collective-permute-done.15.refs_1_ = bf16[64,6144]{1,0:T(8,128)(2,1)} collective-permute-done((bf16[64,6144]{1,0:T(8,128)(2,1)}, bf16[64,6144]{1,0:T(8,128)(2,1)}, u32[]{:S(2)}, u32[]{:S(2)}) %collective-permute-start.15) | collective-permute-done | bytes 786464 | tf_op jit(solution)/shard_map/ppermute | solution.py:465
  249.3 15.0 %shard_map.101 = (bf16[4,2,64,6144]{3,2,1,0:T(8,128)(2,1)}, bf16[64,6144]{1,0:T(8,128)(2,1)S(1)}, bf16[64,6144]{1,0:T(8,128)(2,1)S(1)}, bf16[64,6144]{1,0:T(8,128)(2,1)S(1)}, bf16[64,6144]{1,0:T(8,128)(2,1)S(1)}) custom-call(s32[4]{0:T(128)S(1)} %pad_add_fusion.where, bf16[4,2,64,768]{3,2,1,0:T(8,128)(2,1)S(1)} %copy-done.15, ...), custom_call_target="tpu_custom_call", output_to_operand_aliasing={{0}: (8, {})} | custom-call | tf_op jit(solution)/shard_map/pallas_call | solution.py:227
  271.5 3.6 collective-permute-done.22.refs_5_.refs_22_
  275.1 13.7 %collective-permute-start.31 = (bf16[64,6144]{1,0:T(8,128)(2,1)}, bf16[64,6144]{1,0:T(8,128)(2,1)S(1)}, u32[]{:S(2)}, u32[]{:S(2)}) collective-permute-start(bf16[64,6144]{1,0:T(8,128)(2,1)} %copy-done.43), channel_id=1, source_target_pairs={{0,4},{4,8},{8,12},{12,0},{1,5},{5,9},{9,13},{13,1},{2,6},{6,10},{... | collective-permute-start | bytes 2359304 | tf_op jit(solution)/shard_map/ppermute | solution.py:465
  288.8 10.5 %collective-permute-done.34.refs_5_.refs_22_ = bf16[768,768]{1,0:T(8,128)(2,1)} collective-permute-done((bf16[768,768]{1,0:T(8,128)(2,1)}, bf16[768,768]{1,0:T(8,128)(2,1)}, u32[]{:S(2)}, u32[]{:S(2)}) %collective-permute-start.34) | collective-permute-done | bytes 1179680 | tf_op jit(solution)/shard_map/ppermute | solution.py:462
  299.3 1.8 collective-permute-start.32
  301.2 12.6 %collective-permute-start.33 = (bf16[64,6144]{1,0:T(8,128)(2,1)}, bf16[64,6144]{1,0:T(8,128)(2,1)}, u32[]{:S(2)}, u32[]{:S(2)}) collective-permute-start(bf16[64,6144]{1,0:T(8,128)(2,1)} %copy-done.41), channel_id=1, source_target_pairs={{0,12},{4,0},{8,4},{12,8},{1,13},{5,1},{9,5},{13,9},{2,14},{6,2},{... | collective-permute-start | bytes 2359304 | tf_op jit(solution)/shard_map/ppermute | solution.py:465
  313.7 6.9 %collective-permute-done.21.refs_3_ = bf16[64,6144]{1,0:T(8,128)(2,1)S(1)} collective-permute-done((bf16[64,6144]{1,0:T(8,128)(2,1)}, bf16[64,6144]{1,0:T(8,128)(2,1)S(1)}, u32[]{:S(2)}, u32[]{:S(2)}) %collective-permute-start.21) | collective-permute-done | bytes 786464 | tf_op jit(solution)/shard_map/ppermute | solution.py:459
  322.4 15.5 %collective-permute-done.32.refs_1_ = bf16[64,6144]{1,0:T(8,128)(2,1)} collective-permute-done((bf16[64,6144]{1,0:T(8,128)(2,1)}, bf16[64,6144]{1,0:T(8,128)(2,1)}, u32[]{:S(2)}, u32[]{:S(2)}) %collective-permute-start.32) | collective-permute-done | bytes 786464 | tf_op jit(solution)/shard_map/ppermute | solution.py:465
  339.1 16.0 %collective-permute-start.38 = (bf16[768,768]{1,0:T(8,128)(2,1)}, bf16[768,768]{1,0:T(8,128)(2,1)}, u32[]{:S(2)}, u32[]{:S(2)}) collective-permute-start(bf16[768,768]{1,0:T(8,128)(2,1)} %get-tuple-element.76.refs_23_), channel_id=1, source_target_pairs={{0,4},{4,8},{8,12},{12,0},{1,5},{5,9},{9,13},{13,1},{2,6},{6,10},{... | collective-permute-start | bytes 3538952 | tf_op jit(solution)/shard_map/ppermute | solution.py:465
  356.0 19.0 %shard_map.105 = (bf16[4,64,256]{2,1,0:T(8,128)(2,1)S(1)}, bf16[4,64,256]{2,1,0:T(8,128)(2,1)S(1)}, bf16[4,64,256]{2,1,0:T(8,128)(2,1)S(1)}, bf16[4,64,256]{2,1,0:T(8,128)(2,1)S(1)}) custom-call(s32[4]{0:T(128)S(1)} %pad_add_fusion.where, bf16[64,6144]{1,0:T(8,128)(2,1)} %get-tuple-element.60.refs_1_.refs_0_, ...), custom_call_target="tpu_custom_call" | custom-call | flops 9663676416 | bytes 22020096 | tf_op jit(solution)/shard_map/pallas_call | solution.py:340
  377.6 6.2 %collective-permute-done.38.refs_0_ = bf16[768,768]{1,0:T(8,128)(2,1)} collective-permute-done((bf16[768,768]{1,0:T(8,128)(2,1)}, bf16[768,768]{1,0:T(8,128)(2,1)}, u32[]{:S(2)}, u32[]{:S(2)}) %collective-permute-start.38) | collective-permute-done | bytes 1179680 | tf_op jit(solution)/shard_map/ppermute | solution.py:465
  383.7 1.5 collective-permute-start.44
  387.8 19.0 %shard_map.107 = (bf16[4,64,256]{2,1,0:T(8,128)(2,1)S(1)}, bf16[4,64,256]{2,1,0:T(8,128)(2,1)S(1)}, bf16[4,64,256]{2,1,0:T(8,128)(2,1)S(1)}, bf16[4,64,256]{2,1,0:T(8,128)(2,1)S(1)}) custom-call(s32[4]{0:T(128)S(1)} %pad_add_fusion.where, bf16[64,6144]{1,0:T(8,128)(2,1)} %get-tuple-element.60.refs_1_.refs_0_, ...), custom_call_target="tpu_custom_call" | custom-call | flops 9663676416 | bytes 22020096 | tf_op jit(solution)/shard_map/pallas_call | solution.py:340
  407.5 5.8 collective-permute-done.42.refs_0_
  413.8 7.5 %collective-permute-done.45.refs_1_ = bf16[64,6144]{1,0:T(8,128)(2,1)} collective-permute-done((bf16[64,6144]{1,0:T(8,128)(2,1)}, bf16[64,6144]{1,0:T(8,128)(2,1)}, u32[]{:S(2)}, u32[]{:S(2)}) %collective-permute-start.45) | collective-permute-done | bytes 786464 | tf_op jit(solution)/shard_map/ppermute | solution.py:459
  421.4 16.8 %collective-permute-done.46.refs_2_ = bf16[64,6144]{1,0:T(8,128)(2,1)} collective-permute-done((bf16[64,6144]{1,0:T(8,128)(2,1)}, bf16[64,6144]{1,0:T(8,128)(2,1)}, u32[]{:S(2)}, u32[]{:S(2)}) %collective-permute-start.46) | collective-permute-done | bytes 786464 | tf_op jit(solution)/shard_map/ppermute | solution.py:459
  438.2 15.4 %collective-permute-done.47.refs_3_ = bf16[64,6144]{1,0:T(8,128)(2,1)} collective-permute-done((bf16[64,6144]{1,0:T(8,128)(2,1)}, bf16[64,6144]{1,0:T(8,128)(2,1)}, u32[]{:S(2)}, u32[]{:S(2)}) %collective-permute-start.47) | collective-permute-done | bytes 786464 | tf_op jit(solution)/shard_map/ppermute | solution.py:459
  454.2 2.0 collective-permute-done.53.refs_10_
  458.5 3.0 collective-permute-start.36
  461.5 1.7 collective-permute-start.37
  467.5 19.0 %shard_map.111 = (bf16[4,64,256]{2,1,0:T(8,128)(2,1)S(1)}, bf16[4,64,256]{2,1,0:T(8,128)(2,1)S(1)}, bf16[4,64,256]{2,1,0:T(8,128)(2,1)S(1)}, bf16[4,64,256]{2,1,0:T(8,128)(2,1)S(1)}) custom-call(s32[4]{0:T(128)S(1)} %pad_add_fusion.where, bf16[64,6144]{1,0:T(8,128)(2,1)S(1)} %copy-done.31, bf16[64,6144]{1,0:T(8,128)(2,1)S(1)} %copy-done.33, ...), custom_call_target="tpu_custom_call" | custom-call | flops 9663676416 | bytes 22020096 | tf_op jit(solution)/shard_map/pallas_call | solution.py:340
  486.5 19.1 %shard_map.112 = (bf16[4,64,256]{2,1,0:T(8,128)(2,1)S(1)}, bf16[4,64,256]{2,1,0:T(8,128)(2,1)S(1)}, bf16[4,64,256]{2,1,0:T(8,128)(2,1)S(1)}, bf16[4,64,256]{2,1,0:T(8,128)(2,1)S(1)}) custom-call(s32[4]{0:T(128)S(1)} %pad_add_fusion.where, bf16[64,6144]{1,0:T(8,128)(2,1)S(1)} %copy-done.31, bf16[64,6144]{1,0:T(8,128)(2,1)S(1)} %copy-done.33, ...), custom_call_target="tpu_custom_call" | custom-call | flops 9663676416 | bytes 22020096 | tf_op jit(solution)/shard_map/pallas_call | solution.py:340
  506.0 10.4 %collective-permute-done.50.refs_22_ = bf16[768,768]{1,0:T(8,128)(2,1)S(1)} collective-permute-done((bf16[768,768]{1,0:T(8,128)(2,1)}, bf16[768,768]{1,0:T(8,128)(2,1)S(1)}, u32[]{:S(2)}, u32[]{:S(2)}) %collective-permute-start.50) | collective-permute-done | bytes 1179680 | tf_op jit(solution)/shard_map/ppermute | solution.py:462
  517.4 19.0 %shard_map.113 = (bf16[4,64,256]{2,1,0:T(8,128)(2,1)S(1)}, bf16[4,64,256]{2,1,0:T(8,128)(2,1)S(1)}, bf16[4,64,256]{2,1,0:T(8,128)(2,1)S(1)}, bf16[4,64,256]{2,1,0:T(8,128)(2,1)S(1)}) custom-call(s32[4]{0:T(128)S(1)} %pad_add_fusion.where, bf16[64,6144]{1,0:T(8,128)(2,1)} %get-tuple-element.60.refs_1_.refs_0_, ...), custom_call_target="tpu_custom_call" | custom-call | flops 9663676416 | bytes 22020096 | tf_op jit(solution)/shard_map/pallas_call | solution.py:340
  538.5 1.9 collective-permute-start.66
  540.4 19.1 %shard_map.114 = (bf16[4,64,256]{2,1,0:T(8,128)(2,1)S(1)}, bf16[4,64,256]{2,1,0:T(8,128)(2,1)S(1)}, bf16[4,64,256]{2,1,0:T(8,128)(2,1)S(1)}, bf16[4,64,256]{2,1,0:T(8,128)(2,1)S(1)}) custom-call(s32[4]{0:T(128)S(1)} %pad_add_fusion.where, bf16[64,6144]{1,0:T(8,128)(2,1)S(1)} %copy-done.31, bf16[64,6144]{1,0:T(8,128)(2,1)S(1)} %copy-done.34, ...), custom_call_target="tpu_custom_call" | custom-call | flops 9663676416 | bytes 22020096 | tf_op jit(solution)/shard_map/pallas_call | solution.py:340
  562.9 2.9 collective-permute-start.64
  565.8 4.1 collective-permute-done.67.refs_19_
  569.9 2.5 collective-permute-start.69
  572.3 3.9 collective-permute-start.70
  576.2 5.7 collective-permute-done.63.refs_14_
  581.9 6.1 %collective-permute-start.60 = (bf16[4,64,256]{2,1,0:T(8,128)(2,1)S(1)}, bf16[4,64,256]{2,1,0:T(8,128)(2,1)S(1)}, u32[]{:S(2)}, u32[]{:S(2)}) collective-permute-start(bf16[4,64,256]{2,1,0:T(8,128)(2,1)S(1)} %get-tuple-element.96), channel_id=1, source_target_pairs={{0,8},{4,12},{8,0},{12,4},{1,9},{5,13},{9,1},{13,5},{2,10},{6,14},... | collective-permute-start | bytes 393224 | tf_op jit(solution)/shard_map/ppermute | solution.py:465
  588.0 1.5 collective-permute-start.61
  590.9 6.2 %collective-permute-done.60.refs_10_ = bf16[4,64,256]{2,1,0:T(8,128)(2,1)S(1)} collective-permute-done((bf16[4,64,256]{2,1,0:T(8,128)(2,1)S(1)}, bf16[4,64,256]{2,1,0:T(8,128)(2,1)S(1)}, u32[]{:S(2)}, u32[]{:S(2)}) %collective-permute-start.60) | collective-permute-done | bytes 131104 | tf_op jit(solution)/shard_map/ppermute | solution.py:465
  597.0 3.3 shard_map.115
  (233 shorter events, 50.3 us)
Async XLA Ops:
  0.6 18.9 %collective-permute-start.2 = (bf16[768,6144]{1,0:T(8,128)(2,1)}, bf16[768,6144]{1,0:T(8,128)(2,1)}, u32[]{:S(2)}, u32[]{:S(2)}) collective-permute-start(bf16[768,6144]{1,0:T(8,128)(2,1)} %own_ref.7), channel_id=1, source_target_pairs={{0,1},{1,0},{2,3},{3,2},{4,5},{5,4},{6,7},{7,6},{8,9},{9,8},{10,11... | collective-permute-start | bytes 28311560 | tf_op jit(solution)/shard_map/ppermute | solution.py:456
  29.9 109.4 %collective-permute-start.5 = (bf16[256,6144]{1,0:T(8,128)(2,1)}, bf16[256,6144]{1,0:T(8,128)(2,1)}, u32[]{:S(2)}, u32[]{:S(2)}) collective-permute-start(bf16[256,6144]{1,0:T(8,128)(2,1)} %shard_map.89.refs_1_), channel_id=1, source_target_pairs={{0,2},{2,0},{1,3},{3,1},{4,6},{6,4},{5,7},{7,5},{8,10},{10,8},{9,1... | collective-permute-start | bytes 9437192 | tf_op jit(solution)/shard_map/ppermute | solution.py:459
  32.5 30.7 %collective-permute-start = (bf16[768,768]{1,0:T(8,128)(2,1)S(1)}, bf16[768,768]{1,0:T(8,128)(2,1)}, u32[]{:S(2)}, u32[]{:S(2)}) collective-permute-start(bf16[768,768]{1,0:T(8,128)(2,1)S(1)} %shard_map.86.refs_0_), channel_id=1, source_target_pairs={{0,4},{4,8},{8,12},{12,0},{1,5},{5,9},{9,13},{13,1},{2,6},{6,10},{... | collective-permute-start | bytes 3538952 | tf_op jit(solution)/shard_map/ppermute | solution.py:465
  34.1 54.4 %collective-permute-start.4 = (bf16[768,768]{1,0:T(8,128)(2,1)}, bf16[768,768]{1,0:T(8,128)(2,1)}, u32[]{:S(2)}, u32[]{:S(2)}) collective-permute-start(bf16[768,768]{1,0:T(8,128)(2,1)} %shard_map.88.refs_0_), channel_id=1, source_target_pairs={{0,4},{4,8},{8,12},{12,0},{1,5},{5,9},{9,13},{13,1},{2,6},{6,10},{... | collective-permute-start | bytes 3538952 | tf_op jit(solution)/shard_map/ppermute | solution.py:465
  75.2 38.6 %collective-permute-start.7 = (bf16[768,768]{1,0:T(8,128)(2,1)}, bf16[768,768]{1,0:T(8,128)(2,1)}, u32[]{:S(2)}, u32[]{:S(2)}) collective-permute-start(bf16[768,768]{1,0:T(8,128)(2,1)} %shard_map.90.refs_0_.refs_17_), channel_id=1, source_target_pairs={{0,4},{4,8},{8,12},{12,0},{1,5},{5,9},{9,13},{13,1},{2,6},{6,10},{... | collective-permute-start | bytes 3538952 | tf_op jit(solution)/shard_map/ppermute | solution.py:465
  88.5 49.6 %collective-permute-start.6 = (bf16[768,768]{1,0:T(8,128)(2,1)}, bf16[768,768]{1,0:T(8,128)(2,1)S(1)}, u32[]{:S(2)}, u32[]{:S(2)}) collective-permute-start(bf16[768,768]{1,0:T(8,128)(2,1)} %shard_map.93.refs_0_.refs_17_), channel_id=1, source_target_pairs={{0,4},{4,8},{8,12},{12,0},{1,5},{5,9},{9,13},{13,1},{2,6},{6,10},{... | collective-permute-start | bytes 3538952 | tf_op jit(solution)/shard_map/ppermute | solution.py:465
  88.5 49.6 %collective-permute-start.8 = (bf16[768,768]{1,0:T(8,128)(2,1)}, bf16[768,768]{1,0:T(8,128)(2,1)}, u32[]{:S(2)}, u32[]{:S(2)}) collective-permute-start(bf16[768,768]{1,0:T(8,128)(2,1)} %shard_map.90.refs_0_.refs_17_), channel_id=1, source_target_pairs={{0,16},{16,0},{1,17},{17,1},{2,18},{18,2},{3,19},{19,3},{4,20},{20... | collective-permute-start | bytes 3538952 | tf_op jit(solution)/shard_map/ppermute | solution.py:462
  139.2 107.5 %collective-permute-start.9 = (bf16[256,6144]{1,0:T(8,128)(2,1)}, bf16[256,6144]{1,0:T(8,128)(2,1)}, u32[]{:S(2)}, u32[]{:S(2)}) collective-permute-start(bf16[256,6144]{1,0:T(8,128)(2,1)} %shard_map.97.rest_0_), channel_id=1, source_target_pairs={{0,2},{2,0},{1,3},{3,1},{4,6},{6,4},{5,7},{7,5},{8,10},{10,8},{9,1... | collective-permute-start | bytes 9437192 | tf_op jit(solution)/shard_map/ppermute | solution.py:459
  139.7 29.1 %collective-permute-start.12 = (bf16[768,768]{1,0:T(8,128)(2,1)}, bf16[768,768]{1,0:T(8,128)(2,1)S(1)}, u32[]{:S(2)}, u32[]{:S(2)}) collective-permute-start(bf16[768,768]{1,0:T(8,128)(2,1)} %shard_map.93.refs_0_.refs_17_), channel_id=1, source_target_pairs={{0,16},{16,0},{1,17},{17,1},{2,18},{18,2},{3,19},{19,3},{4,20},{20... | collective-permute-start | bytes 3538952 | tf_op jit(solution)/shard_map/ppermute | solution.py:462
  141.2 48.7 %collective-permute-start.11 = (bf16[768,768]{1,0:T(8,128)(2,1)}, bf16[768,768]{1,0:T(8,128)(2,1)S(1)}, u32[]{:S(2)}, u32[]{:S(2)}) collective-permute-start(bf16[768,768]{1,0:T(8,128)(2,1)} %shard_map.95.refs_1_.refs_18_), channel_id=1, source_target_pairs={{0,4},{4,8},{8,12},{12,0},{1,5},{5,9},{9,13},{13,1},{2,6},{6,10},{... | collective-permute-start | bytes 3538952 | tf_op jit(solution)/shard_map/ppermute | solution.py:465
  141.2 56.4 %collective-permute-start.10 = (bf16[768,768]{1,0:T(8,128)(2,1)}, bf16[768,768]{1,0:T(8,128)(2,1)S(1)}, u32[]{:S(2)}, u32[]{:S(2)}) collective-permute-start(bf16[768,768]{1,0:T(8,128)(2,1)} %shard_map.96.refs_2_.refs_18_), channel_id=1, source_target_pairs={{0,4},{4,8},{8,12},{12,0},{1,5},{5,9},{9,13},{13,1},{2,6},{6,10},{... | collective-permute-start | bytes 3538952 | tf_op jit(solution)/shard_map/ppermute | solution.py:465
  142.5 55.1 %collective-permute-start.13 = (bf16[768,768]{1,0:T(8,128)(2,1)}, bf16[768,768]{1,0:T(8,128)(2,1)S(1)}, u32[]{:S(2)}, u32[]{:S(2)}) collective-permute-start(bf16[768,768]{1,0:T(8,128)(2,1)} %shard_map.95.refs_1_.refs_18_), channel_id=1, source_target_pairs={{0,16},{16,0},{1,17},{17,1},{2,18},{18,2},{3,19},{19,3},{4,20},{20... | collective-permute-start | bytes 3538952 | tf_op jit(solution)/shard_map/ppermute | solution.py:462
  168.9 48.8 %collective-permute-start.17 = (bf16[768,768]{1,0:T(8,128)(2,1)}, bf16[768,768]{1,0:T(8,128)(2,1)S(1)}, u32[]{:S(2)}, u32[]{:S(2)}) collective-permute-start(bf16[768,768]{1,0:T(8,128)(2,1)} %shard_map.96.refs_2_.refs_18_), channel_id=1, source_target_pairs={{0,16},{16,0},{1,17},{17,1},{2,18},{18,2},{3,19},{19,3},{4,20},{20... | collective-permute-start | bytes 3538952 | tf_op jit(solution)/shard_map/ppermute | solution.py:462
  189.9 29.0 %collective-permute-start.14 = (bf16[64,6144]{1,0:T(8,128)(2,1)S(1)}, bf16[64,6144]{1,0:T(8,128)(2,1)}, u32[]{:S(2)}, u32[]{:S(2)}) collective-permute-start(bf16[64,6144]{1,0:T(8,128)(2,1)S(1)} %get-tuple-element.62), channel_id=1, source_target_pairs={{0,4},{4,8},{8,12},{12,0},{1,5},{5,9},{9,13},{13,1},{2,6},{6,10},{... | collective-permute-start | bytes 2359304 | tf_op jit(solution)/shard_map/ppermute | solution.py:465
  197.6 48.3 %collective-permute-start.15 = (bf16[64,6144]{1,0:T(8,128)(2,1)}, bf16[64,6144]{1,0:T(8,128)(2,1)}, u32[]{:S(2)}, u32[]{:S(2)}) collective-permute-start(bf16[64,6144]{1,0:T(8,128)(2,1)} %get-tuple-element.63), channel_id=1, source_target_pairs={{0,8},{4,12},{8,0},{12,4},{1,9},{5,13},{9,1},{13,5},{2,10},{6,14},... | collective-permute-start | bytes 2359304 | tf_op jit(solution)/shard_map/ppermute | solution.py:465
  197.6 70.3 %collective-permute-start.16 = (bf16[64,6144]{1,0:T(8,128)(2,1)}, bf16[64,6144]{1,0:T(8,128)(2,1)}, u32[]{:S(2)}, u32[]{:S(2)}) collective-permute-start(bf16[64,6144]{1,0:T(8,128)(2,1)} %get-tuple-element.64), channel_id=1, source_target_pairs={{0,12},{4,0},{8,4},{12,8},{1,13},{5,1},{9,5},{13,9},{2,14},{6,2},{... | collective-permute-start | bytes 2359304 | tf_op jit(solution)/shard_map/ppermute | solution.py:465
  217.7 51.8 %collective-permute-start.18 = (bf16[64,6144]{1,0:T(8,128)(2,1)}, bf16[64,6144]{1,0:T(8,128)(2,1)S(1)}, u32[]{:S(2)}, u32[]{:S(2)}) collective-permute-start(bf16[64,6144]{1,0:T(8,128)(2,1)} %get-tuple-element.60.refs_1_.refs_0_), channel_id=1, source_target_pairs={{0,2},{2,0},{1,3},{3,1},{4,6},{6,4},{5,7},{7,5},{8,10},{10,8},{9,1... | collective-permute-start | bytes 2359304 | tf_op jit(solution)/shard_map/ppermute | solution.py:459
  218.9 51.0 %collective-permute-start.23 = (bf16[64,6144]{1,0:T(8,128)(2,1)}, bf16[64,6144]{1,0:T(8,128)(2,1)}, u32[]{:S(2)}, u32[]{:S(2)}) collective-permute-start(bf16[64,6144]{1,0:T(8,128)(2,1)} %get-tuple-element.60.refs_1_.refs_0_), channel_id=1, source_target_pairs={{0,1},{1,0},{2,3},{3,2},{4,5},{5,4},{6,7},{7,6},{8,9},{9,8},{10,11... | collective-permute-start | bytes 2359304 | tf_op jit(solution)/shard_map/ppermute | solution.py:456
  245.9 29.2 %collective-permute-start.22 = (bf16[768,768]{1,0:T(8,128)(2,1)}, bf16[768,768]{1,0:T(8,128)(2,1)}, u32[]{:S(2)}, u32[]{:S(2)}) collective-permute-start(bf16[768,768]{1,0:T(8,128)(2,1)} %shard_map.99.refs_1_.refs_19_), channel_id=1, source_target_pairs={{0,16},{16,0},{1,17},{17,1},{2,18},{18,2},{3,19},{19,3},{4,20},{20... | collective-permute-start | bytes 3538952 | tf_op jit(solution)/shard_map/ppermute | solution.py:462
  246.7 52.6 %collective-permute-start.34 = (bf16[768,768]{1,0:T(8,128)(2,1)}, bf16[768,768]{1,0:T(8,128)(2,1)}, u32[]{:S(2)}, u32[]{:S(2)}) collective-permute-start(bf16[768,768]{1,0:T(8,128)(2,1)} %shard_map.100.rest_1_.refs_19_), channel_id=1, source_target_pairs={{0,16},{16,0},{1,17},{17,1},{2,18},{18,2},{3,19},{19,3},{4,20},{20... | collective-permute-start | bytes 3538952 | tf_op jit(solution)/shard_map/ppermute | solution.py:462
  267.9 33.2 %collective-permute-start.19 = (bf16[64,6144]{1,0:T(8,128)(2,1)}, bf16[64,6144]{1,0:T(8,128)(2,1)S(1)}, u32[]{:S(2)}, u32[]{:S(2)}) collective-permute-start(bf16[64,6144]{1,0:T(8,128)(2,1)} %get-tuple-element.66.refs_4_.refs_1_), channel_id=1, source_target_pairs={{0,2},{2,0},{1,3},{3,1},{4,6},{6,4},{5,7},{7,5},{8,10},{10,8},{9,1... | collective-permute-start | bytes 2359304 | tf_op jit(solution)/shard_map/ppermute | solution.py:459
  269.4 44.3 %collective-permute-start.20 = (bf16[64,6144]{1,0:T(8,128)(2,1)}, bf16[64,6144]{1,0:T(8,128)(2,1)S(1)}, u32[]{:S(2)}, u32[]{:S(2)}) collective-permute-start(bf16[64,6144]{1,0:T(8,128)(2,1)} %get-tuple-element.67.refs_2_), channel_id=1, source_target_pairs={{0,2},{2,0},{1,3},{3,1},{4,6},{6,4},{5,7},{7,5},{8,10},{10,8},{9,1... | collective-permute-start | bytes 2359304 | tf_op jit(solution)/shard_map/ppermute | solution.py:459
  270.0 50.7 %collective-permute-start.21 = (bf16[64,6144]{1,0:T(8,128)(2,1)}, bf16[64,6144]{1,0:T(8,128)(2,1)S(1)}, u32[]{:S(2)}, u32[]{:S(2)}) collective-permute-start(bf16[64,6144]{1,0:T(8,128)(2,1)} %get-tuple-element.68.refs_3_), channel_id=1, source_target_pairs={{0,2},{2,0},{1,3},{3,1},{4,6},{6,4},{5,7},{7,5},{8,10},{10,8},{9,1... | collective-permute-start | bytes 2359304 | tf_op jit(solution)/shard_map/ppermute | solution.py:459
  275.1 45.5 %collective-permute-start.31 = (bf16[64,6144]{1,0:T(8,128)(2,1)}, bf16[64,6144]{1,0:T(8,128)(2,1)S(1)}, u32[]{:S(2)}, u32[]{:S(2)}) collective-permute-start(bf16[64,6144]{1,0:T(8,128)(2,1)} %copy-done.43), channel_id=1, source_target_pairs={{0,4},{4,8},{8,12},{12,0},{1,5},{5,9},{9,13},{13,1},{2,6},{6,10},{... | collective-permute-start | bytes 2359304 | tf_op jit(solution)/shard_map/ppermute | solution.py:465
  299.3 38.6 %collective-permute-start.32 = (bf16[64,6144]{1,0:T(8,128)(2,1)}, bf16[64,6144]{1,0:T(8,128)(2,1)}, u32[]{:S(2)}, u32[]{:S(2)}) collective-permute-start(bf16[64,6144]{1,0:T(8,128)(2,1)} %copy-done.42), channel_id=1, source_target_pairs={{0,8},{4,12},{8,0},{12,4},{1,9},{5,13},{9,1},{13,5},{2,10},{6,14},... | collective-permute-start | bytes 2359304 | tf_op jit(solution)/shard_map/ppermute | solution.py:465
  301.2 36.8 %collective-permute-start.33 = (bf16[64,6144]{1,0:T(8,128)(2,1)}, bf16[64,6144]{1,0:T(8,128)(2,1)}, u32[]{:S(2)}, u32[]{:S(2)}) collective-permute-start(bf16[64,6144]{1,0:T(8,128)(2,1)} %copy-done.41), channel_id=1, source_target_pairs={{0,12},{4,0},{8,4},{12,8},{1,13},{5,1},{9,5},{13,9},{2,14},{6,2},{... | collective-permute-start | bytes 2359304 | tf_op jit(solution)/shard_map/ppermute | solution.py:465
  313.7 24.7 %collective-permute-start.24 = (bf16[64,6144]{1,0:T(8,128)(2,1)}, bf16[64,6144]{1,0:T(8,128)(2,1)}, u32[]{:S(2)}, u32[]{:S(2)}) collective-permute-start(bf16[64,6144]{1,0:T(8,128)(2,1)} %get-tuple-element.66.refs_4_.refs_1_), channel_id=1, source_target_pairs={{0,1},{1,0},{2,3},{3,2},{4,5},{5,4},{6,7},{7,6},{8,9},{9,8},{10,11... | collective-permute-start | bytes 2359304 | tf_op jit(solution)/shard_map/ppermute | solution.py:456
  320.6 17.9 %collective-permute-start.25 = (bf16[64,6144]{1,0:T(8,128)(2,1)}, bf16[64,6144]{1,0:T(8,128)(2,1)}, u32[]{:S(2)}, u32[]{:S(2)}) collective-permute-start(bf16[64,6144]{1,0:T(8,128)(2,1)} %get-tuple-element.67.refs_2_), channel_id=1, source_target_pairs={{0,1},{1,0},{2,3},{3,2},{4,5},{5,4},{6,7},{7,6},{8,9},{9,8},{10,11... | collective-permute-start | bytes 2359304 | tf_op jit(solution)/shard_map/ppermute | solution.py:456
  321.6 17.5 %collective-permute-start.26 = (bf16[64,6144]{1,0:T(8,128)(2,1)}, bf16[64,6144]{1,0:T(8,128)(2,1)}, u32[]{:S(2)}, u32[]{:S(2)}) collective-permute-start(bf16[64,6144]{1,0:T(8,128)(2,1)} %get-tuple-element.68.refs_3_), channel_id=1, source_target_pairs={{0,1},{1,0},{2,3},{3,2},{4,5},{5,4},{6,7},{7,6},{8,9},{9,8},{10,11... | collective-permute-start | bytes 2359304 | tf_op jit(solution)/shard_map/ppermute | solution.py:456
  337.9 17.1 %collective-permute-start.27 = (bf16[64,6144]{1,0:T(8,128)(2,1)}, bf16[64,6144]{1,0:T(8,128)(2,1)S(1)}, u32[]{:S(2)}, u32[]{:S(2)}) collective-permute-start(bf16[64,6144]{1,0:T(8,128)(2,1)} %get-tuple-element.69.refs_4_), channel_id=1, source_target_pairs={{0,1},{1,0},{2,3},{3,2},{4,5},{5,4},{6,7},{7,6},{8,9},{9,8},{10,11... | collective-permute-start | bytes 2359304 | tf_op jit(solution)/shard_map/ppermute | solution.py:456
  337.9 17.1 %collective-permute-start.28 = (bf16[64,6144]{1,0:T(8,128)(2,1)}, bf16[64,6144]{1,0:T(8,128)(2,1)}, u32[]{:S(2)}, u32[]{:S(2)}) collective-permute-start(bf16[64,6144]{1,0:T(8,128)(2,1)} %get-tuple-element.70.refs_5_), channel_id=1, source_target_pairs={{0,1},{1,0},{2,3},{3,2},{4,5},{5,4},{6,7},{7,6},{8,9},{9,8},{10,11... | collective-permute-start | bytes 2359304 | tf_op jit(solution)/shard_map/ppermute | solution.py:456
  338.5 16.6 %collective-permute-start.29 = (bf16[64,6144]{1,0:T(8,128)(2,1)}, bf16[64,6144]{1,0:T(8,128)(2,1)}, u32[]{:S(2)}, u32[]{:S(2)}) collective-permute-start(bf16[64,6144]{1,0:T(8,128)(2,1)} %get-tuple-element.71.refs_6_), channel_id=1, source_target_pairs={{0,1},{1,0},{2,3},{3,2},{4,5},{5,4},{6,7},{7,6},{8,9},{9,8},{10,11... | collective-permute-start | bytes 2359304 | tf_op jit(solution)/shard_map/ppermute | solution.py:456
  338.5 16.6 %collective-permute-start.30 = (bf16[64,6144]{1,0:T(8,128)(2,1)}, bf16[64,6144]{1,0:T(8,128)(2,1)}, u32[]{:S(2)}, u32[]{:S(2)}) collective-permute-start(bf16[64,6144]{1,0:T(8,128)(2,1)} %get-tuple-element.72.refs_7_), channel_id=1, source_target_pairs={{0,1},{1,0},{2,3},{3,2},{4,5},{5,4},{6,7},{7,6},{8,9},{9,8},{10,11... | collective-permute-start | bytes 2359304 | tf_op jit(solution)/shard_map/ppermute | solution.py:456
  339.1 44.7 %collective-permute-start.38 = (bf16[768,768]{1,0:T(8,128)(2,1)}, bf16[768,768]{1,0:T(8,128)(2,1)}, u32[]{:S(2)}, u32[]{:S(2)}) collective-permute-start(bf16[768,768]{1,0:T(8,128)(2,1)} %get-tuple-element.76.refs_23_), channel_id=1, source_target_pairs={{0,4},{4,8},{8,12},{12,0},{1,5},{5,9},{9,13},{13,1},{2,6},{6,10},{... | collective-permute-start | bytes 3538952 | tf_op jit(solution)/shard_map/ppermute | solution.py:465
  383.7 29.6 %collective-permute-start.42 = (bf16[768,768]{1,0:T(8,128)(2,1)}, bf16[768,768]{1,0:T(8,128)(2,1)}, u32[]{:S(2)}, u32[]{:S(2)}) collective-permute-start(bf16[768,768]{1,0:T(8,128)(2,1)} %shard_map.106.refs_23_.refs_17_), channel_id=1, source_target_pairs={{0,4},{4,8},{8,12},{12,0},{1,5},{5,9},{9,13},{13,1},{2,6},{6,10},{... | collective-permute-start | bytes 3538952 | tf_op jit(solution)/shard_map/ppermute | solution.py:465
  383.7 30.1 %collective-permute-start.44 = (bf16[64,6144]{1,0:T(8,128)(2,1)}, bf16[64,6144]{1,0:T(8,128)(2,1)S(1)}, u32[]{:S(2)}, u32[]{:S(2)}) collective-permute-start(bf16[64,6144]{1,0:T(8,128)(2,1)} %copy-done.30), channel_id=1, source_target_pairs={{0,2},{2,0},{1,3},{3,1},{4,6},{6,4},{5,7},{7,5},{8,10},{10,8},{9,1... | collective-permute-start | bytes 2359304 | tf_op jit(solution)/shard_map/ppermute | solution.py:459
  385.3 36.1 %collective-permute-start.45 = (bf16[64,6144]{1,0:T(8,128)(2,1)}, bf16[64,6144]{1,0:T(8,128)(2,1)}, u32[]{:S(2)}, u32[]{:S(2)}) collective-permute-start(bf16[64,6144]{1,0:T(8,128)(2,1)} %get-tuple-element.85.refs_1_), channel_id=1, source_target_pairs={{0,2},{2,0},{1,3},{3,1},{4,6},{6,4},{5,7},{7,5},{8,10},{10,8},{9,1... | collective-permute-start | bytes 2359304 | tf_op jit(solution)/shard_map/ppermute | solution.py:459
  385.8 52.5 %collective-permute-start.46 = (bf16[64,6144]{1,0:T(8,128)(2,1)}, bf16[64,6144]{1,0:T(8,128)(2,1)}, u32[]{:S(2)}, u32[]{:S(2)}) collective-permute-start(bf16[64,6144]{1,0:T(8,128)(2,1)} %get-tuple-element.86.refs_2_), channel_id=1, source_target_pairs={{0,2},{2,0},{1,3},{3,1},{4,6},{6,4},{5,7},{7,5},{8,10},{10,8},{9,1... | collective-permute-start | bytes 2359304 | tf_op jit(solution)/shard_map/ppermute | solution.py:459
  387.3 66.3 %collective-permute-start.47 = (bf16[64,6144]{1,0:T(8,128)(2,1)}, bf16[64,6144]{1,0:T(8,128)(2,1)}, u32[]{:S(2)}, u32[]{:S(2)}) collective-permute-start(bf16[64,6144]{1,0:T(8,128)(2,1)} %get-tuple-element.87.refs_3_), channel_id=1, source_target_pairs={{0,2},{2,0},{1,3},{3,1},{4,6},{6,4},{5,7},{7,5},{8,10},{10,8},{9,1... | collective-permute-start | bytes 2359304 | tf_op jit(solution)/shard_map/ppermute | solution.py:459
  413.3 43.1 %collective-permute-start.48 = (bf16[768,768]{1,0:T(8,128)(2,1)}, bf16[768,768]{1,0:T(8,128)(2,1)}, u32[]{:S(2)}, u32[]{:S(2)}) collective-permute-start(bf16[768,768]{1,0:T(8,128)(2,1)} %shard_map.106.refs_23_.refs_17_), channel_id=1, source_target_pairs={{0,16},{16,0},{1,17},{17,1},{2,18},{18,2},{3,19},{19,3},{4,20},{20... | collective-permute-start | bytes 3538952 | tf_op jit(solution)/shard_map/ppermute | solution.py:462
  413.8 42.9 %collective-permute-start.43 = (bf16[768,768]{1,0:T(8,128)(2,1)}, bf16[768,768]{1,0:T(8,128)(2,1)}, u32[]{:S(2)}, u32[]{:S(2)}) collective-permute-start(bf16[768,768]{1,0:T(8,128)(2,1)} %shard_map.108.refs_4_.refs_18_), channel_id=1, source_target_pairs={{0,4},{4,8},{8,12},{12,0},{1,5},{5,9},{9,13},{13,1},{2,6},{6,10},{... | collective-permute-start | bytes 3538952 | tf_op jit(solution)/shard_map/ppermute | solution.py:465
  421.4 32.3 %collective-permute-start.51 = (bf16[64,6144]{1,0:T(8,128)(2,1)}, bf16[64,6144]{1,0:T(8,128)(2,1)}, u32[]{:S(2)}, u32[]{:S(2)}) collective-permute-start(bf16[64,6144]{1,0:T(8,128)(2,1)} %copy-done.30), channel_id=1, source_target_pairs={{0,1},{1,0},{2,3},{3,2},{4,5},{5,4},{6,7},{7,6},{8,9},{9,8},{10,11... | collective-permute-start | bytes 2359304 | tf_op jit(solution)/shard_map/ppermute | solution.py:456
  438.2 15.9 %collective-permute-start.52 = (bf16[64,6144]{1,0:T(8,128)(2,1)}, bf16[64,6144]{1,0:T(8,128)(2,1)}, u32[]{:S(2)}, u32[]{:S(2)}) collective-permute-start(bf16[64,6144]{1,0:T(8,128)(2,1)} %get-tuple-element.85.refs_1_), channel_id=1, source_target_pairs={{0,1},{1,0},{2,3},{3,2},{4,5},{5,4},{6,7},{7,6},{8,9},{9,8},{10,11... | collective-permute-start | bytes 2359304 | tf_op jit(solution)/shard_map/ppermute | solution.py:456
  456.8 6.9 %collective-permute-start.58 = (bf16[64,6144]{1,0:T(8,128)(2,1)}, bf16[64,6144]{1,0:T(8,128)(2,1)}, u32[]{:S(2)}, u32[]{:S(2)}) collective-permute-start(bf16[64,6144]{1,0:T(8,128)(2,1)} %get-tuple-element.91.refs_7_), channel_id=1, source_target_pairs={{0,1},{1,0},{2,3},{3,2},{4,5},{5,4},{6,7},{7,6},{8,9},{9,8},{10,11... | collective-permute-start | bytes 2359304 | tf_op jit(solution)/shard_map/ppermute | solution.py:456
  457.4 79.0 %collective-permute-start.35 = (bf16[4,64,256]{2,1,0:T(8,128)(2,1)}, bf16[4,64,256]{2,1,0:T(8,128)(2,1)S(1)}, u32[]{:S(2)}, u32[]{:S(2)}) collective-permute-start(bf16[4,64,256]{2,1,0:T(8,128)(2,1)} %copy-done.46), channel_id=1, source_target_pairs={{0,4},{4,8},{8,12},{12,0},{1,5},{5,9},{9,13},{13,1},{2,6},{6,10},{... | collective-permute-start | bytes 393224 | tf_op jit(solution)/shard_map/ppermute | solution.py:465
  458.5 79.4 %collective-permute-start.36 = (bf16[4,64,256]{2,1,0:T(8,128)(2,1)}, bf16[4,64,256]{2,1,0:T(8,128)(2,1)S(1)}, u32[]{:S(2)}, u32[]{:S(2)}) collective-permute-start(bf16[4,64,256]{2,1,0:T(8,128)(2,1)} %copy-done.45), channel_id=1, source_target_pairs={{0,8},{4,12},{8,0},{12,4},{1,9},{5,13},{9,1},{13,5},{2,10},{6,14},... | collective-permute-start | bytes 393224 | tf_op jit(solution)/shard_map/ppermute | solution.py:465
  461.5 77.0 %collective-permute-start.37 = (bf16[4,64,256]{2,1,0:T(8,128)(2,1)}, bf16[4,64,256]{2,1,0:T(8,128)(2,1)S(1)}, u32[]{:S(2)}, u32[]{:S(2)}) collective-permute-start(bf16[4,64,256]{2,1,0:T(8,128)(2,1)} %copy-done.44), channel_id=1, source_target_pairs={{0,12},{4,0},{8,4},{12,8},{1,13},{5,1},{9,5},{13,9},{2,14},{6,2},{... | collective-permute-start | bytes 393224 | tf_op jit(solution)/shard_map/ppermute | solution.py:465
  463.2 42.4 %collective-permute-start.49 = (bf16[768,768]{1,0:T(8,128)(2,1)}, bf16[768,768]{1,0:T(8,128)(2,1)S(1)}, u32[]{:S(2)}, u32[]{:S(2)}) collective-permute-start(bf16[768,768]{1,0:T(8,128)(2,1)} %shard_map.108.refs_4_.refs_18_), channel_id=1, source_target_pairs={{0,16},{16,0},{1,17},{17,1},{2,18},{18,2},{3,19},{19,3},{4,20},{20... | collective-permute-start | bytes 3538952 | tf_op jit(solution)/shard_map/ppermute | solution.py:462
  463.7 52.7 %collective-permute-start.50 = (bf16[768,768]{1,0:T(8,128)(2,1)}, bf16[768,768]{1,0:T(8,128)(2,1)S(1)}, u32[]{:S(2)}, u32[]{:S(2)}) collective-permute-start(bf16[768,768]{1,0:T(8,128)(2,1)} %shard_map.110.refs_23_.refs_19_), channel_id=1, source_target_pairs={{0,16},{16,0},{1,17},{17,1},{2,18},{18,2},{3,19},{19,3},{4,20},{20... | collective-permute-start | bytes 3538952 | tf_op jit(solution)/shard_map/ppermute | solution.py:462
  505.6 53.9 %collective-permute-start.39 = (bf16[4,64,256]{2,1,0:T(8,128)(2,1)S(1)}, bf16[4,64,256]{2,1,0:T(8,128)(2,1)S(1)}, u32[]{:S(2)}, u32[]{:S(2)}) collective-permute-start(bf16[4,64,256]{2,1,0:T(8,128)(2,1)S(1)} %get-tuple-element.82), channel_id=1, source_target_pairs={{0,4},{4,8},{8,12},{12,0},{1,5},{5,9},{9,13},{13,1},{2,6},{6,10},{... | collective-permute-start | bytes 393224 | tf_op jit(solution)/shard_map/ppermute | solution.py:465
  516.4 44.5 %collective-permute-start.40 = (bf16[4,64,256]{2,1,0:T(8,128)(2,1)S(1)}, bf16[4,64,256]{2,1,0:T(8,128)(2,1)S(1)}, u32[]{:S(2)}, u32[]{:S(2)}) collective-permute-start(bf16[4,64,256]{2,1,0:T(8,128)(2,1)S(1)} %get-tuple-element.83), channel_id=1, source_target_pairs={{0,8},{4,12},{8,0},{12,4},{1,9},{5,13},{9,1},{13,5},{2,10},{6,14},... | collective-permute-start | bytes 393224 | tf_op jit(solution)/shard_map/ppermute | solution.py:465
  536.4 25.2 %collective-permute-start.41 = (bf16[4,64,256]{2,1,0:T(8,128)(2,1)S(1)}, bf16[4,64,256]{2,1,0:T(8,128)(2,1)S(1)}, u32[]{:S(2)}, u32[]{:S(2)}) collective-permute-start(bf16[4,64,256]{2,1,0:T(8,128)(2,1)S(1)} %get-tuple-element.84), channel_id=1, source_target_pairs={{0,12},{4,0},{8,4},{12,8},{1,13},{5,1},{9,5},{13,9},{2,14},{6,2},{... | collective-permute-start | bytes 393224 | tf_op jit(solution)/shard_map/ppermute | solution.py:465
  537.9 25.1 %collective-permute-start.65 = (bf16[4,64,256]{2,1,0:T(8,128)(2,1)S(1)}, bf16[4,64,256]{2,1,0:T(8,128)(2,1)S(1)}, u32[]{:S(2)}, u32[]{:S(2)}) collective-permute-start(bf16[4,64,256]{2,1,0:T(8,128)(2,1)S(1)} %get-tuple-element.101), channel_id=1, source_target_pairs={{0,4},{4,8},{8,12},{12,0},{1,5},{5,9},{9,13},{13,1},{2,6},{6,10},{... | collective-permute-start | bytes 393224 | tf_op jit(solution)/shard_map/ppermute | solution.py:465
  538.5 27.3 %collective-permute-start.66 = (bf16[4,64,256]{2,1,0:T(8,128)(2,1)S(1)}, bf16[4,64,256]{2,1,0:T(8,128)(2,1)S(1)}, u32[]{:S(2)}, u32[]{:S(2)}) collective-permute-start(bf16[4,64,256]{2,1,0:T(8,128)(2,1)S(1)} %get-tuple-element.102), channel_id=1, source_target_pairs={{0,8},{4,12},{8,0},{12,4},{1,9},{5,13},{9,1},{13,5},{2,10},{6,14},... | collective-permute-start | bytes 393224 | tf_op jit(solution)/shard_map/ppermute | solution.py:465
  559.5 10.4 %collective-permute-start.67 = (bf16[4,64,256]{2,1,0:T(8,128)(2,1)S(1)}, bf16[4,64,256]{2,1,0:T(8,128)(2,1)S(1)}, u32[]{:S(2)}, u32[]{:S(2)}) collective-permute-start(bf16[4,64,256]{2,1,0:T(8,128)(2,1)S(1)} %get-tuple-element.103), channel_id=1, source_target_pairs={{0,12},{4,0},{8,4},{12,8},{1,13},{5,1},{9,5},{13,9},{2,14},{6,2},{... | collective-permute-start | bytes 393224 | tf_op jit(solution)/shard_map/ppermute | solution.py:465
  560.9 11.4 %collective-permute-start.62 = (bf16[4,64,256]{2,1,0:T(8,128)(2,1)S(1)}, bf16[4,64,256]{2,1,0:T(8,128)(2,1)S(1)}, u32[]{:S(2)}, u32[]{:S(2)}) collective-permute-start(bf16[4,64,256]{2,1,0:T(8,128)(2,1)S(1)} %get-tuple-element.98), channel_id=1, source_target_pairs={{0,4},{4,8},{8,12},{12,0},{1,5},{5,9},{9,13},{13,1},{2,6},{6,10},{... | collective-permute-start | bytes 393224 | tf_op jit(solution)/shard_map/ppermute | solution.py:465
  561.6 20.3 %collective-permute-start.63 = (bf16[4,64,256]{2,1,0:T(8,128)(2,1)S(1)}, bf16[4,64,256]{2,1,0:T(8,128)(2,1)S(1)}, u32[]{:S(2)}, u32[]{:S(2)}) collective-permute-start(bf16[4,64,256]{2,1,0:T(8,128)(2,1)S(1)} %get-tuple-element.99), channel_id=1, source_target_pairs={{0,8},{4,12},{8,0},{12,4},{1,9},{5,13},{9,1},{13,5},{2,10},{6,14},... | collective-permute-start | bytes 393224 | tf_op jit(solution)/shard_map/ppermute | solution.py:465
  562.9 19.0 %collective-permute-start.64 = (bf16[4,64,256]{2,1,0:T(8,128)(2,1)S(1)}, bf16[4,64,256]{2,1,0:T(8,128)(2,1)S(1)}, u32[]{:S(2)}, u32[]{:S(2)}) collective-permute-start(bf16[4,64,256]{2,1,0:T(8,128)(2,1)S(1)} %get-tuple-element.100), channel_id=1, source_target_pairs={{0,12},{4,0},{8,4},{12,8},{1,13},{5,1},{9,5},{13,9},{2,14},{6,2},{... | collective-permute-start | bytes 393224 | tf_op jit(solution)/shard_map/ppermute | solution.py:465
  565.8 22.3 %collective-permute-start.68 = (bf16[4,64,256]{2,1,0:T(8,128)(2,1)S(1)}, bf16[4,64,256]{2,1,0:T(8,128)(2,1)S(1)}, u32[]{:S(2)}, u32[]{:S(2)}) collective-permute-start(bf16[4,64,256]{2,1,0:T(8,128)(2,1)S(1)} %get-tuple-element.105), channel_id=1, source_target_pairs={{0,4},{4,8},{8,12},{12,0},{1,5},{5,9},{9,13},{13,1},{2,6},{6,10},{... | collective-permute-start | bytes 393224 | tf_op jit(solution)/shard_map/ppermute | solution.py:465
  569.9 21.0 %collective-permute-start.69 = (bf16[4,64,256]{2,1,0:T(8,128)(2,1)S(1)}, bf16[4,64,256]{2,1,0:T(8,128)(2,1)S(1)}, u32[]{:S(2)}, u32[]{:S(2)}) collective-permute-start(bf16[4,64,256]{2,1,0:T(8,128)(2,1)S(1)} %get-tuple-element.106), channel_id=1, source_target_pairs={{0,8},{4,12},{8,0},{12,4},{1,9},{5,13},{9,1},{13,5},{2,10},{6,14},... | collective-permute-start | bytes 393224 | tf_op jit(solution)/shard_map/ppermute | solution.py:465
  572.3 18.6 %collective-permute-start.70 = (bf16[4,64,256]{2,1,0:T(8,128)(2,1)S(1)}, bf16[4,64,256]{2,1,0:T(8,128)(2,1)S(1)}, u32[]{:S(2)}, u32[]{:S(2)}) collective-permute-start(bf16[4,64,256]{2,1,0:T(8,128)(2,1)S(1)} %get-tuple-element.107), channel_id=1, source_target_pairs={{0,12},{4,0},{8,4},{12,8},{1,13},{5,1},{9,5},{13,9},{2,14},{6,2},{... | collective-permute-start | bytes 393224 | tf_op jit(solution)/shard_map/ppermute | solution.py:465
  581.9 9.0 %collective-permute-start.59 = (bf16[4,64,256]{2,1,0:T(8,128)(2,1)S(1)}, bf16[4,64,256]{2,1,0:T(8,128)(2,1)S(1)}, u32[]{:S(2)}, u32[]{:S(2)}) collective-permute-start(bf16[4,64,256]{2,1,0:T(8,128)(2,1)S(1)} %get-tuple-element.95), channel_id=1, source_target_pairs={{0,4},{4,8},{8,12},{12,0},{1,5},{5,9},{9,13},{13,1},{2,6},{6,10},{... | collective-permute-start | bytes 393224 | tf_op jit(solution)/shard_map/ppermute | solution.py:465
  581.9 15.1 %collective-permute-start.60 = (bf16[4,64,256]{2,1,0:T(8,128)(2,1)S(1)}, bf16[4,64,256]{2,1,0:T(8,128)(2,1)S(1)}, u32[]{:S(2)}, u32[]{:S(2)}) collective-permute-start(bf16[4,64,256]{2,1,0:T(8,128)(2,1)S(1)} %get-tuple-element.96), channel_id=1, source_target_pairs={{0,8},{4,12},{8,0},{12,4},{1,9},{5,13},{9,1},{13,5},{2,10},{6,14},... | collective-permute-start | bytes 393224 | tf_op jit(solution)/shard_map/ppermute | solution.py:465
  588.0 9.0 %collective-permute-start.61 = (bf16[4,64,256]{2,1,0:T(8,128)(2,1)S(1)}, bf16[4,64,256]{2,1,0:T(8,128)(2,1)S(1)}, u32[]{:S(2)}, u32[]{:S(2)}) collective-permute-start(bf16[4,64,256]{2,1,0:T(8,128)(2,1)S(1)} %get-tuple-element.97), channel_id=1, source_target_pairs={{0,12},{4,0},{8,4},{12,8},{1,13},{5,1},{9,5},{13,9},{2,14},{6,2},{... | collective-permute-start | bytes 393224 | tf_op jit(solution)/shard_map/ppermute | solution.py:465
  (68 other events, 594.5 us)

commit v3 on v2

--- a/solution.py
+++ b/solution.py
@@ -246,42 +246,37 @@
     )(where, keep, came, own_weight, other_weight, branch, resid, gain, *written, *earlier)
 
 
-def project_kernel(steps, ways, share, piece_rows, part_at, where, *refs):
-    pieces = refs[:steps * 2 * ways]
-    at = steps * 2 * ways
-    own_ref, near, far = refs[at], refs[at + 1:at + ways], refs[at + ways:at + 2 * ways - 1]
+def project_kernel(steps, ways, share, places, block, other, where, *refs):
+    pieces = refs[:steps * 2]
+    own_ref, came = refs[steps * 2], refs[steps * 2 + 1:steps * 2 + 1 + len(places)]
     outs = refs[-5 - ways:-5]
     rows_buf, weight_buf, qkv_buf, rows_sem, weight_sem = refs[-5:]
-    plane, home = where[3], where[2]
-    half = near[0].shape[0]
-    group = ways * piece_rows
-    heads = qkv_buf.shape[2] // HD
-
-    width = heads * HD
+    home = where[2]
+    part_at = 1 - where[3] if other else where[3]
+    group = pieces[0].shape[0]
+    piece_rows = group // ways
+    width = qkv_buf.shape[1] // 3
+    heads = width // HD
+
     copies = [pltpu.make_async_copy(
-        own_ref.at[part, :, part_at * width:(part_at + 1) * width],
+        own_ref.at[part, :, pl.ds(pl.multiple_of(part_at * width, width), width)],
         weight_buf.at[
-            pl.ds(pl.multiple_of(home * 2 * half, half), 2 * half),
+            pl.ds(pl.multiple_of(home * block, block), block),
             part * width:(part + 1) * width,
         ],
-        weight_sem.at[2 * ways - 2 + part]) for part in range(3)]
-    for way in range(1, ways):
-        base = lax.rem(home + ways - way, ways) * 2 * half
+        weight_sem.at[len(places) + part]) for part in range(3)]
+    for n, (way, first) in enumerate(places):
+        rows = came[n].shape[0]
+        base = pl.multiple_of(lax.rem(home + ways - way, ways) * block + first, rows)
         copies.append(pltpu.make_async_copy(
-            near[way - 1],
-            weight_buf.at[pl.ds(pl.multiple_of(base + plane * half, half), half)],
-            weight_sem.at[2 * way - 2]))
-        copies.append(pltpu.make_async_copy(
-            far[way - 1],
-            weight_buf.at[pl.ds(pl.multiple_of(base + (1 - plane) * half, half), half)],
-            weight_sem.at[2 * way - 1]))
+            came[n], weight_buf.at[pl.ds(base, rows)], weight_sem.at[n]))
 
     def row_copies(step):
         slot = step % 2
         return [pltpu.make_async_copy(
-            pieces[step * 2 * ways + n],
-            rows_buf.at[slot, pl.ds(n * piece_rows, piece_rows)],
-            rows_sem.at[slot, n]) for n in range(2 * ways)]
+            pieces[step * 2 + n],
+            rows_buf.at[slot, pl.ds(n * group, group)],
+            rows_sem.at[slot, n]) for n in range(2)]
 
     for copy in row_copies(0):
         copy.start()
@@ -305,21 +300,17 @@
                     for copy in copies:
                         copy.wait()
 
-        def column(part, carry):
-            lanes = pl.ds(pl.multiple_of(part * heads * HD, heads * HD), heads * HD)
-            qkv_buf[part] = jnp.dot(
-                rows_buf[slot], weight_buf[:, lanes], preferred_element_type=jnp.float32
-            ).astype(jnp.bfloat16)
-            return carry
-
-        lax.fori_loop(0, 3, column, 0)
+        qkv_buf[...] = jnp.dot(
+            rows_buf[slot], weight_buf[...], preferred_element_type=jnp.float32
+        ).astype(jnp.bfloat16)
         for which in range(2):
             rows = slice(which * group, (which + 1) * group)
             for head in range(heads):
                 lanes = slice(head * HD, (head + 1) * HD)
-                context = attend(
-                    qkv_buf[0, rows, lanes], qkv_buf[1, rows, lanes], qkv_buf[2, rows, lanes], same
-                )
+                context = attend(*[
+                    qkv_buf[rows, part * width + head * HD:part * width + (head + 1) * HD]
+                    for part in range(3)
+                ], same)
                 for way in range(ways):
                     outs[way][step * 2 + which, :, lanes] = context[
                         way * piece_rows:(way + 1) * piece_rows
@@ -329,37 +320,38 @@
     lax.fori_loop(0, steps, body, 0)
 
 
-def project(where, pieces, weight, near, far, group, ways, share, earlier):
+def project(where, pieces, weight, came, other, ways, share, earlier):
     groups = len(pieces)
     steps = groups // 2
-    piece_rows, model = pieces[0][0].shape
-    width = near[0].shape[1] // 3
-    flat = [piece for group in pieces for piece in group]
-    rows = piece_rows * ways * groups
-    out = (groups, piece_rows, width)
-    return pl.pallas_call(
-        functools.partial(project_kernel, steps, ways, share, piece_rows, group),
+    rows, model = pieces[0].shape
+    block = weight.shape[1]
+    places = [(way, first) for way, first, _ in came]
+    came = [array for _, _, array in came]
+    width = came[0].shape[1] // 3
+    out = (groups, rows // ways, width)
+    return pl.pallas_call(
+        functools.partial(project_kernel, steps, ways, share, places, block, other),
         grid_spec=pltpu.PrefetchScalarGridSpec(
             num_scalar_prefetch=1,
             grid=(1,),
-            in_specs=[pl.BlockSpec(memory_space=pl.ANY)] * (len(flat) + 2 * ways - 1 + len(earlier)),
+            in_specs=[pl.BlockSpec(memory_space=pl.ANY)] * (groups + 1 + len(came) + len(earlier)),
             out_specs=[pl.BlockSpec(out, lambda n, w: (0, 0, 0))] * ways,
             scratch_shapes=[
-                pltpu.VMEM((2, 2 * ways * piece_rows, model), jnp.bfloat16),
+                pltpu.VMEM((2, 2 * rows, model), jnp.bfloat16),
                 pltpu.VMEM((model, 3 * width), jnp.bfloat16),
-                pltpu.VMEM((3, 2 * ways * piece_rows, width), jnp.bfloat16),
-                pltpu.SemaphoreType.DMA((2, 2 * ways)),
-                pltpu.SemaphoreType.DMA((2 * ways + 1,)),
+                pltpu.VMEM((2 * rows, 3 * width), jnp.bfloat16),
+                pltpu.SemaphoreType.DMA((2, 2)),
+                pltpu.SemaphoreType.DMA((len(came) + 3,)),
             ],
         ),
         out_shape=[jax.ShapeDtypeStruct(out, jnp.bfloat16)] * ways,
-        compiler_params=pltpu.CompilerParams(vmem_limit_bytes=48 * MIB),
+        compiler_params=pltpu.CompilerParams(vmem_limit_bytes=52 * MIB),
         cost_estimate=pl.CostEstimate(
-            flops=6 * rows * model * width,
-            bytes_accessed=2 * rows * model + 6 * model * width,
-            transcendentals=rows * ways * piece_rows,
-        ),
-    )(where, *flat, weight, *near, *far, *earlier)
+            flops=6 * rows * groups * model * width,
+            bytes_accessed=2 * rows * groups * model + 6 * model * width,
+            transcendentals=rows * rows * groups * width // HD,
+        ),
+    )(where, *pieces, weight, *came, *earlier)
 
 
 def assemble_kernel(clips, sources, ways, groups, share, where, *refs):
@@ -375,7 +367,9 @@
                     ((side * 2 + core) * ways + origin) * share, share
                 )
                 for group in range(groups):
-                    out_ref[0, clip, pl.ds(row, share), group * width:(group + 1) * width] = refs[
+                    part_at = where[3] if group == 0 else 1 - where[3]
+                    lanes = pl.ds(pl.multiple_of(part_at * width, width), width)
+                    out_ref[0, clip, pl.ds(row, share), lanes] = refs[
                         (clip * groups + group) * ways + way
                     ][source]
 
@@ -422,31 +416,50 @@
         half_ref[:, part * width:(part + 1) * width] = weight_ref[part]
 
 
-def columns_of(where, weight, group, groups, earlier):
+def columns_of(where, weight):
     _, block, width = weight.shape
-    width = width // groups
-    steps = 2
-    rows = block // (2 * steps)
+    width = width // 2
+    rows = block // 4
     return pl.pallas_call(
         columns_kernel,
         grid_spec=pltpu.PrefetchScalarGridSpec(
             num_scalar_prefetch=1,
-            grid=(steps,),
-            in_specs=[pl.BlockSpec((3, rows, width), lambda n, w: (0, n + steps * w[3], group))]
-            + [pl.BlockSpec(memory_space=pl.ANY)] * len(earlier),
+            grid=(4,),
+            in_specs=[pl.BlockSpec((3, rows, width), lambda n, w: (0, n, w[3]))],
             out_specs=pl.BlockSpec((rows, 3 * width), lambda n, w: (n, 0)),
         ),
-        out_shape=jax.ShapeDtypeStruct((block // 2, 3 * width), jnp.bfloat16),
+        out_shape=jax.ShapeDtypeStruct((block, 3 * width), jnp.bfloat16),
         compiler_params=pltpu.CompilerParams(vmem_limit_bytes=32 * MIB),
         cost_estimate=pl.CostEstimate(flops=0, bytes_accessed=0, transcendentals=0),
-    )(where, weight, *earlier)
+    )(where, weight)
+
+
+def join_kernel(ways, *refs):
+    out_ref = refs[-1]
+    rows = refs[0].shape[0]
+    for way in range(ways):
+        out_ref[way * rows:(way + 1) * rows] = refs[way][...]
+
+
+def join(arrays, tile, *earlier):
+    ways = len(arrays)
+    rows, width = arrays[0].shape
+    return pl.pallas_call(
+        functools.partial(join_kernel, ways),
+        grid=(width // tile,),
+        in_specs=[pl.BlockSpec((rows, tile), lambda n: (0, n))] * ways
+        + [pl.BlockSpec(memory_space=pl.ANY)] * len(earlier),
+        out_specs=pl.BlockSpec((ways * rows, tile), lambda n: (0, n)),
+        out_shape=jax.ShapeDtypeStruct((ways * rows, width), arrays[0].dtype),
+        compiler_params=pltpu.CompilerParams(vmem_limit_bytes=32 * MIB),
+        cost_estimate=pl.CostEstimate(flops=0, bytes_accessed=0, transcendentals=0),
+    )(*arrays, *earlier)
 
 
 def per_device(ways, resid, spatial_q, spatial_k, spatial_v, out_weight, norm_gain, qkv_weight):
     frames, clips, rows, model = resid.shape
     patches, width = spatial_q.shape[2:]
     share = rows // ways
-    groups = 3
     tile = 1024
 
     plane, home, place = lax.axis_index("clip"), lax.axis_index("tm"), lax.axis_index("tensor")
@@ -472,75 +485,67 @@
 
     weight = qkv_weight.transpose(1, 0, 2)
     gain = norm_gain.reshape(1, model)
-    near = [[] for _ in range(groups)]
-    far = [[] for _ in range(groups)]
-
-    def pass_on(group, *earlier):
-        (came,) = after([near[group][-1]], *earlier)
-        near[group][-1] = came
-        far[group].append(other_plane(came))
-        if len(near[group]) < ways - 1:
-            near[group].append(along(came, 1))
-        return came
+    near, far = [], []
 
     other_weight = other_core(out_weight)
-    start = [columns_of(where, weight, 0, groups, [])]
-    near[0].append(along(start[0], 1))
-    keep, send = spatial(where, spatial_q, spatial_k, spatial_v, 0, rows, [start[0]])
+    start = columns_of(where, weight)
+    near.append(along(start, 1))
+    keep, send = spatial(where, spatial_q, spatial_k, spatial_v, 0, rows, [start])
     attended = [(keep, other_core(send))]
-    start.append(columns_of(where, weight, 1, groups, [send]))
-    near[1].append(along(start[1], 1))
-    first = branch_for_other(where, *attended[0], out_weight, other_weight, tile, [start[1]])
+    first = branch_for_other(where, *attended[0], out_weight, other_weight, tile, [])
     branches = [other_side(first)]
-    latest = pass_on(0, first)
-    keep, send = spatial(where, spatial_q, spatial_k, spatial_v, 1, rows, [latest])
+    keep, send = spatial(where, spatial_q, spatial_k, spatial_v, 1, rows, [first])
     attended.append((keep, other_core(send)))
-    start.append(columns_of(where, weight, 2, groups, [send]))
-    latest = pass_on(1, start[2])
-    second = branch_for_other(where, *attended[1], out_weight, other_weight, tile, [latest])
-    latest = pass_on(0, second)
-    latest = pass_on(1, latest, far[0][0])
-    (second,) = after([second], branches[0], latest)
+    second = branch_for_other(where, *attended[1], out_weight, other_weight, tile, [])
+    (near[0],) = after([near[0]], second)
+    far.append(other_plane(near[0]))
+    near.append(along(near[0], 1))
+    (second,) = after([second], branches[0], near[0])
     branches.append(other_side(second))
     resid_out, *normed = norm_of(0, [], second)
-    mine = [[normed[0]] + [along(normed[way], way) for way in range(1, ways)]]
-    latest = pass_on(0, normed[0], far[1][0])
-    latest = pass_on(1, latest, far[0][1])
-    resid_out, *normed = norm_of(1, [resid_out], latest)
-    mine.append([normed[0]] + [along(normed[way], way) for way in range(1, ways)])
-    mine[0][1:] = after(mine[0][1:], normed[0], far[1][1])
-    beside = [[other_side(piece) for piece in mine[0]]]
-    beside[0] = after(beside[0], mine[0][1], far[0][2])
-    across = [[other_core(piece) for piece in mine[0] + beside[0]]]
-
-    def project_of(clip, group, *earlier):
-        pieces = [mine[clip], beside[clip], across[clip][:ways], across[clip][ways:]]
-        return project(
-            where, pieces, weight, near[group], far[group], group, ways, share, earlier
-        )
-
-    arrived = [[None] * groups for _ in range(clips)]
-
-    def give_back(clip, group, contexts):
-        arrived[clip][group] = [contexts[0]] + [
-            along(contexts[way], ways - way) for way in range(1, ways)
-        ]
+    moved = [[normed[0]] + [along(normed[way], way) for way in range(1, ways)]]
+    (near[1],) = after([near[1]], normed[0])
+    far.append(other_plane(near[1]))
+    resid_out, *normed = norm_of(1, [resid_out], near[1], far[0])
+    moved.append([normed[0]] + [along(normed[way], way) for way in range(1, ways)])
+    mine, beside, across = [], [], [None, None]
+
+    def gather(clip, *earlier):
+        mine.append(join(moved[clip], tile, *earlier))
+        beside.append(other_side(mine[clip]))
+
+    def project_of(clip, other, *earlier):
+        pieces = [mine[clip], beside[clip], *across[clip]]
+        arrays = far if other else near
+        block = weight.shape[1]
+        came = [(1, 0, arrays[0]), (2, 0, arrays[1]), (3, 0, arrays[2]), (3, block // 2, arrays[3])]
+        return project(where, pieces, weight, came, other, ways, share, earlier)
+
+    arrived = [[], []]
+
+    def give_back(clip, contexts, *earlier):
+        leaving = after(contexts[1:], *earlier) if earlier else contexts[1:]
+        arrived[clip].append([contexts[0]] + [
+            along(leaving[way - 1], ways - way) for way in range(1, ways)
+        ])
         return contexts[0]
 
-    *mine[1][1:], travelling = after(mine[1][1:] + [start[2]], beside[0][0], far[1][2])
-    beside.append([other_side(piece) for piece in mine[1]])
-    near[2].append(along(travelling, 1))
-    latest = give_back(0, 0, project_of(0, 0, travelling))
-    latest = pass_on(2, latest)
-    latest = give_back(0, 1, project_of(0, 1, latest))
-    latest = pass_on(2, latest)
-    beside[1] = after(beside[1], latest)
-    across.append([other_core(piece) for piece in mine[1] + beside[1]])
-    latest = pass_on(2, beside[1][0], far[2][0])
-    latest = give_back(1, 0, project_of(1, 0, latest))
-    latest = give_back(1, 1, project_of(1, 1, latest))
-    latest = give_back(0, 2, project_of(0, 2, latest))
-    latest = give_back(1, 2, project_of(1, 2, latest))
+    gather(0, normed[0])
+    gather(1, beside[0])
+    half = weight.shape[1] // 2
+    mine[0], beside[0], near[1] = after([mine[0], beside[0], near[1]], mine[1], far[1])
+    near.append(along(near[1][:half], 1))
+    near.append(along(near[1][half:], 1))
+    across[0] = [other_core(mine[0]), other_core(beside[0])]
+    (near[2],) = after([near[2]], *across[0])
+    far.append(other_plane(near[2]))
+    mine[1], beside[1], near[3] = after([mine[1], beside[1], near[3]], near[2])
+    across[1] = [other_core(mine[1]), other_core(beside[1])]
+    far.append(other_plane(near[3]))
+    latest = give_back(0, project_of(0, False, near[3]))
+    latest = give_back(1, project_of(1, False, latest), *arrived[0][0])
+    latest = give_back(0, project_of(0, True, latest), *arrived[1][0])
+    latest = give_back(1, project_of(1, True, latest), *arrived[0][1])
     ordered = [
         [[got[0]] + [got[ways - way] for way in range(1, ways)] for got in by_group]
         for by_group in arrived

time: 601 us -> 582 us (0.968); the launches traced: 600 us -> 572 us
  starting transfers between devices: 104 us -> 57.5 us
  waiting for transfers between devices: 272 us -> 281 us
  local copies, waits for them, and re-layouts: 39.9 us -> 47.4 us
    ppermute x33 -> x22, waiting for transfers between devices: 149 us -> 240 us  [along(): lax.ppermute(array, 'tm', [(n, (n + way) % ways) for n in range(ways)])]
    ppermute x9 -> x4, waiting for transfers between devices: 70 us -> 9.67 us  [other_plane(): return lax.ppermute(array, 'clip', [(0, 1), (1, 0)])]
    ppermute x33 -> x22, starting transfers between devices: 79.3 us -> 44.7 us  [along(): lax.ppermute(array, 'tm', [(n, (n + way) % ways) for n in range(ways)])]
    ppermute x10 -> x4, waiting for transfers between devices: 46.7 us -> 26.8 us  [other_side(): return lax.ppermute(array, 'tensor', [(0, 2), (2, 0), (1, 3), (3, 1)])]
    ppermute x10 -> x4, starting transfers between devices: 12 us -> 5.93 us  [other_side(): return lax.ppermute(array, 'tensor', [(0, 2), (2, 0), (1, 3), (3, 1)])]
    unnamed x122 -> x132, local copies, waits for them, and re-layouts: 39.9 us -> 43.9 us
  transfers between devices with their start and end apart: 71 -> 37, of which waited for: 27 -> 14; matrix products, arithmetic and copies ran while one was open for 0% -> 1% of each run, Pallas kernels for 28% -> 32%
where the time goes in v3:
time: 582 us; the launch traced here: 572 us
  waiting for transfers between devices  281 us (48%)
  Pallas kernels  184 us (32%)
  starting transfers between devices  57.5 us (10%)
  local copies, waits for them, and re-layouts  47.4 us (8%)
    ppermute x22, waiting for transfers between devices, along(): lax.ppermute(array, 'tm', [(n, (n + way) % ways) for n in range(ways)])  240 us
    pallas_call x4, Pallas kernels, project(): pl.pallas_call(functools.partial(project_kernel, steps, ways, share, plac...  112 us
    ppermute x22, starting transfers between devices, along(): lax.ppermute(array, 'tm', [(n, (n + way) % ways) for n in range(ways)])  44.7 us
    unnamed x132, local copies, waits for them, and re-layouts  43.9 us
    pallas_call x2, Pallas kernels, norm(): pl.pallas_call(functools.partial(norm_kernel, tiles, tile, ways), grid_sp...  30.7 us
    ppermute x4, waiting for transfers between devices, other_side(): return lax.ppermute(array, 'tensor', [(0, 2), (2, 0), (1, 3), (3, 1)])  26.8 us
    pallas_call x2, Pallas kernels, branch_for_other(): pl.pallas_call(send_kernel, grid_spec=pltpu.PrefetchScalarGridSpec(num_sc...  20.2 us
    pallas_call x2, Pallas kernels, spatial(): pl.pallas_call(functools.partial(spatial_kernel, heads, sides, rows), gri...  12.1 us
  transfers between devices with their start and end apart: 37, of which 14 were waited for; matrix products, arithmetic and copies ran while one was open for 1% of the time, Pallas kernels for 32%

profile of v3, /device:TPU:0, one launch (start us, length us, event | category | flops | bytes accessed | tf_op | source)
XLA Modules:
  0.0 571.6 jit_solution(8920384614136488839)
XLA Ops:
  1.2 3.0 copy-done.13
  4.2 1.3 shard_map.86.refs_0_
  5.6 2.7 collective-permute-start.4
  8.2 1.9 copy-done.6
  10.1 1.9 copy-done.8
  12.0 1.9 copy-done.10
  13.9 6.1 %shard_map.87 = (bf16[4,2,64,768]{3,2,1,0:T(8,128)(2,1)S(1)}, bf16[4,2,64,768]{3,2,1,0:T(8,128)(2,1)S(1)}) custom-call(s32[4]{0:T(128)S(1)} %pad_add_fusion.where, bf16[4,2,256,768]{3,2,1,0:T(8,128)(2,1)S(1)} %copy-done.6, bf16[4,2,256,768]{3,2,1,0:T(8,128)(2,1)S(1)} %copy-done.8, bf16[4,2,256,768]{3,2,1,0:T(8,128)(2,1)S(1)} %copy-done.10, ...), custom_call_target="tpu_custom_call" | custom-call | tf_op jit(solution)/shard_map/pallas_call | solution.py:123
  20.3 2.1 collective-permute-done.came_ref
  22.4 10.8 %shard_map.88.refs_0_ = bf16[256,6144]{1,0:T(8,128)(2,1)} custom-call(s32[4]{0:T(128)S(1)} %pad_add_fusion.where, bf16[4,2,64,768]{3,2,1,0:T(8,128)(2,1)S(1)} %get-tuple-element.47.keep_ref, bf16[4,2,64,768]{3,2,1,0:T(8,128)(2,1)S(1)} %collective-permute-done.came_ref, bf16[768,6144]{1,0:T(8,128)(2,1)S(1)} %bitcast.7, ...), custom_call_target="tpu_custom_call" | custom-call | tf_op jit(solution)/shard_map/pallas_call | solution.py:167
  33.2 1.5 collective-permute-start.3
  34.8 1.9 copy-done.9
  36.6 6.1 %shard_map.89 = (bf16[4,2,64,768]{3,2,1,0:T(8,128)(2,1)S(1)}, bf16[4,2,64,768]{3,2,1,0:T(8,128)(2,1)S(1)}) custom-call(s32[4]{0:T(128)S(1)} %pad_add_fusion.where, bf16[4,2,256,768]{3,2,1,0:T(8,128)(2,1)S(1)} %copy-done.7, bf16[4,2,256,768]{3,2,1,0:T(8,128)(2,1)S(1)} %copy-done.9, bf16[4,2,256,768]{3,2,1,0:T(8,128)(2,1)S(1)} %copy-done.10, ...), custom_call_target="tpu_custom_call" | custom-call | tf_op jit(solution)/shard_map/pallas_call | solution.py:123
  42.8 2.3 collective-permute-done.2.came_ref
  45.1 9.4 %shard_map.90.refs_1_.refs_0_ = bf16[256,6144]{1,0:T(8,128)(2,1)S(1)} custom-call(s32[4]{0:T(128)S(1)} %pad_add_fusion.where, bf16[4,2,64,768]{3,2,1,0:T(8,128)(2,1)S(1)} %get-tuple-element.49.keep_ref, bf16[4,2,64,768]{3,2,1,0:T(8,128)(2,1)S(1)} %collective-permute-done.2.came_ref, bf16[768,6144]{1,0:T(8,128)(2,1)S(1)} %bitcast.7, ...), custom_call_target="tpu_custom_call" | custom-call | tf_op jit(solution)/shard_map/pallas_call | solution.py:167
  54.5 1.7 copy-done.2
  56.2 31.2 %collective-permute-done.4.refs_0_ = bf16[1536,1152]{1,0:T(8,128)(2,1)S(1)} collective-permute-done((bf16[1536,1152]{1,0:T(8,128)(2,1)S(1)}, bf16[1536,1152]{1,0:T(8,128)(2,1)S(1)}, u32[]{:S(2)}, u32[]{:S(2)}) %collective-permute-start.4) | collective-permute-done | bytes 3538976 | tf_op jit(solution)/shard_map/ppermute | solution.py:478
  87.4 1.8 copy-done.59
  89.2 1.5 collective-permute-start.7
  90.7 13.0 %collective-permute-done.3.refs_1_.branch_ref = bf16[256,6144]{1,0:T(8,128)(2,1)} collective-permute-done((bf16[256,6144]{1,0:T(8,128)(2,1)}, bf16[256,6144]{1,0:T(8,128)(2,1)}, u32[]{:S(2)}, u32[]{:S(2)}) %collective-permute-start.3) | collective-permute-done | bytes 3145760 | tf_op jit(solution)/shard_map/ppermute | solution.py:472
  103.7 1.6 collective-permute-start.5
  105.3 1.9 copy-done.3
  107.2 1.1 copy-done.19
  108.4 1.1 copy-done.21
  110.2 15.8 %shard_map.93 = (bf16[4,2,64,6144]{3,2,1,0:T(8,128)(2,1)}, bf16[64,6144]{1,0:T(8,128)(2,1)S(1)}, bf16[64,6144]{1,0:T(8,128)(2,1)}, bf16[64,6144]{1,0:T(8,128)(2,1)}, bf16[64,6144]{1,0:T(8,128)(2,1)}) custom-call(s32[4]{0:T(128)S(1)} %pad_add_fusion.where, bf16[4,2,64,768]{3,2,1,0:T(8,128)(2,1)S(1)} %copy-done.19, bf16[4,2,64,768]{3,2,1,0:T(8,128)(2,1)S(1)} %copy-done.21, ...), custom_call_target="tpu_custom_call" | custom-call | tf_op jit(solution)/shard_map/pallas_call | solution.py:227
  126.9 2.9 collective-permute-start.10
  129.9 40.8 %collective-permute-done.6.refs_0_ = bf16[1536,1152]{1,0:T(8,128)(2,1)S(1)} collective-permute-done((bf16[1536,1152]{1,0:T(8,128)(2,1)}, bf16[1536,1152]{1,0:T(8,128)(2,1)S(1)}, u32[]{:S(2)}, u32[]{:S(2)}) %collective-permute-start.6) | collective-permute-done | bytes 3538976 | tf_op jit(solution)/shard_map/ppermute | solution.py:478
  170.7 15.6 %collective-permute-start.9 = (bf16[64,6144]{1,0:T(8,128)(2,1)}, bf16[64,6144]{1,0:T(8,128)(2,1)}, u32[]{:S(2)}, u32[]{:S(2)}) collective-permute-start(bf16[64,6144]{1,0:T(8,128)(2,1)} %get-tuple-element.55), channel_id=1, source_target_pairs={{0,8},{4,12},{8,0},{12,4},{1,9},{5,13},{9,1},{13,5},{2,10},{6,14},... | collective-permute-start | bytes 2359304 | tf_op jit(solution)/shard_map/ppermute | solution.py:478
  186.3 1.5 collective-permute-start.15
  187.8 2.0 copy-done.1
  189.8 1.1 copy-done.15
  190.9 1.1 copy-done.17
  192.8 14.9 %shard_map.95 = (bf16[4,2,64,6144]{3,2,1,0:T(8,128)(2,1)}, bf16[64,6144]{1,0:T(8,128)(2,1)S(1)}, bf16[64,6144]{1,0:T(8,128)(2,1)S(1)}, bf16[64,6144]{1,0:T(8,128)(2,1)S(1)}, bf16[64,6144]{1,0:T(8,128)(2,1)S(1)}) custom-call(s32[4]{0:T(128)S(1)} %pad_add_fusion.where, bf16[4,2,64,768]{3,2,1,0:T(8,128)(2,1)S(1)} %copy-done.15, ...), custom_call_target="tpu_custom_call", output_to_operand_aliasing={{0}: (8, {})} | custom-call | tf_op jit(solution)/shard_map/pallas_call | solution.py:227
  207.8 29.3 %collective-permute-done.9.refs_2_ = bf16[64,6144]{1,0:T(8,128)(2,1)} collective-permute-done((bf16[64,6144]{1,0:T(8,128)(2,1)}, bf16[64,6144]{1,0:T(8,128)(2,1)}, u32[]{:S(2)}, u32[]{:S(2)}) %collective-permute-start.9) | collective-permute-done | bytes 786464 | tf_op jit(solution)/shard_map/ppermute | solution.py:478
  237.1 3.6 shard_map.96.refs_0_
  240.7 1.4 collective-permute-start.11
  242.6 3.9 collective-permute-start.14
  246.5 18.0 %collective-permute-done.12.refs_1_ = bf16[64,6144]{1,0:T(8,128)(2,1)S(1)} collective-permute-done((bf16[64,6144]{1,0:T(8,128)(2,1)S(1)}, bf16[64,6144]{1,0:T(8,128)(2,1)S(1)}, u32[]{:S(2)}, u32[]{:S(2)}) %collective-permute-start.12) | collective-permute-done | bytes 786464 | tf_op jit(solution)/shard_map/ppermute | solution.py:478
  264.5 32.4 %collective-permute-done.13.refs_2_ = bf16[64,6144]{1,0:T(8,128)(2,1)S(1)} collective-permute-done((bf16[64,6144]{1,0:T(8,128)(2,1)S(1)}, bf16[64,6144]{1,0:T(8,128)(2,1)S(1)}, u32[]{:S(2)}, u32[]{:S(2)}) %collective-permute-start.13) | collective-permute-done | bytes 786464 | tf_op jit(solution)/shard_map/ppermute | solution.py:478
  296.9 13.8 %collective-permute-done.11.refs_4_.refs_1_ = bf16[256,6144]{1,0:T(8,128)(2,1)S(1)} collective-permute-done((bf16[256,6144]{1,0:T(8,128)(2,1)S(1)}, bf16[256,6144]{1,0:T(8,128)(2,1)S(1)}, u32[]{:S(2)}, u32[]{:S(2)}) %collective-permute-start.11) | collective-permute-done | bytes 3145760 | tf_op jit(solution)/shard_map/ppermute | solution.py:472
  311.5 0.9 copy-done.12
  312.4 1.7 copy-done.4
  314.7 1.4 copy-done.5
  316.0 1.4 collective-permute-start.19
  317.4 3.5 fusion
  320.9 1.9 collective-permute-start.18
  322.8 41.6 %collective-permute-done.18.refs_0_ = bf16[768,1152]{1,0:T(8,128)(2,1)} collective-permute-done((bf16[768,1152]{1,0:T(8,128)(2,1)S(1)}, bf16[768,1152]{1,0:T(8,128)(2,1)}, u32[]{:S(2)}, u32[]{:S(2)}) %collective-permute-start.18) | collective-permute-done | bytes 1769504 | tf_op jit(solution)/shard_map/ppermute | solution.py:478
  364.4 35.6 %collective-permute-done.20.refs_2_ = bf16[768,1152]{1,0:T(8,128)(2,1)} collective-permute-done((bf16[768,1152]{1,0:T(8,128)(2,1)}, bf16[768,1152]{1,0:T(8,128)(2,1)}, u32[]{:S(2)}, u32[]{:S(2)}) %collective-permute-start.20) | collective-permute-done | bytes 1769504 | tf_op jit(solution)/shard_map/ppermute | solution.py:478
  400.5 1.5 collective-permute-start.24
  402.6 28.0 %shard_map.101 = (bf16[4,64,384]{2,1,0:T(8,128)(2,1)S(1)}, bf16[4,64,384]{2,1,0:T(8,128)(2,1)S(1)}, bf16[4,64,384]{2,1,0:T(8,128)(2,1)S(1)}, bf16[4,64,384]{2,1,0:T(8,128)(2,1)S(1)}) custom-call(s32[4]{0:T(128)S(1)} %pad_add_fusion.where, bf16[256,6144]{1,0:T(8,128)(2,1)} %get-tuple-element.61.refs_0_, bf16[256,6144]{1,0:T(8,128)(2,1)} %get-tuple-element.62.refs_1_, ...), custom_call_target="tpu_custom_call" | custom-call | flops 14495514624 | bytes 26738688 | tf_op jit(solution)/shard_map/pallas_call | solution.py:332
  430.8 3.9 collective-permute-start.23
  434.7 28.0 %shard_map.102 = (bf16[4,64,384]{2,1,0:T(8,128)(2,1)S(1)}, bf16[4,64,384]{2,1,0:T(8,128)(2,1)S(1)}, bf16[4,64,384]{2,1,0:T(8,128)(2,1)S(1)}, bf16[4,64,384]{2,1,0:T(8,128)(2,1)S(1)}) custom-call(s32[4]{0:T(128)S(1)} %pad_add_fusion.where, bf16[256,6144]{1,0:T(8,128)(2,1)} %get-tuple-element.69.refs_0_, bf16[256,6144]{1,0:T(8,128)(2,1)} %get-tuple-element.70.refs_1_, ...), custom_call_target="tpu_custom_call" | custom-call | flops 14495514624 | bytes 26738688 | tf_op jit(solution)/shard_map/pallas_call | solution.py:332
  465.5 2.3 collective-permute-start.28
  467.9 1.1 collective-permute-start.29
  469.7 9.7 %collective-permute-done.25.refs_8_ = bf16[768,1152]{1,0:T(8,128)(2,1)} collective-permute-done((bf16[768,1152]{1,0:T(8,128)(2,1)}, bf16[768,1152]{1,0:T(8,128)(2,1)}, u32[]{:S(2)}, u32[]{:S(2)}) %collective-permute-start.25) | collective-permute-done | bytes 1769504 | tf_op jit(solution)/shard_map/ppermute | solution.py:475
  479.4 1.2 copy-done.62
  480.5 28.0 %shard_map.103 = (bf16[4,64,384]{2,1,0:T(8,128)(2,1)S(1)}, bf16[4,64,384]{2,1,0:T(8,128)(2,1)S(1)}, bf16[4,64,384]{2,1,0:T(8,128)(2,1)S(1)}, bf16[4,64,384]{2,1,0:T(8,128)(2,1)S(1)}) custom-call(s32[4]{0:T(128)S(1)} %pad_add_fusion.where, bf16[256,6144]{1,0:T(8,128)(2,1)} %get-tuple-element.61.refs_0_, bf16[256,6144]{1,0:T(8,128)(2,1)} %get-tuple-element.62.refs_1_, ...), custom_call_target="tpu_custom_call" | custom-call | flops 14495514624 | bytes 26738688 | tf_op jit(solution)/shard_map/pallas_call | solution.py:332
  512.3 3.9 collective-permute-start.33
  516.3 28.3 %shard_map.106 = (bf16[4,64,384]{2,1,0:T(8,128)(2,1)S(1)}, bf16[4,64,384]{2,1,0:T(8,128)(2,1)S(1)}, bf16[4,64,384]{2,1,0:T(8,128)(2,1)S(1)}, bf16[4,64,384]{2,1,0:T(8,128)(2,1)S(1)}) custom-call(s32[4]{0:T(128)S(1)} %pad_add_fusion.where, bf16[256,6144]{1,0:T(8,128)(2,1)} %get-tuple-element.69.refs_0_, bf16[256,6144]{1,0:T(8,128)(2,1)} %get-tuple-element.70.refs_1_, ...), custom_call_target="tpu_custom_call" | custom-call | flops 14495514624 | bytes 26738688 | tf_op jit(solution)/shard_map/pallas_call | solution.py:332
  548.7 1.4 collective-permute-start.35
  550.2 2.9 collective-permute-start.36
  553.1 5.0 collective-permute-done.34.refs_13_
  558.1 6.2 %collective-permute-done.35.refs_14_ = bf16[4,64,384]{2,1,0:T(8,128)(2,1)S(1)} collective-permute-done((bf16[4,64,384]{2,1,0:T(8,128)(2,1)}, bf16[4,64,384]{2,1,0:T(8,128)(2,1)S(1)}, u32[]{:S(2)}, u32[]{:S(2)}) %collective-permute-start.35) | collective-permute-done | bytes 196640 | tf_op jit(solution)/shard_map/ppermute | solution.py:478
  565.2 0.9 copy-done.43
  568.0 3.3 shard_map.108
  (168 shorter events, 20.6 us)
Async XLA Ops:
  0.6 21.7 %collective-permute-start.1 = (bf16[768,6144]{1,0:T(8,128)(2,1)}, bf16[768,6144]{1,0:T(8,128)(2,1)}, u32[]{:S(2)}, u32[]{:S(2)}) collective-permute-start(bf16[768,6144]{1,0:T(8,128)(2,1)} %own_ref.7), channel_id=1, source_target_pairs={{0,1},{1,0},{2,3},{3,2},{4,5},{5,4},{6,7},{7,6},{8,9},{9,8},{10,11... | collective-permute-start | bytes 28311560 | tf_op jit(solution)/shard_map/ppermute | solution.py:469
  1.2 3.0 copy-start.13
  4.2 18.1 %slice-start = ((s8[9437184]{0:T(1024)(128)(4,1)}), s8[4194304]{0:T(1024)(128)(4,1)S(1)}, s32[]{:S(2)}) async-start(s8[9437184]{0:T(1024)(128)(4,1)} %bitcast.6), calls=%async_computation | async-start | bytes 8388608
  4.2 18.1 %slice-start.1 = ((s8[9437184]{0:T(1024)(128)(4,1)}), s8[4194304]{0:T(1024)(128)(4,1)S(1)}, s32[]{:S(2)}) async-start(s8[9437184]{0:T(1024)(128)(4,1)} %bitcast.6), calls=%async_computation.1 | async-start | bytes 8388608
  5.6 16.8 %slice-start.2 = ((s8[9437184]{0:T(1024)(128)(4,1)}), s8[1048576]{0:T(1024)(128)(4,1)S(1)}, s32[]{:S(2)}) async-start(s8[9437184]{0:T(1024)(128)(4,1)} %bitcast.6), calls=%async_computation.2 | async-start | bytes 2097152
  5.6 81.9 %collective-permute-start.4 = (bf16[1536,1152]{1,0:T(8,128)(2,1)S(1)}, bf16[1536,1152]{1,0:T(8,128)(2,1)S(1)}, u32[]{:S(2)}, u32[]{:S(2)}) collective-permute-start(bf16[1536,1152]{1,0:T(8,128)(2,1)S(1)} %shard_map.86.refs_0_), channel_id=1, source_target_pairs={{0,4},{4,8},{8,12},{12,0},{1,5},{5,9},{9,13},{13,1},{2,6},{6,10},{... | collective-permute-start | bytes 10616840 | tf_op jit(solution)/shard_map/ppermute | solution.py:478
  20.0 13.2 %copy-start.18 = (bf16[4,2,64,768]{3,2,1,0:T(8,128)(2,1)}, bf16[4,2,64,768]{3,2,1,0:T(8,128)(2,1)S(1)}, u32[]{:S(2)}) copy-start(bf16[4,2,64,768]{3,2,1,0:T(8,128)(2,1)S(1)} %get-tuple-element.47.keep_ref) | copy-start | bytes 2359300
  20.0 2.4 collective-permute-start
  22.3 10.9 %copy-start.20 = (bf16[4,2,64,768]{3,2,1,0:T(8,128)(2,1)}, bf16[4,2,64,768]{3,2,1,0:T(8,128)(2,1)S(1)}, u32[]{:S(2)}) copy-start(bf16[4,2,64,768]{3,2,1,0:T(8,128)(2,1)S(1)} %collective-permute-done.came_ref) | copy-start | bytes 2359300
  22.4 12.4 %copy-start.7 = (bf16[4,2,256,768]{3,2,1,0:T(8,128)(2,1)S(1)}, bf16[4,2,256,768]{3,2,1,0:T(8,128)(2,1)}, u32[]{:S(2)}) copy-start(bf16[4,2,256,768]{3,2,1,0:T(8,128)(2,1)} %q_ref.3) | copy-start | bytes 9437188
  33.2 70.5 %collective-permute-start.3 = (bf16[256,6144]{1,0:T(8,128)(2,1)}, bf16[256,6144]{1,0:T(8,128)(2,1)}, u32[]{:S(2)}, u32[]{:S(2)}) collective-permute-start(bf16[256,6144]{1,0:T(8,128)(2,1)} %shard_map.88.refs_0_), channel_id=1, source_target_pairs={{0,2},{2,0},{1,3},{3,1},{4,6},{6,4},{5,7},{7,5},{8,10},{10,8},{9,1... | collective-permute-start | bytes 9437192 | tf_op jit(solution)/shard_map/ppermute | solution.py:472
  34.8 1.9 copy-start.9
  42.7 11.8 %copy-start.14 = (bf16[4,2,64,768]{3,2,1,0:T(8,128)(2,1)}, bf16[4,2,64,768]{3,2,1,0:T(8,128)(2,1)S(1)}, u32[]{:S(2)}) copy-start(bf16[4,2,64,768]{3,2,1,0:T(8,128)(2,1)S(1)} %get-tuple-element.49.keep_ref) | copy-start | bytes 2359300
  42.7 2.4 collective-permute-start.2
  45.1 9.4 %copy-start.16 = (bf16[4,2,64,768]{3,2,1,0:T(8,128)(2,1)}, bf16[4,2,64,768]{3,2,1,0:T(8,128)(2,1)S(1)}, u32[]{:S(2)}) copy-start(bf16[4,2,64,768]{3,2,1,0:T(8,128)(2,1)S(1)} %collective-permute-done.2.came_ref) | copy-start | bytes 2359300
  89.2 81.5 %collective-permute-start.6 = (bf16[1536,1152]{1,0:T(8,128)(2,1)}, bf16[1536,1152]{1,0:T(8,128)(2,1)S(1)}, u32[]{:S(2)}, u32[]{:S(2)}) collective-permute-start(bf16[1536,1152]{1,0:T(8,128)(2,1)} %shard_map.91.refs_2_.refs_5_), channel_id=1, source_target_pairs={{0,4},{4,8},{8,12},{12,0},{1,5},{5,9},{9,13},{13,1},{2,6},{6,10},{... | collective-permute-start | bytes 10616840 | tf_op jit(solution)/shard_map/ppermute | solution.py:478
  89.2 97.0 %collective-permute-start.7 = (bf16[1536,1152]{1,0:T(8,128)(2,1)}, bf16[1536,1152]{1,0:T(8,128)(2,1)}, u32[]{:S(2)}, u32[]{:S(2)}) collective-permute-start(bf16[1536,1152]{1,0:T(8,128)(2,1)} %shard_map.91.refs_2_.refs_5_), channel_id=1, source_target_pairs={{0,16},{16,0},{1,17},{17,1},{2,18},{18,2},{3,19},{19,3},{4,20},{20... | collective-permute-start | bytes 10616840 | tf_op jit(solution)/shard_map/ppermute | solution.py:475
  103.7 84.0 %collective-permute-start.5 = (bf16[256,6144]{1,0:T(8,128)(2,1)}, bf16[256,6144]{1,0:T(8,128)(2,1)}, u32[]{:S(2)}, u32[]{:S(2)}) collective-permute-start(bf16[256,6144]{1,0:T(8,128)(2,1)} %shard_map.92.rest_0_), channel_id=1, source_target_pairs={{0,2},{2,0},{1,3},{3,1},{4,6},{6,4},{5,7},{7,5},{8,10},{10,8},{9,1... | collective-permute-start | bytes 9437192 | tf_op jit(solution)/shard_map/ppermute | solution.py:472
  105.3 1.9 copy-start.3
  126.9 80.8 %collective-permute-start.10 = (bf16[64,6144]{1,0:T(8,128)(2,1)}, bf16[64,6144]{1,0:T(8,128)(2,1)}, u32[]{:S(2)}, u32[]{:S(2)}) collective-permute-start(bf16[64,6144]{1,0:T(8,128)(2,1)} %get-tuple-element.56), channel_id=1, source_target_pairs={{0,12},{4,0},{8,4},{12,8},{1,13},{5,1},{9,5},{13,9},{2,14},{6,2},{... | collective-permute-start | bytes 2359304 | tf_op jit(solution)/shard_map/ppermute | solution.py:478
  129.9 77.9 %collective-permute-start.8 = (bf16[64,6144]{1,0:T(8,128)(2,1)}, bf16[64,6144]{1,0:T(8,128)(2,1)}, u32[]{:S(2)}, u32[]{:S(2)}) collective-permute-start(bf16[64,6144]{1,0:T(8,128)(2,1)} %get-tuple-element.54), channel_id=1, source_target_pairs={{0,4},{4,8},{8,12},{12,0},{1,5},{5,9},{9,13},{13,1},{2,6},{6,10},{... | collective-permute-start | bytes 2359304 | tf_op jit(solution)/shard_map/ppermute | solution.py:478
  170.7 15.6 %copy-start = (bf16[1536,1152]{1,0:T(8,128)(2,1)}, bf16[1536,1152]{1,0:T(8,128)(2,1)S(1)}, u32[]{:S(2)}) copy-start(bf16[1536,1152]{1,0:T(8,128)(2,1)S(1)} %collective-permute-done.6.refs_0_) | copy-start | bytes 10616836
  170.7 66.4 %collective-permute-start.9 = (bf16[64,6144]{1,0:T(8,128)(2,1)}, bf16[64,6144]{1,0:T(8,128)(2,1)}, u32[]{:S(2)}, u32[]{:S(2)}) collective-permute-start(bf16[64,6144]{1,0:T(8,128)(2,1)} %get-tuple-element.55), channel_id=1, source_target_pairs={{0,8},{4,12},{8,0},{12,4},{1,9},{5,13},{9,1},{13,5},{2,10},{6,14},... | collective-permute-start | bytes 2359304 | tf_op jit(solution)/shard_map/ppermute | solution.py:478
  186.3 127.9 %collective-permute-start.15 = (bf16[1536,1152]{1,0:T(8,128)(2,1)}, bf16[1536,1152]{1,0:T(8,128)(2,1)}, u32[]{:S(2)}, u32[]{:S(2)}) collective-permute-start(bf16[1536,1152]{1,0:T(8,128)(2,1)} %shard_map.94.rest_1_.refs_2_), channel_id=1, source_target_pairs={{0,16},{16,0},{1,17},{17,1},{2,18},{18,2},{3,19},{19,3},{4,20},{20... | collective-permute-start | bytes 10616840 | tf_op jit(solution)/shard_map/ppermute | solution.py:475
  187.8 2.0 copy-start.1
  192.8 44.3 %copy-start.23 = (bf16[64,6144]{1,0:T(8,128)(2,1)S(1)}, bf16[64,6144]{1,0:T(8,128)(2,1)}, u32[]{:S(2)}) copy-start(bf16[64,6144]{1,0:T(8,128)(2,1)} %copy-done.22) | copy-start | bytes 2359300
  240.7 56.2 %copy-start.11 = (bf16[256,6144]{1,0:T(8,128)(2,1)}, bf16[256,6144]{1,0:T(8,128)(2,1)S(1)}, u32[]{:S(2)}) copy-start(bf16[256,6144]{1,0:T(8,128)(2,1)S(1)} %shard_map.96.refs_0_) | copy-start | bytes 9437188
  240.7 70.0 %collective-permute-start.11 = (bf16[256,6144]{1,0:T(8,128)(2,1)S(1)}, bf16[256,6144]{1,0:T(8,128)(2,1)S(1)}, u32[]{:S(2)}, u32[]{:S(2)}) collective-permute-start(bf16[256,6144]{1,0:T(8,128)(2,1)S(1)} %shard_map.96.refs_0_), channel_id=1, source_target_pairs={{0,2},{2,0},{1,3},{3,1},{4,6},{6,4},{5,7},{7,5},{8,10},{10,8},{9,1... | collective-permute-start | bytes 9437192 | tf_op jit(solution)/shard_map/ppermute | solution.py:472
  242.2 22.4 %collective-permute-start.12 = (bf16[64,6144]{1,0:T(8,128)(2,1)S(1)}, bf16[64,6144]{1,0:T(8,128)(2,1)S(1)}, u32[]{:S(2)}, u32[]{:S(2)}) collective-permute-start(bf16[64,6144]{1,0:T(8,128)(2,1)S(1)} %get-tuple-element.58), channel_id=1, source_target_pairs={{0,4},{4,8},{8,12},{12,0},{1,5},{5,9},{9,13},{13,1},{2,6},{6,10},{... | collective-permute-start | bytes 2359304 | tf_op jit(solution)/shard_map/ppermute | solution.py:478
  242.2 54.8 %collective-permute-start.13 = (bf16[64,6144]{1,0:T(8,128)(2,1)S(1)}, bf16[64,6144]{1,0:T(8,128)(2,1)S(1)}, u32[]{:S(2)}, u32[]{:S(2)}) collective-permute-start(bf16[64,6144]{1,0:T(8,128)(2,1)S(1)} %get-tuple-element.59), channel_id=1, source_target_pairs={{0,8},{4,12},{8,0},{12,4},{1,9},{5,13},{9,1},{13,5},{2,10},{6,14},... | collective-permute-start | bytes 2359304 | tf_op jit(solution)/shard_map/ppermute | solution.py:478
  242.6 54.3 %collective-permute-start.14 = (bf16[64,6144]{1,0:T(8,128)(2,1)S(1)}, bf16[64,6144]{1,0:T(8,128)(2,1)S(1)}, u32[]{:S(2)}, u32[]{:S(2)}) collective-permute-start(bf16[64,6144]{1,0:T(8,128)(2,1)S(1)} %get-tuple-element.60), channel_id=1, source_target_pairs={{0,12},{4,0},{8,4},{12,8},{1,13},{5,1},{9,5},{13,9},{2,14},{6,2},{... | collective-permute-start | bytes 2359304 | tf_op jit(solution)/shard_map/ppermute | solution.py:478
  314.2 1.9 copy-start.5
  314.2 50.3 %collective-permute-start.16 = (bf16[256,6144]{1,0:T(8,128)(2,1)}, bf16[256,6144]{1,0:T(8,128)(2,1)}, u32[]{:S(2)}, u32[]{:S(2)}) collective-permute-start(bf16[256,6144]{1,0:T(8,128)(2,1)} %get-tuple-element.61.refs_0_), channel_id=1, source_target_pairs={{0,1},{1,0},{2,3},{3,2},{4,5},{5,4},{6,7},{7,6},{8,9},{9,8},{10,11... | collective-permute-start | bytes 9437192 | tf_op jit(solution)/shard_map/ppermute | solution.py:469
  314.2 50.2 %collective-permute-start.17 = (bf16[256,6144]{1,0:T(8,128)(2,1)}, bf16[256,6144]{1,0:T(8,128)(2,1)}, u32[]{:S(2)}, u32[]{:S(2)}) collective-permute-start(bf16[256,6144]{1,0:T(8,128)(2,1)} %get-tuple-element.62.refs_1_), channel_id=1, source_target_pairs={{0,1},{1,0},{2,3},{3,2},{4,5},{5,4},{6,7},{7,6},{8,9},{9,8},{10,11... | collective-permute-start | bytes 9437192 | tf_op jit(solution)/shard_map/ppermute | solution.py:469
  316.0 84.0 %collective-permute-start.19 = (bf16[256,6144]{1,0:T(8,128)(2,1)S(1)}, bf16[256,6144]{1,0:T(8,128)(2,1)}, u32[]{:S(2)}, u32[]{:S(2)}) collective-permute-start(bf16[256,6144]{1,0:T(8,128)(2,1)S(1)} %copy-done.5), channel_id=1, source_target_pairs={{0,2},{2,0},{1,3},{3,1},{4,6},{6,4},{5,7},{7,5},{8,10},{10,8},{9,1... | collective-permute-start | bytes 9437192 | tf_op jit(solution)/shard_map/ppermute | solution.py:472
  320.9 43.5 %collective-permute-start.18 = (bf16[768,1152]{1,0:T(8,128)(2,1)S(1)}, bf16[768,1152]{1,0:T(8,128)(2,1)}, u32[]{:S(2)}, u32[]{:S(2)}) collective-permute-start(bf16[768,1152]{1,0:T(8,128)(2,1)S(1)} %get-tuple-element.93), channel_id=1, source_target_pairs={{0,4},{4,8},{8,12},{12,0},{1,5},{5,9},{9,13},{13,1},{2,6},{6,10},{... | collective-permute-start | bytes 5308424 | tf_op jit(solution)/shard_map/ppermute | solution.py:478
  322.8 77.2 %collective-permute-start.20 = (bf16[768,1152]{1,0:T(8,128)(2,1)}, bf16[768,1152]{1,0:T(8,128)(2,1)}, u32[]{:S(2)}, u32[]{:S(2)}) collective-permute-start(bf16[768,1152]{1,0:T(8,128)(2,1)} %get-tuple-element.92), channel_id=1, source_target_pairs={{0,4},{4,8},{8,12},{12,0},{1,5},{5,9},{9,13},{13,1},{2,6},{6,10},{... | collective-permute-start | bytes 5308424 | tf_op jit(solution)/shard_map/ppermute | solution.py:478
  400.0 30.7 %collective-permute-start.26 = (bf16[256,6144]{1,0:T(8,128)(2,1)}, bf16[256,6144]{1,0:T(8,128)(2,1)S(1)}, u32[]{:S(2)}, u32[]{:S(2)}) collective-permute-start(bf16[256,6144]{1,0:T(8,128)(2,1)} %get-tuple-element.69.refs_0_), channel_id=1, source_target_pairs={{0,1},{1,0},{2,3},{3,2},{4,5},{5,4},{6,7},{7,6},{8,9},{9,8},{10,11... | collective-permute-start | bytes 9437192 | tf_op jit(solution)/shard_map/ppermute | solution.py:469
  400.0 30.7 %collective-permute-start.27 = (bf16[256,6144]{1,0:T(8,128)(2,1)}, bf16[256,6144]{1,0:T(8,128)(2,1)S(1)}, u32[]{:S(2)}, u32[]{:S(2)}) collective-permute-start(bf16[256,6144]{1,0:T(8,128)(2,1)} %get-tuple-element.70.refs_1_), channel_id=1, source_target_pairs={{0,1},{1,0},{2,3},{3,2},{4,5},{5,4},{6,7},{7,6},{8,9},{9,8},{10,11... | collective-permute-start | bytes 9437192 | tf_op jit(solution)/shard_map/ppermute | solution.py:469
  400.5 78.8 %collective-permute-start.24 = (bf16[768,1152]{1,0:T(8,128)(2,1)}, bf16[768,1152]{1,0:T(8,128)(2,1)S(1)}, u32[]{:S(2)}, u32[]{:S(2)}) collective-permute-start(bf16[768,1152]{1,0:T(8,128)(2,1)} %shard_map.99.refs_3_.refs_7_), channel_id=1, source_target_pairs={{0,16},{16,0},{1,17},{17,1},{2,18},{18,2},{3,19},{19,3},{4,20},{20... | collective-permute-start | bytes 5308424 | tf_op jit(solution)/shard_map/ppermute | solution.py:475
  402.0 77.3 %collective-permute-start.25 = (bf16[768,1152]{1,0:T(8,128)(2,1)}, bf16[768,1152]{1,0:T(8,128)(2,1)}, u32[]{:S(2)}, u32[]{:S(2)}) collective-permute-start(bf16[768,1152]{1,0:T(8,128)(2,1)} %get-tuple-element.64.refs_8_.refs_9_), channel_id=1, source_target_pairs={{0,16},{16,0},{1,17},{17,1},{2,18},{18,2},{3,19},{19,3},{4,20},{20... | collective-permute-start | bytes 5308424 | tf_op jit(solution)/shard_map/ppermute | solution.py:475
  430.6 32.1 %copy-start.24 = (bf16[4,64,384]{2,1,0:T(8,128)(2,1)}, bf16[4,64,384]{2,1,0:T(8,128)(2,1)S(1)}, u32[]{:S(2)}) copy-start(bf16[4,64,384]{2,1,0:T(8,128)(2,1)S(1)} %get-tuple-element.65.refs_9_.refs_3_.refs_0_) | copy-start | bytes 589828
  430.6 34.2 %collective-permute-start.21 = (bf16[4,64,384]{2,1,0:T(8,128)(2,1)S(1)}, bf16[4,64,384]{2,1,0:T(8,128)(2,1)S(1)}, u32[]{:S(2)}, u32[]{:S(2)}) collective-permute-start(bf16[4,64,384]{2,1,0:T(8,128)(2,1)S(1)} %get-tuple-element.66), channel_id=1, source_target_pairs={{0,4},{4,8},{8,12},{12,0},{1,5},{5,9},{9,13},{13,1},{2,6},{6,10},{... | collective-permute-start | bytes 589832 | tf_op jit(solution)/shard_map/ppermute | solution.py:478
  430.7 4.0 copy-start.60
  430.7 34.0 %collective-permute-start.22 = (bf16[4,64,384]{2,1,0:T(8,128)(2,1)S(1)}, bf16[4,64,384]{2,1,0:T(8,128)(2,1)S(1)}, u32[]{:S(2)}, u32[]{:S(2)}) collective-permute-start(bf16[4,64,384]{2,1,0:T(8,128)(2,1)S(1)} %get-tuple-element.67), channel_id=1, source_target_pairs={{0,8},{4,12},{8,0},{12,4},{1,9},{5,13},{9,1},{13,5},{2,10},{6,14},... | collective-permute-start | bytes 589832 | tf_op jit(solution)/shard_map/ppermute | solution.py:478
  430.8 4.0 copy-start.61
  430.8 34.0 %collective-permute-start.23 = (bf16[4,64,384]{2,1,0:T(8,128)(2,1)S(1)}, bf16[4,64,384]{2,1,0:T(8,128)(2,1)S(1)}, u32[]{:S(2)}, u32[]{:S(2)}) collective-permute-start(bf16[4,64,384]{2,1,0:T(8,128)(2,1)S(1)} %get-tuple-element.68), channel_id=1, source_target_pairs={{0,12},{4,0},{8,4},{12,8},{1,13},{5,1},{9,5},{13,9},{2,14},{6,2},{... | collective-permute-start | bytes 589832 | tf_op jit(solution)/shard_map/ppermute | solution.py:478
  465.5 45.8 %collective-permute-start.28 = (bf16[4,64,384]{2,1,0:T(8,128)(2,1)}, bf16[4,64,384]{2,1,0:T(8,128)(2,1)S(1)}, u32[]{:S(2)}, u32[]{:S(2)}) collective-permute-start(bf16[4,64,384]{2,1,0:T(8,128)(2,1)} %get-tuple-element.79), channel_id=1, source_target_pairs={{0,12},{4,0},{8,4},{12,8},{1,13},{5,1},{9,5},{13,9},{2,14},{6,2},{... | collective-permute-start | bytes 589832 | tf_op jit(solution)/shard_map/ppermute | solution.py:478
  467.9 43.5 %collective-permute-start.29 = (bf16[4,64,384]{2,1,0:T(8,128)(2,1)}, bf16[4,64,384]{2,1,0:T(8,128)(2,1)S(1)}, u32[]{:S(2)}, u32[]{:S(2)}) collective-permute-start(bf16[4,64,384]{2,1,0:T(8,128)(2,1)} %get-tuple-element.80), channel_id=1, source_target_pairs={{0,8},{4,12},{8,0},{12,4},{1,9},{5,13},{9,1},{13,5},{2,10},{6,14},... | collective-permute-start | bytes 589832 | tf_op jit(solution)/shard_map/ppermute | solution.py:478
  469.0 42.4 %collective-permute-start.30 = (bf16[4,64,384]{2,1,0:T(8,128)(2,1)}, bf16[4,64,384]{2,1,0:T(8,128)(2,1)S(1)}, u32[]{:S(2)}, u32[]{:S(2)}) collective-permute-start(bf16[4,64,384]{2,1,0:T(8,128)(2,1)} %get-tuple-element.81), channel_id=1, source_target_pairs={{0,4},{4,8},{8,12},{12,0},{1,5},{5,9},{9,13},{13,1},{2,6},{6,10},{... | collective-permute-start | bytes 589832 | tf_op jit(solution)/shard_map/ppermute | solution.py:478
  512.2 35.1 %collective-permute-start.31 = (bf16[4,64,384]{2,1,0:T(8,128)(2,1)}, bf16[4,64,384]{2,1,0:T(8,128)(2,1)S(1)}, u32[]{:S(2)}, u32[]{:S(2)}) collective-permute-start(bf16[4,64,384]{2,1,0:T(8,128)(2,1)} %get-tuple-element.82), channel_id=1, source_target_pairs={{0,4},{4,8},{8,12},{12,0},{1,5},{5,9},{9,13},{13,1},{2,6},{6,10},{... | collective-permute-start | bytes 589832 | tf_op jit(solution)/shard_map/ppermute | solution.py:478
  512.3 35.0 %collective-permute-start.32 = (bf16[4,64,384]{2,1,0:T(8,128)(2,1)}, bf16[4,64,384]{2,1,0:T(8,128)(2,1)S(1)}, u32[]{:S(2)}, u32[]{:S(2)}) collective-permute-start(bf16[4,64,384]{2,1,0:T(8,128)(2,1)} %get-tuple-element.83), channel_id=1, source_target_pairs={{0,8},{4,12},{8,0},{12,4},{1,9},{5,13},{9,1},{13,5},{2,10},{6,14},... | collective-permute-start | bytes 589832 | tf_op jit(solution)/shard_map/ppermute | solution.py:478
  512.3 35.0 %collective-permute-start.33 = (bf16[4,64,384]{2,1,0:T(8,128)(2,1)}, bf16[4,64,384]{2,1,0:T(8,128)(2,1)S(1)}, u32[]{:S(2)}, u32[]{:S(2)}) collective-permute-start(bf16[4,64,384]{2,1,0:T(8,128)(2,1)} %get-tuple-element.84), channel_id=1, source_target_pairs={{0,12},{4,0},{8,4},{12,8},{1,13},{5,1},{9,5},{13,9},{2,14},{6,2},{... | collective-permute-start | bytes 589832 | tf_op jit(solution)/shard_map/ppermute | solution.py:478
  516.3 48.0 %copy-start.25 = (bf16[4,64,384]{2,1,0:T(8,128)(2,1)S(1)}, bf16[4,64,384]{2,1,0:T(8,128)(2,1)}, u32[]{:S(2)}) copy-start(bf16[4,64,384]{2,1,0:T(8,128)(2,1)} %copy-done.24) | copy-start | bytes 589828
  516.3 48.0 %copy-start.27 = (bf16[4,64,384]{2,1,0:T(8,128)(2,1)S(1)}, bf16[4,64,384]{2,1,0:T(8,128)(2,1)}, u32[]{:S(2)}) copy-start(bf16[4,64,384]{2,1,0:T(8,128)(2,1)} %copy-done.26) | copy-start | bytes 589828
  516.3 48.0 %copy-start.29 = (bf16[4,64,384]{2,1,0:T(8,128)(2,1)S(1)}, bf16[4,64,384]{2,1,0:T(8,128)(2,1)}, u32[]{:S(2)}) copy-start(bf16[4,64,384]{2,1,0:T(8,128)(2,1)} %copy-done.28) | copy-start | bytes 589828
  516.3 48.0 %copy-start.31 = (bf16[4,64,384]{2,1,0:T(8,128)(2,1)S(1)}, bf16[4,64,384]{2,1,0:T(8,128)(2,1)}, u32[]{:S(2)}) copy-start(bf16[4,64,384]{2,1,0:T(8,128)(2,1)} %copy-done.30) | copy-start | bytes 589828
  516.3 48.0 %copy-start.33 = (bf16[4,64,384]{2,1,0:T(8,128)(2,1)S(1)}, bf16[4,64,384]{2,1,0:T(8,128)(2,1)}, u32[]{:S(2)}) copy-start(bf16[4,64,384]{2,1,0:T(8,128)(2,1)} %copy-done.32) | copy-start | bytes 589828
  516.3 48.0 %copy-start.35 = (bf16[4,64,384]{2,1,0:T(8,128)(2,1)S(1)}, bf16[4,64,384]{2,1,0:T(8,128)(2,1)}, u32[]{:S(2)}) copy-start(bf16[4,64,384]{2,1,0:T(8,128)(2,1)} %copy-done.34) | copy-start | bytes 589828
  516.3 48.0 %copy-start.37 = (bf16[4,64,384]{2,1,0:T(8,128)(2,1)S(1)}, bf16[4,64,384]{2,1,0:T(8,128)(2,1)}, u32[]{:S(2)}) copy-start(bf16[4,64,384]{2,1,0:T(8,128)(2,1)} %copy-done.36) | copy-start | bytes 589828
  516.3 48.0 %copy-start.39 = (bf16[4,64,384]{2,1,0:T(8,128)(2,1)S(1)}, bf16[4,64,384]{2,1,0:T(8,128)(2,1)}, u32[]{:S(2)}) copy-start(bf16[4,64,384]{2,1,0:T(8,128)(2,1)} %copy-done.38) | copy-start | bytes 589828
  548.1 9.9 %collective-permute-start.34 = (bf16[4,64,384]{2,1,0:T(8,128)(2,1)}, bf16[4,64,384]{2,1,0:T(8,128)(2,1)S(1)}, u32[]{:S(2)}, u32[]{:S(2)}) collective-permute-start(bf16[4,64,384]{2,1,0:T(8,128)(2,1)} %get-tuple-element.89), channel_id=1, source_target_pairs={{0,4},{4,8},{8,12},{12,0},{1,5},{5,9},{9,13},{13,1},{2,6},{6,10},{... | collective-permute-start | bytes 589832 | tf_op jit(solution)/shard_map/ppermute | solution.py:478
  548.7 15.5 %collective-permute-start.35 = (bf16[4,64,384]{2,1,0:T(8,128)(2,1)}, bf16[4,64,384]{2,1,0:T(8,128)(2,1)S(1)}, u32[]{:S(2)}, u32[]{:S(2)}) collective-permute-start(bf16[4,64,384]{2,1,0:T(8,128)(2,1)} %get-tuple-element.90), channel_id=1, source_target_pairs={{0,8},{4,12},{8,0},{12,4},{1,9},{5,13},{9,1},{13,5},{2,10},{6,14},... | collective-permute-start | bytes 589832 | tf_op jit(solution)/shard_map/ppermute | solution.py:478
  550.2 14.1 %collective-permute-start.36 = (bf16[4,64,384]{2,1,0:T(8,128)(2,1)}, bf16[4,64,384]{2,1,0:T(8,128)(2,1)S(1)}, u32[]{:S(2)}, u32[]{:S(2)}) collective-permute-start(bf16[4,64,384]{2,1,0:T(8,128)(2,1)} %get-tuple-element.91), channel_id=1, source_target_pairs={{0,12},{4,0},{8,4},{12,8},{1,13},{5,1},{9,5},{13,9},{2,14},{6,2},{... | collective-permute-start | bytes 589832 | tf_op jit(solution)/shard_map/ppermute | solution.py:478
  (39 other events, 38.8 us)

commit v4 on v3

--- a/solution.py
+++ b/solution.py
@@ -94,10 +94,9 @@
         scores = jnp.where(same, scores, -jnp.inf)
     top = jnp.max(scores, axis=1, keepdims=True)
     raised = jnp.exp(scores - top)
-    total = jnp.sum(raised, axis=1, keepdims=True)
-    probs = (raised * (1.0 / total)).astype(jnp.bfloat16)
-    context = jnp.dot(probs, values, preferred_element_type=jnp.float32)
-    return context.astype(jnp.bfloat16)
+    summed = jnp.concatenate([values, jnp.ones_like(values)], axis=1)
+    context = jnp.dot(raised.astype(jnp.bfloat16), summed, preferred_element_type=jnp.float32)
+    return (context[:, :HD] / context[:, HD:]).astype(jnp.bfloat16)
 
 
 def spatial_kernel(heads, sides, rows, where, q_ref, k_ref, v_ref, *refs):

time: 582 us -> 580 us (level)
  Pallas kernels: 184 us -> 175 us
  waiting for transfers between devices: 281 us -> 288 us
    ppermute x22, waiting for transfers between devices: 240 us -> 247 us  [along(): lax.ppermute(array, 'tm', [(n, (n + way) % ways) for n in range(ways)])]
  transfers between devices with their start and end apart: 37 -> 37, of which waited for: 14 -> 14; matrix products, arithmetic and copies ran while one was open for 1% -> 1% of each run, Pallas kernels for 32% -> 30%
where the time goes in v4:
time: 580 us; the launch traced here: 569 us
  waiting for transfers between devices  288 us (50%)
  Pallas kernels  175 us (30%)
  starting transfers between devices  57.4 us (10%)
  local copies, waits for them, and re-layouts  47.4 us (8%)
    ppermute x22, waiting for transfers between devices, along(): lax.ppermute(array, 'tm', [(n, (n + way) % ways) for n in range(ways)])  247 us
    pallas_call x4, Pallas kernels, project(): pl.pallas_call(functools.partial(project_kernel, steps, ways, share, plac...  108 us
    ppermute x22, starting transfers between devices, along(): lax.ppermute(array, 'tm', [(n, (n + way) % ways) for n in range(ways)])  44.6 us
    unnamed x132, local copies, waits for them, and re-layouts  43.9 us
    pallas_call x2, Pallas kernels, norm(): pl.pallas_call(functools.partial(norm_kernel, tiles, tile, ways), grid_sp...  30.7 us
    ppermute x4, waiting for transfers between devices, other_side(): return lax.ppermute(array, 'tensor', [(0, 2), (2, 0), (1, 3), (3, 1)])  24.6 us
    pallas_call x2, Pallas kernels, branch_for_other(): pl.pallas_call(send_kernel, grid_spec=pltpu.PrefetchScalarGridSpec(num_sc...  20.2 us
    ppermute x4, waiting for transfers between devices, other_plane(): return lax.ppermute(array, 'clip', [(0, 1), (1, 0)])  11.9 us
  transfers between devices with their start and end apart: 37, of which 14 were waited for; matrix products, arithmetic and copies ran while one was open for 1% of the time, Pallas kernels for 30%

profile of v4, /device:TPU:0, one launch (start us, length us, event | category | flops | bytes accessed | tf_op | source)
XLA Modules:
  0.0 569.4 jit_solution(16257509641905374865)
XLA Ops:
  1.2 3.0 copy-done.13
  4.2 1.3 shard_map.86.refs_0_
  5.6 2.7 collective-permute-start.4
  8.2 1.9 copy-done.6
  10.1 1.9 copy-done.8
  12.0 1.9 copy-done.10
  13.9 3.8 shard_map.87
  18.0 2.1 collective-permute-done.came_ref
  20.2 10.8 %shard_map.88.refs_0_ = bf16[256,6144]{1,0:T(8,128)(2,1)} custom-call(s32[4]{0:T(128)S(1)} %pad_add_fusion.where, bf16[4,2,64,768]{3,2,1,0:T(8,128)(2,1)S(1)} %get-tuple-element.47.keep_ref, bf16[4,2,64,768]{3,2,1,0:T(8,128)(2,1)S(1)} %collective-permute-done.came_ref, bf16[768,6144]{1,0:T(8,128)(2,1)S(1)} %bitcast.7, ...), custom_call_target="tpu_custom_call" | custom-call | tf_op jit(solution)/shard_map/pallas_call | solution.py:166
  31.0 1.5 collective-permute-start.3
  32.5 1.9 copy-done.9
  34.4 3.8 shard_map.89
  38.4 2.3 collective-permute-done.2.came_ref
  40.6 9.4 %shard_map.90.refs_1_.refs_0_ = bf16[256,6144]{1,0:T(8,128)(2,1)S(1)} custom-call(s32[4]{0:T(128)S(1)} %pad_add_fusion.where, bf16[4,2,64,768]{3,2,1,0:T(8,128)(2,1)S(1)} %get-tuple-element.49.keep_ref, bf16[4,2,64,768]{3,2,1,0:T(8,128)(2,1)S(1)} %collective-permute-done.2.came_ref, bf16[768,6144]{1,0:T(8,128)(2,1)S(1)} %bitcast.7, ...), custom_call_target="tpu_custom_call" | custom-call | tf_op jit(solution)/shard_map/pallas_call | solution.py:166
  50.1 1.7 copy-done.2
  51.8 35.6 %collective-permute-done.4.refs_0_ = bf16[1536,1152]{1,0:T(8,128)(2,1)S(1)} collective-permute-done((bf16[1536,1152]{1,0:T(8,128)(2,1)S(1)}, bf16[1536,1152]{1,0:T(8,128)(2,1)S(1)}, u32[]{:S(2)}, u32[]{:S(2)}) %collective-permute-start.4) | collective-permute-done | bytes 3538976 | tf_op jit(solution)/shard_map/ppermute | solution.py:477
  87.4 1.8 copy-done.59
  89.2 1.5 collective-permute-start.7
  90.7 10.8 %collective-permute-done.3.refs_1_.branch_ref = bf16[256,6144]{1,0:T(8,128)(2,1)} collective-permute-done((bf16[256,6144]{1,0:T(8,128)(2,1)}, bf16[256,6144]{1,0:T(8,128)(2,1)}, u32[]{:S(2)}, u32[]{:S(2)}) %collective-permute-start.3) | collective-permute-done | bytes 3145760 | tf_op jit(solution)/shard_map/ppermute | solution.py:471
  101.5 1.6 collective-permute-start.5
  103.1 1.9 copy-done.3
  105.0 1.1 copy-done.19
  106.2 1.1 copy-done.21
  108.0 15.8 %shard_map.93 = (bf16[4,2,64,6144]{3,2,1,0:T(8,128)(2,1)}, bf16[64,6144]{1,0:T(8,128)(2,1)S(1)}, bf16[64,6144]{1,0:T(8,128)(2,1)}, bf16[64,6144]{1,0:T(8,128)(2,1)}, bf16[64,6144]{1,0:T(8,128)(2,1)}) custom-call(s32[4]{0:T(128)S(1)} %pad_add_fusion.where, bf16[4,2,64,768]{3,2,1,0:T(8,128)(2,1)S(1)} %copy-done.19, bf16[4,2,64,768]{3,2,1,0:T(8,128)(2,1)S(1)} %copy-done.21, ...), custom_call_target="tpu_custom_call" | custom-call | tf_op jit(solution)/shard_map/pallas_call | solution.py:226
  124.7 2.9 collective-permute-start.10
  127.6 43.1 %collective-permute-done.6.refs_0_ = bf16[1536,1152]{1,0:T(8,128)(2,1)S(1)} collective-permute-done((bf16[1536,1152]{1,0:T(8,128)(2,1)}, bf16[1536,1152]{1,0:T(8,128)(2,1)S(1)}, u32[]{:S(2)}, u32[]{:S(2)}) %collective-permute-start.6) | collective-permute-done | bytes 3538976 | tf_op jit(solution)/shard_map/ppermute | solution.py:477
  170.7 15.6 %collective-permute-start.9 = (bf16[64,6144]{1,0:T(8,128)(2,1)}, bf16[64,6144]{1,0:T(8,128)(2,1)}, u32[]{:S(2)}, u32[]{:S(2)}) collective-permute-start(bf16[64,6144]{1,0:T(8,128)(2,1)} %get-tuple-element.55), channel_id=1, source_target_pairs={{0,8},{4,12},{8,0},{12,4},{1,9},{5,13},{9,1},{13,5},{2,10},{6,14},... | collective-permute-start | bytes 2359304 | tf_op jit(solution)/shard_map/ppermute | solution.py:477
  186.3 1.5 collective-permute-start.15
  187.8 2.0 copy-done.1
  189.8 1.1 copy-done.15
  190.9 1.1 copy-done.17
  192.8 14.9 %shard_map.95 = (bf16[4,2,64,6144]{3,2,1,0:T(8,128)(2,1)}, bf16[64,6144]{1,0:T(8,128)(2,1)S(1)}, bf16[64,6144]{1,0:T(8,128)(2,1)S(1)}, bf16[64,6144]{1,0:T(8,128)(2,1)S(1)}, bf16[64,6144]{1,0:T(8,128)(2,1)S(1)}) custom-call(s32[4]{0:T(128)S(1)} %pad_add_fusion.where, bf16[4,2,64,768]{3,2,1,0:T(8,128)(2,1)S(1)} %copy-done.15, ...), custom_call_target="tpu_custom_call", output_to_operand_aliasing={{0}: (8, {})} | custom-call | tf_op jit(solution)/shard_map/pallas_call | solution.py:226
  207.8 29.3 %collective-permute-done.9.refs_2_ = bf16[64,6144]{1,0:T(8,128)(2,1)} collective-permute-done((bf16[64,6144]{1,0:T(8,128)(2,1)}, bf16[64,6144]{1,0:T(8,128)(2,1)}, u32[]{:S(2)}, u32[]{:S(2)}) %collective-permute-start.9) | collective-permute-done | bytes 786464 | tf_op jit(solution)/shard_map/ppermute | solution.py:477
  237.1 3.6 shard_map.96.refs_0_
  240.7 1.4 collective-permute-start.11
  242.6 3.4 collective-permute-start.14
  246.0 18.5 %collective-permute-done.12.refs_1_ = bf16[64,6144]{1,0:T(8,128)(2,1)S(1)} collective-permute-done((bf16[64,6144]{1,0:T(8,128)(2,1)S(1)}, bf16[64,6144]{1,0:T(8,128)(2,1)S(1)}, u32[]{:S(2)}, u32[]{:S(2)}) %collective-permute-start.12) | collective-permute-done | bytes 786464 | tf_op jit(solution)/shard_map/ppermute | solution.py:477
  264.5 32.4 %collective-permute-done.13.refs_2_ = bf16[64,6144]{1,0:T(8,128)(2,1)S(1)} collective-permute-done((bf16[64,6144]{1,0:T(8,128)(2,1)S(1)}, bf16[64,6144]{1,0:T(8,128)(2,1)S(1)}, u32[]{:S(2)}, u32[]{:S(2)}) %collective-permute-start.13) | collective-permute-done | bytes 786464 | tf_op jit(solution)/shard_map/ppermute | solution.py:477
  296.9 13.8 %collective-permute-done.11.refs_4_.refs_1_ = bf16[256,6144]{1,0:T(8,128)(2,1)S(1)} collective-permute-done((bf16[256,6144]{1,0:T(8,128)(2,1)S(1)}, bf16[256,6144]{1,0:T(8,128)(2,1)S(1)}, u32[]{:S(2)}, u32[]{:S(2)}) %collective-permute-start.11) | collective-permute-done | bytes 3145760 | tf_op jit(solution)/shard_map/ppermute | solution.py:471
  311.5 0.9 copy-done.12
  312.4 1.7 copy-done.4
  314.7 1.4 copy-done.5
  316.0 1.4 collective-permute-start.19
  317.4 3.5 fusion
  320.9 1.9 collective-permute-start.18
  323.3 41.0 %collective-permute-done.18.refs_0_ = bf16[768,1152]{1,0:T(8,128)(2,1)} collective-permute-done((bf16[768,1152]{1,0:T(8,128)(2,1)S(1)}, bf16[768,1152]{1,0:T(8,128)(2,1)}, u32[]{:S(2)}, u32[]{:S(2)}) %collective-permute-start.18) | collective-permute-done | bytes 1769504 | tf_op jit(solution)/shard_map/ppermute | solution.py:477
  364.4 35.6 %collective-permute-done.20.refs_2_ = bf16[768,1152]{1,0:T(8,128)(2,1)} collective-permute-done((bf16[768,1152]{1,0:T(8,128)(2,1)}, bf16[768,1152]{1,0:T(8,128)(2,1)}, u32[]{:S(2)}, u32[]{:S(2)}) %collective-permute-start.20) | collective-permute-done | bytes 1769504 | tf_op jit(solution)/shard_map/ppermute | solution.py:477
  400.5 1.5 collective-permute-start.24
  402.6 26.9 %shard_map.101 = (bf16[4,64,384]{2,1,0:T(8,128)(2,1)S(1)}, bf16[4,64,384]{2,1,0:T(8,128)(2,1)S(1)}, bf16[4,64,384]{2,1,0:T(8,128)(2,1)S(1)}, bf16[4,64,384]{2,1,0:T(8,128)(2,1)S(1)}) custom-call(s32[4]{0:T(128)S(1)} %pad_add_fusion.where, bf16[256,6144]{1,0:T(8,128)(2,1)} %get-tuple-element.61.refs_0_, bf16[256,6144]{1,0:T(8,128)(2,1)} %get-tuple-element.62.refs_1_, ...), custom_call_target="tpu_custom_call" | custom-call | flops 14495514624 | bytes 26738688 | tf_op jit(solution)/shard_map/pallas_call | solution.py:331
  429.7 3.9 collective-permute-start.23
  433.6 26.9 %shard_map.102 = (bf16[4,64,384]{2,1,0:T(8,128)(2,1)S(1)}, bf16[4,64,384]{2,1,0:T(8,128)(2,1)S(1)}, bf16[4,64,384]{2,1,0:T(8,128)(2,1)S(1)}, bf16[4,64,384]{2,1,0:T(8,128)(2,1)S(1)}) custom-call(s32[4]{0:T(128)S(1)} %pad_add_fusion.where, bf16[256,6144]{1,0:T(8,128)(2,1)} %get-tuple-element.69.refs_0_, bf16[256,6144]{1,0:T(8,128)(2,1)} %get-tuple-element.70.refs_1_, ...), custom_call_target="tpu_custom_call" | custom-call | flops 14495514624 | bytes 26738688 | tf_op jit(solution)/shard_map/pallas_call | solution.py:331
  463.3 2.3 collective-permute-start.28
  465.6 1.1 collective-permute-start.29
  467.5 11.9 %collective-permute-done.25.refs_8_ = bf16[768,1152]{1,0:T(8,128)(2,1)} collective-permute-done((bf16[768,1152]{1,0:T(8,128)(2,1)}, bf16[768,1152]{1,0:T(8,128)(2,1)}, u32[]{:S(2)}, u32[]{:S(2)}) %collective-permute-start.25) | collective-permute-done | bytes 1769504 | tf_op jit(solution)/shard_map/ppermute | solution.py:474
  479.4 1.2 copy-done.62
  480.5 26.9 %shard_map.103 = (bf16[4,64,384]{2,1,0:T(8,128)(2,1)S(1)}, bf16[4,64,384]{2,1,0:T(8,128)(2,1)S(1)}, bf16[4,64,384]{2,1,0:T(8,128)(2,1)S(1)}, bf16[4,64,384]{2,1,0:T(8,128)(2,1)S(1)}) custom-call(s32[4]{0:T(128)S(1)} %pad_add_fusion.where, bf16[256,6144]{1,0:T(8,128)(2,1)} %get-tuple-element.61.refs_0_, bf16[256,6144]{1,0:T(8,128)(2,1)} %get-tuple-element.62.refs_1_, ...), custom_call_target="tpu_custom_call" | custom-call | flops 14495514624 | bytes 26738688 | tf_op jit(solution)/shard_map/pallas_call | solution.py:331
  511.2 3.9 collective-permute-start.33
  515.2 27.1 %shard_map.106 = (bf16[4,64,384]{2,1,0:T(8,128)(2,1)S(1)}, bf16[4,64,384]{2,1,0:T(8,128)(2,1)S(1)}, bf16[4,64,384]{2,1,0:T(8,128)(2,1)S(1)}, bf16[4,64,384]{2,1,0:T(8,128)(2,1)S(1)}) custom-call(s32[4]{0:T(128)S(1)} %pad_add_fusion.where, bf16[256,6144]{1,0:T(8,128)(2,1)} %get-tuple-element.69.refs_0_, bf16[256,6144]{1,0:T(8,128)(2,1)} %get-tuple-element.70.refs_1_, ...), custom_call_target="tpu_custom_call" | custom-call | flops 14495514624 | bytes 26738688 | tf_op jit(solution)/shard_map/pallas_call | solution.py:331
  546.5 1.4 collective-permute-start.35
  547.9 2.9 collective-permute-start.36
  550.9 5.0 collective-permute-done.34.refs_13_
  555.8 6.2 %collective-permute-done.35.refs_14_ = bf16[4,64,384]{2,1,0:T(8,128)(2,1)S(1)} collective-permute-done((bf16[4,64,384]{2,1,0:T(8,128)(2,1)}, bf16[4,64,384]{2,1,0:T(8,128)(2,1)S(1)}, u32[]{:S(2)}, u32[]{:S(2)}) %collective-permute-start.35) | collective-permute-done | bytes 196640 | tf_op jit(solution)/shard_map/ppermute | solution.py:477
  563.0 0.9 copy-done.43
  565.8 3.3 shard_map.108
  (168 shorter events, 21.0 us)
Async XLA Ops:
  0.6 19.5 %collective-permute-start.1 = (bf16[768,6144]{1,0:T(8,128)(2,1)}, bf16[768,6144]{1,0:T(8,128)(2,1)}, u32[]{:S(2)}, u32[]{:S(2)}) collective-permute-start(bf16[768,6144]{1,0:T(8,128)(2,1)} %own_ref.7), channel_id=1, source_target_pairs={{0,1},{1,0},{2,3},{3,2},{4,5},{5,4},{6,7},{7,6},{8,9},{9,8},{10,11... | collective-permute-start | bytes 28311560 | tf_op jit(solution)/shard_map/ppermute | solution.py:468
  1.2 3.0 copy-start.13
  4.2 15.9 %slice-start = ((s8[9437184]{0:T(1024)(128)(4,1)}), s8[4194304]{0:T(1024)(128)(4,1)S(1)}, s32[]{:S(2)}) async-start(s8[9437184]{0:T(1024)(128)(4,1)} %bitcast.6), calls=%async_computation | async-start | bytes 8388608
  4.2 15.9 %slice-start.1 = ((s8[9437184]{0:T(1024)(128)(4,1)}), s8[4194304]{0:T(1024)(128)(4,1)S(1)}, s32[]{:S(2)}) async-start(s8[9437184]{0:T(1024)(128)(4,1)} %bitcast.6), calls=%async_computation.1 | async-start | bytes 8388608
  5.6 14.6 %slice-start.2 = ((s8[9437184]{0:T(1024)(128)(4,1)}), s8[1048576]{0:T(1024)(128)(4,1)S(1)}, s32[]{:S(2)}) async-start(s8[9437184]{0:T(1024)(128)(4,1)} %bitcast.6), calls=%async_computation.2 | async-start | bytes 2097152
  5.6 81.9 %collective-permute-start.4 = (bf16[1536,1152]{1,0:T(8,128)(2,1)S(1)}, bf16[1536,1152]{1,0:T(8,128)(2,1)S(1)}, u32[]{:S(2)}, u32[]{:S(2)}) collective-permute-start(bf16[1536,1152]{1,0:T(8,128)(2,1)S(1)} %shard_map.86.refs_0_), channel_id=1, source_target_pairs={{0,4},{4,8},{8,12},{12,0},{1,5},{5,9},{9,13},{13,1},{2,6},{6,10},{... | collective-permute-start | bytes 10616840 | tf_op jit(solution)/shard_map/ppermute | solution.py:477
  17.8 13.2 %copy-start.18 = (bf16[4,2,64,768]{3,2,1,0:T(8,128)(2,1)}, bf16[4,2,64,768]{3,2,1,0:T(8,128)(2,1)S(1)}, u32[]{:S(2)}) copy-start(bf16[4,2,64,768]{3,2,1,0:T(8,128)(2,1)S(1)} %get-tuple-element.47.keep_ref) | copy-start | bytes 2359300
  17.8 2.4 collective-permute-start
  20.1 10.9 %copy-start.20 = (bf16[4,2,64,768]{3,2,1,0:T(8,128)(2,1)}, bf16[4,2,64,768]{3,2,1,0:T(8,128)(2,1)S(1)}, u32[]{:S(2)}) copy-start(bf16[4,2,64,768]{3,2,1,0:T(8,128)(2,1)S(1)} %collective-permute-done.came_ref) | copy-start | bytes 2359300
  20.2 12.4 %copy-start.7 = (bf16[4,2,256,768]{3,2,1,0:T(8,128)(2,1)S(1)}, bf16[4,2,256,768]{3,2,1,0:T(8,128)(2,1)}, u32[]{:S(2)}) copy-start(bf16[4,2,256,768]{3,2,1,0:T(8,128)(2,1)} %q_ref.3) | copy-start | bytes 9437188
  31.0 70.5 %collective-permute-start.3 = (bf16[256,6144]{1,0:T(8,128)(2,1)}, bf16[256,6144]{1,0:T(8,128)(2,1)}, u32[]{:S(2)}, u32[]{:S(2)}) collective-permute-start(bf16[256,6144]{1,0:T(8,128)(2,1)} %shard_map.88.refs_0_), channel_id=1, source_target_pairs={{0,2},{2,0},{1,3},{3,1},{4,6},{6,4},{5,7},{7,5},{8,10},{10,8},{9,1... | collective-permute-start | bytes 9437192 | tf_op jit(solution)/shard_map/ppermute | solution.py:471
  32.5 1.9 copy-start.9
  38.3 11.8 %copy-start.14 = (bf16[4,2,64,768]{3,2,1,0:T(8,128)(2,1)}, bf16[4,2,64,768]{3,2,1,0:T(8,128)(2,1)S(1)}, u32[]{:S(2)}) copy-start(bf16[4,2,64,768]{3,2,1,0:T(8,128)(2,1)S(1)} %get-tuple-element.49.keep_ref) | copy-start | bytes 2359300
  38.3 2.4 collective-permute-start.2
  40.6 9.4 %copy-start.16 = (bf16[4,2,64,768]{3,2,1,0:T(8,128)(2,1)}, bf16[4,2,64,768]{3,2,1,0:T(8,128)(2,1)S(1)}, u32[]{:S(2)}) copy-start(bf16[4,2,64,768]{3,2,1,0:T(8,128)(2,1)S(1)} %collective-permute-done.2.came_ref) | copy-start | bytes 2359300
  89.2 81.5 %collective-permute-start.6 = (bf16[1536,1152]{1,0:T(8,128)(2,1)}, bf16[1536,1152]{1,0:T(8,128)(2,1)S(1)}, u32[]{:S(2)}, u32[]{:S(2)}) collective-permute-start(bf16[1536,1152]{1,0:T(8,128)(2,1)} %shard_map.91.refs_2_.refs_5_), channel_id=1, source_target_pairs={{0,4},{4,8},{8,12},{12,0},{1,5},{5,9},{9,13},{13,1},{2,6},{6,10},{... | collective-permute-start | bytes 10616840 | tf_op jit(solution)/shard_map/ppermute | solution.py:477
  89.2 97.0 %collective-permute-start.7 = (bf16[1536,1152]{1,0:T(8,128)(2,1)}, bf16[1536,1152]{1,0:T(8,128)(2,1)}, u32[]{:S(2)}, u32[]{:S(2)}) collective-permute-start(bf16[1536,1152]{1,0:T(8,128)(2,1)} %shard_map.91.refs_2_.refs_5_), channel_id=1, source_target_pairs={{0,16},{16,0},{1,17},{17,1},{2,18},{18,2},{3,19},{19,3},{4,20},{20... | collective-permute-start | bytes 10616840 | tf_op jit(solution)/shard_map/ppermute | solution.py:474
  101.5 86.2 %collective-permute-start.5 = (bf16[256,6144]{1,0:T(8,128)(2,1)}, bf16[256,6144]{1,0:T(8,128)(2,1)}, u32[]{:S(2)}, u32[]{:S(2)}) collective-permute-start(bf16[256,6144]{1,0:T(8,128)(2,1)} %shard_map.92.rest_0_), channel_id=1, source_target_pairs={{0,2},{2,0},{1,3},{3,1},{4,6},{6,4},{5,7},{7,5},{8,10},{10,8},{9,1... | collective-permute-start | bytes 9437192 | tf_op jit(solution)/shard_map/ppermute | solution.py:471
  103.1 1.9 copy-start.3
  124.7 83.0 %collective-permute-start.10 = (bf16[64,6144]{1,0:T(8,128)(2,1)}, bf16[64,6144]{1,0:T(8,128)(2,1)}, u32[]{:S(2)}, u32[]{:S(2)}) collective-permute-start(bf16[64,6144]{1,0:T(8,128)(2,1)} %get-tuple-element.56), channel_id=1, source_target_pairs={{0,12},{4,0},{8,4},{12,8},{1,13},{5,1},{9,5},{13,9},{2,14},{6,2},{... | collective-permute-start | bytes 2359304 | tf_op jit(solution)/shard_map/ppermute | solution.py:477
  127.6 80.1 %collective-permute-start.8 = (bf16[64,6144]{1,0:T(8,128)(2,1)}, bf16[64,6144]{1,0:T(8,128)(2,1)}, u32[]{:S(2)}, u32[]{:S(2)}) collective-permute-start(bf16[64,6144]{1,0:T(8,128)(2,1)} %get-tuple-element.54), channel_id=1, source_target_pairs={{0,4},{4,8},{8,12},{12,0},{1,5},{5,9},{9,13},{13,1},{2,6},{6,10},{... | collective-permute-start | bytes 2359304 | tf_op jit(solution)/shard_map/ppermute | solution.py:477
  170.7 15.6 %copy-start = (bf16[1536,1152]{1,0:T(8,128)(2,1)}, bf16[1536,1152]{1,0:T(8,128)(2,1)S(1)}, u32[]{:S(2)}) copy-start(bf16[1536,1152]{1,0:T(8,128)(2,1)S(1)} %collective-permute-done.6.refs_0_) | copy-start | bytes 10616836
  170.7 66.4 %collective-permute-start.9 = (bf16[64,6144]{1,0:T(8,128)(2,1)}, bf16[64,6144]{1,0:T(8,128)(2,1)}, u32[]{:S(2)}, u32[]{:S(2)}) collective-permute-start(bf16[64,6144]{1,0:T(8,128)(2,1)} %get-tuple-element.55), channel_id=1, source_target_pairs={{0,8},{4,12},{8,0},{12,4},{1,9},{5,13},{9,1},{13,5},{2,10},{6,14},... | collective-permute-start | bytes 2359304 | tf_op jit(solution)/shard_map/ppermute | solution.py:477
  186.3 127.9 %collective-permute-start.15 = (bf16[1536,1152]{1,0:T(8,128)(2,1)}, bf16[1536,1152]{1,0:T(8,128)(2,1)}, u32[]{:S(2)}, u32[]{:S(2)}) collective-permute-start(bf16[1536,1152]{1,0:T(8,128)(2,1)} %shard_map.94.rest_1_.refs_2_), channel_id=1, source_target_pairs={{0,16},{16,0},{1,17},{17,1},{2,18},{18,2},{3,19},{19,3},{4,20},{20... | collective-permute-start | bytes 10616840 | tf_op jit(solution)/shard_map/ppermute | solution.py:474
  187.8 2.0 copy-start.1
  192.8 44.3 %copy-start.23 = (bf16[64,6144]{1,0:T(8,128)(2,1)S(1)}, bf16[64,6144]{1,0:T(8,128)(2,1)}, u32[]{:S(2)}) copy-start(bf16[64,6144]{1,0:T(8,128)(2,1)} %copy-done.22) | copy-start | bytes 2359300
  240.7 56.2 %copy-start.11 = (bf16[256,6144]{1,0:T(8,128)(2,1)}, bf16[256,6144]{1,0:T(8,128)(2,1)S(1)}, u32[]{:S(2)}) copy-start(bf16[256,6144]{1,0:T(8,128)(2,1)S(1)} %shard_map.96.refs_0_) | copy-start | bytes 9437188
  240.7 70.0 %collective-permute-start.11 = (bf16[256,6144]{1,0:T(8,128)(2,1)S(1)}, bf16[256,6144]{1,0:T(8,128)(2,1)S(1)}, u32[]{:S(2)}, u32[]{:S(2)}) collective-permute-start(bf16[256,6144]{1,0:T(8,128)(2,1)S(1)} %shard_map.96.refs_0_), channel_id=1, source_target_pairs={{0,2},{2,0},{1,3},{3,1},{4,6},{6,4},{5,7},{7,5},{8,10},{10,8},{9,1... | collective-permute-start | bytes 9437192 | tf_op jit(solution)/shard_map/ppermute | solution.py:471
  242.2 22.4 %collective-permute-start.12 = (bf16[64,6144]{1,0:T(8,128)(2,1)S(1)}, bf16[64,6144]{1,0:T(8,128)(2,1)S(1)}, u32[]{:S(2)}, u32[]{:S(2)}) collective-permute-start(bf16[64,6144]{1,0:T(8,128)(2,1)S(1)} %get-tuple-element.58), channel_id=1, source_target_pairs={{0,4},{4,8},{8,12},{12,0},{1,5},{5,9},{9,13},{13,1},{2,6},{6,10},{... | collective-permute-start | bytes 2359304 | tf_op jit(solution)/shard_map/ppermute | solution.py:477
  242.2 54.8 %collective-permute-start.13 = (bf16[64,6144]{1,0:T(8,128)(2,1)S(1)}, bf16[64,6144]{1,0:T(8,128)(2,1)S(1)}, u32[]{:S(2)}, u32[]{:S(2)}) collective-permute-start(bf16[64,6144]{1,0:T(8,128)(2,1)S(1)} %get-tuple-element.59), channel_id=1, source_target_pairs={{0,8},{4,12},{8,0},{12,4},{1,9},{5,13},{9,1},{13,5},{2,10},{6,14},... | collective-permute-start | bytes 2359304 | tf_op jit(solution)/shard_map/ppermute | solution.py:477
  242.6 54.3 %collective-permute-start.14 = (bf16[64,6144]{1,0:T(8,128)(2,1)S(1)}, bf16[64,6144]{1,0:T(8,128)(2,1)S(1)}, u32[]{:S(2)}, u32[]{:S(2)}) collective-permute-start(bf16[64,6144]{1,0:T(8,128)(2,1)S(1)} %get-tuple-element.60), channel_id=1, source_target_pairs={{0,12},{4,0},{8,4},{12,8},{1,13},{5,1},{9,5},{13,9},{2,14},{6,2},{... | collective-permute-start | bytes 2359304 | tf_op jit(solution)/shard_map/ppermute | solution.py:477
  314.2 1.9 copy-start.5
  314.2 50.2 %collective-permute-start.16 = (bf16[256,6144]{1,0:T(8,128)(2,1)}, bf16[256,6144]{1,0:T(8,128)(2,1)}, u32[]{:S(2)}, u32[]{:S(2)}) collective-permute-start(bf16[256,6144]{1,0:T(8,128)(2,1)} %get-tuple-element.61.refs_0_), channel_id=1, source_target_pairs={{0,1},{1,0},{2,3},{3,2},{4,5},{5,4},{6,7},{7,6},{8,9},{9,8},{10,11... | collective-permute-start | bytes 9437192 | tf_op jit(solution)/shard_map/ppermute | solution.py:468
  314.2 50.2 %collective-permute-start.17 = (bf16[256,6144]{1,0:T(8,128)(2,1)}, bf16[256,6144]{1,0:T(8,128)(2,1)}, u32[]{:S(2)}, u32[]{:S(2)}) collective-permute-start(bf16[256,6144]{1,0:T(8,128)(2,1)} %get-tuple-element.62.refs_1_), channel_id=1, source_target_pairs={{0,1},{1,0},{2,3},{3,2},{4,5},{5,4},{6,7},{7,6},{8,9},{9,8},{10,11... | collective-permute-start | bytes 9437192 | tf_op jit(solution)/shard_map/ppermute | solution.py:468
  316.0 84.0 %collective-permute-start.19 = (bf16[256,6144]{1,0:T(8,128)(2,1)S(1)}, bf16[256,6144]{1,0:T(8,128)(2,1)}, u32[]{:S(2)}, u32[]{:S(2)}) collective-permute-start(bf16[256,6144]{1,0:T(8,128)(2,1)S(1)} %copy-done.5), channel_id=1, source_target_pairs={{0,2},{2,0},{1,3},{3,1},{4,6},{6,4},{5,7},{7,5},{8,10},{10,8},{9,1... | collective-permute-start | bytes 9437192 | tf_op jit(solution)/shard_map/ppermute | solution.py:471
  320.9 43.4 %collective-permute-start.18 = (bf16[768,1152]{1,0:T(8,128)(2,1)S(1)}, bf16[768,1152]{1,0:T(8,128)(2,1)}, u32[]{:S(2)}, u32[]{:S(2)}) collective-permute-start(bf16[768,1152]{1,0:T(8,128)(2,1)S(1)} %get-tuple-element.93), channel_id=1, source_target_pairs={{0,4},{4,8},{8,12},{12,0},{1,5},{5,9},{9,13},{13,1},{2,6},{6,10},{... | collective-permute-start | bytes 5308424 | tf_op jit(solution)/shard_map/ppermute | solution.py:477
  322.8 77.2 %collective-permute-start.20 = (bf16[768,1152]{1,0:T(8,128)(2,1)}, bf16[768,1152]{1,0:T(8,128)(2,1)}, u32[]{:S(2)}, u32[]{:S(2)}) collective-permute-start(bf16[768,1152]{1,0:T(8,128)(2,1)} %get-tuple-element.92), channel_id=1, source_target_pairs={{0,4},{4,8},{8,12},{12,0},{1,5},{5,9},{9,13},{13,1},{2,6},{6,10},{... | collective-permute-start | bytes 5308424 | tf_op jit(solution)/shard_map/ppermute | solution.py:477
  400.0 29.6 %collective-permute-start.26 = (bf16[256,6144]{1,0:T(8,128)(2,1)}, bf16[256,6144]{1,0:T(8,128)(2,1)S(1)}, u32[]{:S(2)}, u32[]{:S(2)}) collective-permute-start(bf16[256,6144]{1,0:T(8,128)(2,1)} %get-tuple-element.69.refs_0_), channel_id=1, source_target_pairs={{0,1},{1,0},{2,3},{3,2},{4,5},{5,4},{6,7},{7,6},{8,9},{9,8},{10,11... | collective-permute-start | bytes 9437192 | tf_op jit(solution)/shard_map/ppermute | solution.py:468
  400.0 29.6 %collective-permute-start.27 = (bf16[256,6144]{1,0:T(8,128)(2,1)}, bf16[256,6144]{1,0:T(8,128)(2,1)S(1)}, u32[]{:S(2)}, u32[]{:S(2)}) collective-permute-start(bf16[256,6144]{1,0:T(8,128)(2,1)} %get-tuple-element.70.refs_1_), channel_id=1, source_target_pairs={{0,1},{1,0},{2,3},{3,2},{4,5},{5,4},{6,7},{7,6},{8,9},{9,8},{10,11... | collective-permute-start | bytes 9437192 | tf_op jit(solution)/shard_map/ppermute | solution.py:468
  400.5 78.8 %collective-permute-start.24 = (bf16[768,1152]{1,0:T(8,128)(2,1)}, bf16[768,1152]{1,0:T(8,128)(2,1)S(1)}, u32[]{:S(2)}, u32[]{:S(2)}) collective-permute-start(bf16[768,1152]{1,0:T(8,128)(2,1)} %shard_map.99.refs_3_.refs_7_), channel_id=1, source_target_pairs={{0,16},{16,0},{1,17},{17,1},{2,18},{18,2},{3,19},{19,3},{4,20},{20... | collective-permute-start | bytes 5308424 | tf_op jit(solution)/shard_map/ppermute | solution.py:474
  402.0 77.3 %collective-permute-start.25 = (bf16[768,1152]{1,0:T(8,128)(2,1)}, bf16[768,1152]{1,0:T(8,128)(2,1)}, u32[]{:S(2)}, u32[]{:S(2)}) collective-permute-start(bf16[768,1152]{1,0:T(8,128)(2,1)} %get-tuple-element.64.refs_8_.refs_9_), channel_id=1, source_target_pairs={{0,16},{16,0},{1,17},{17,1},{2,18},{18,2},{3,19},{19,3},{4,20},{20... | collective-permute-start | bytes 5308424 | tf_op jit(solution)/shard_map/ppermute | solution.py:474
  429.4 31.0 %copy-start.24 = (bf16[4,64,384]{2,1,0:T(8,128)(2,1)}, bf16[4,64,384]{2,1,0:T(8,128)(2,1)S(1)}, u32[]{:S(2)}) copy-start(bf16[4,64,384]{2,1,0:T(8,128)(2,1)S(1)} %get-tuple-element.65.refs_9_.refs_3_.refs_0_) | copy-start | bytes 589828
  429.5 33.0 %collective-permute-start.21 = (bf16[4,64,384]{2,1,0:T(8,128)(2,1)S(1)}, bf16[4,64,384]{2,1,0:T(8,128)(2,1)S(1)}, u32[]{:S(2)}, u32[]{:S(2)}) collective-permute-start(bf16[4,64,384]{2,1,0:T(8,128)(2,1)S(1)} %get-tuple-element.66), channel_id=1, source_target_pairs={{0,4},{4,8},{8,12},{12,0},{1,5},{5,9},{9,13},{13,1},{2,6},{6,10},{... | collective-permute-start | bytes 589832 | tf_op jit(solution)/shard_map/ppermute | solution.py:477
  429.6 4.0 copy-start.60
  429.6 32.9 %collective-permute-start.22 = (bf16[4,64,384]{2,1,0:T(8,128)(2,1)S(1)}, bf16[4,64,384]{2,1,0:T(8,128)(2,1)S(1)}, u32[]{:S(2)}, u32[]{:S(2)}) collective-permute-start(bf16[4,64,384]{2,1,0:T(8,128)(2,1)S(1)} %get-tuple-element.67), channel_id=1, source_target_pairs={{0,8},{4,12},{8,0},{12,4},{1,9},{5,13},{9,1},{13,5},{2,10},{6,14},... | collective-permute-start | bytes 589832 | tf_op jit(solution)/shard_map/ppermute | solution.py:477
  429.6 4.0 copy-start.61
  429.7 32.9 %collective-permute-start.23 = (bf16[4,64,384]{2,1,0:T(8,128)(2,1)S(1)}, bf16[4,64,384]{2,1,0:T(8,128)(2,1)S(1)}, u32[]{:S(2)}, u32[]{:S(2)}) collective-permute-start(bf16[4,64,384]{2,1,0:T(8,128)(2,1)S(1)} %get-tuple-element.68), channel_id=1, source_target_pairs={{0,12},{4,0},{8,4},{12,8},{1,13},{5,1},{9,5},{13,9},{2,14},{6,2},{... | collective-permute-start | bytes 589832 | tf_op jit(solution)/shard_map/ppermute | solution.py:477
  463.3 46.9 %collective-permute-start.28 = (bf16[4,64,384]{2,1,0:T(8,128)(2,1)}, bf16[4,64,384]{2,1,0:T(8,128)(2,1)S(1)}, u32[]{:S(2)}, u32[]{:S(2)}) collective-permute-start(bf16[4,64,384]{2,1,0:T(8,128)(2,1)} %get-tuple-element.79), channel_id=1, source_target_pairs={{0,12},{4,0},{8,4},{12,8},{1,13},{5,1},{9,5},{13,9},{2,14},{6,2},{... | collective-permute-start | bytes 589832 | tf_op jit(solution)/shard_map/ppermute | solution.py:477
  465.6 44.6 %collective-permute-start.29 = (bf16[4,64,384]{2,1,0:T(8,128)(2,1)}, bf16[4,64,384]{2,1,0:T(8,128)(2,1)S(1)}, u32[]{:S(2)}, u32[]{:S(2)}) collective-permute-start(bf16[4,64,384]{2,1,0:T(8,128)(2,1)} %get-tuple-element.80), channel_id=1, source_target_pairs={{0,8},{4,12},{8,0},{12,4},{1,9},{5,13},{9,1},{13,5},{2,10},{6,14},... | collective-permute-start | bytes 589832 | tf_op jit(solution)/shard_map/ppermute | solution.py:477
  466.7 43.5 %collective-permute-start.30 = (bf16[4,64,384]{2,1,0:T(8,128)(2,1)}, bf16[4,64,384]{2,1,0:T(8,128)(2,1)S(1)}, u32[]{:S(2)}, u32[]{:S(2)}) collective-permute-start(bf16[4,64,384]{2,1,0:T(8,128)(2,1)} %get-tuple-element.81), channel_id=1, source_target_pairs={{0,4},{4,8},{8,12},{12,0},{1,5},{5,9},{9,13},{13,1},{2,6},{6,10},{... | collective-permute-start | bytes 589832 | tf_op jit(solution)/shard_map/ppermute | solution.py:477
  511.1 34.0 %collective-permute-start.31 = (bf16[4,64,384]{2,1,0:T(8,128)(2,1)}, bf16[4,64,384]{2,1,0:T(8,128)(2,1)S(1)}, u32[]{:S(2)}, u32[]{:S(2)}) collective-permute-start(bf16[4,64,384]{2,1,0:T(8,128)(2,1)} %get-tuple-element.82), channel_id=1, source_target_pairs={{0,4},{4,8},{8,12},{12,0},{1,5},{5,9},{9,13},{13,1},{2,6},{6,10},{... | collective-permute-start | bytes 589832 | tf_op jit(solution)/shard_map/ppermute | solution.py:477
  511.2 33.9 %collective-permute-start.32 = (bf16[4,64,384]{2,1,0:T(8,128)(2,1)}, bf16[4,64,384]{2,1,0:T(8,128)(2,1)S(1)}, u32[]{:S(2)}, u32[]{:S(2)}) collective-permute-start(bf16[4,64,384]{2,1,0:T(8,128)(2,1)} %get-tuple-element.83), channel_id=1, source_target_pairs={{0,8},{4,12},{8,0},{12,4},{1,9},{5,13},{9,1},{13,5},{2,10},{6,14},... | collective-permute-start | bytes 589832 | tf_op jit(solution)/shard_map/ppermute | solution.py:477
  511.2 33.9 %collective-permute-start.33 = (bf16[4,64,384]{2,1,0:T(8,128)(2,1)}, bf16[4,64,384]{2,1,0:T(8,128)(2,1)S(1)}, u32[]{:S(2)}, u32[]{:S(2)}) collective-permute-start(bf16[4,64,384]{2,1,0:T(8,128)(2,1)} %get-tuple-element.84), channel_id=1, source_target_pairs={{0,12},{4,0},{8,4},{12,8},{1,13},{5,1},{9,5},{13,9},{2,14},{6,2},{... | collective-permute-start | bytes 589832 | tf_op jit(solution)/shard_map/ppermute | solution.py:477
  515.2 46.9 %copy-start.25 = (bf16[4,64,384]{2,1,0:T(8,128)(2,1)S(1)}, bf16[4,64,384]{2,1,0:T(8,128)(2,1)}, u32[]{:S(2)}) copy-start(bf16[4,64,384]{2,1,0:T(8,128)(2,1)} %copy-done.24) | copy-start | bytes 589828
  515.2 46.9 %copy-start.27 = (bf16[4,64,384]{2,1,0:T(8,128)(2,1)S(1)}, bf16[4,64,384]{2,1,0:T(8,128)(2,1)}, u32[]{:S(2)}) copy-start(bf16[4,64,384]{2,1,0:T(8,128)(2,1)} %copy-done.26) | copy-start | bytes 589828
  515.2 46.9 %copy-start.29 = (bf16[4,64,384]{2,1,0:T(8,128)(2,1)S(1)}, bf16[4,64,384]{2,1,0:T(8,128)(2,1)}, u32[]{:S(2)}) copy-start(bf16[4,64,384]{2,1,0:T(8,128)(2,1)} %copy-done.28) | copy-start | bytes 589828
  515.2 46.9 %copy-start.31 = (bf16[4,64,384]{2,1,0:T(8,128)(2,1)S(1)}, bf16[4,64,384]{2,1,0:T(8,128)(2,1)}, u32[]{:S(2)}) copy-start(bf16[4,64,384]{2,1,0:T(8,128)(2,1)} %copy-done.30) | copy-start | bytes 589828
  515.2 46.9 %copy-start.33 = (bf16[4,64,384]{2,1,0:T(8,128)(2,1)S(1)}, bf16[4,64,384]{2,1,0:T(8,128)(2,1)}, u32[]{:S(2)}) copy-start(bf16[4,64,384]{2,1,0:T(8,128)(2,1)} %copy-done.32) | copy-start | bytes 589828
  515.2 46.9 %copy-start.35 = (bf16[4,64,384]{2,1,0:T(8,128)(2,1)S(1)}, bf16[4,64,384]{2,1,0:T(8,128)(2,1)}, u32[]{:S(2)}) copy-start(bf16[4,64,384]{2,1,0:T(8,128)(2,1)} %copy-done.34) | copy-start | bytes 589828
  515.2 46.9 %copy-start.37 = (bf16[4,64,384]{2,1,0:T(8,128)(2,1)S(1)}, bf16[4,64,384]{2,1,0:T(8,128)(2,1)}, u32[]{:S(2)}) copy-start(bf16[4,64,384]{2,1,0:T(8,128)(2,1)} %copy-done.36) | copy-start | bytes 589828
  515.2 46.9 %copy-start.39 = (bf16[4,64,384]{2,1,0:T(8,128)(2,1)S(1)}, bf16[4,64,384]{2,1,0:T(8,128)(2,1)}, u32[]{:S(2)}) copy-start(bf16[4,64,384]{2,1,0:T(8,128)(2,1)} %copy-done.38) | copy-start | bytes 589828
  545.9 9.9 %collective-permute-start.34 = (bf16[4,64,384]{2,1,0:T(8,128)(2,1)}, bf16[4,64,384]{2,1,0:T(8,128)(2,1)S(1)}, u32[]{:S(2)}, u32[]{:S(2)}) collective-permute-start(bf16[4,64,384]{2,1,0:T(8,128)(2,1)} %get-tuple-element.89), channel_id=1, source_target_pairs={{0,4},{4,8},{8,12},{12,0},{1,5},{5,9},{9,13},{13,1},{2,6},{6,10},{... | collective-permute-start | bytes 589832 | tf_op jit(solution)/shard_map/ppermute | solution.py:477
  546.5 15.5 %collective-permute-start.35 = (bf16[4,64,384]{2,1,0:T(8,128)(2,1)}, bf16[4,64,384]{2,1,0:T(8,128)(2,1)S(1)}, u32[]{:S(2)}, u32[]{:S(2)}) collective-permute-start(bf16[4,64,384]{2,1,0:T(8,128)(2,1)} %get-tuple-element.90), channel_id=1, source_target_pairs={{0,8},{4,12},{8,0},{12,4},{1,9},{5,13},{9,1},{13,5},{2,10},{6,14},... | collective-permute-start | bytes 589832 | tf_op jit(solution)/shard_map/ppermute | solution.py:477
  547.9 14.1 %collective-permute-start.36 = (bf16[4,64,384]{2,1,0:T(8,128)(2,1)}, bf16[4,64,384]{2,1,0:T(8,128)(2,1)S(1)}, u32[]{:S(2)}, u32[]{:S(2)}) collective-permute-start(bf16[4,64,384]{2,1,0:T(8,128)(2,1)} %get-tuple-element.91), channel_id=1, source_target_pairs={{0,12},{4,0},{8,4},{12,8},{1,13},{5,1},{9,5},{13,9},{2,14},{6,2},{... | collective-permute-start | bytes 589832 | tf_op jit(solution)/shard_map/ppermute | solution.py:477
  (39 other events, 38.8 us)
